TPU v7x, 32 devices: a whole 2x2x4 slice. The times are simulated.
32 devices in a mesh: dp: 8 (over y, x, core), mp: 4 (over z).
Axes of the slice: x: 2, y: 2, z: 4, core: 2. Of those that a mesh axis runs over, the one named last changes fastest.
Arguments:
- tokens: bfloat16 [32768, 768], P(('dp', 'mp')), may hold values from -6 to 6
- w_query: bfloat16 [768, 768], P(None, 'mp'), may hold values from -0.3125 to 0.3125
- b_query: float32 [768], P('mp'), may hold values from -3 to 3
- w_key: bfloat16 [768, 768], P(None, 'mp'), may hold values from -0.3125 to 0.3125
- w_value: bfloat16 [768, 768], P(None, 'mp'), may hold values from -0.21875 to 0.21875
- b_value: float32 [768], P('mp'), may hold values from -3 to 3
- w_out: bfloat16 [768, 768], P('mp'), may hold values from -0.875 to 0.875
- b_out: float32 [768], replicated, may hold values from -3 to 3
- norm1_gain: float32 [768], replicated, may hold values from 0.25 to 1.75
- norm1_bias: float32 [768], replicated, may hold values from -3 to 3
- w_up: bfloat16 [768, 3072], P(None, 'mp'), may hold values from -0.21875 to 0.21875
- b_up: bfloat16 [3072], P('mp'), may hold values from -3 to 3
- w_down: bfloat16 [3072, 768], P('mp'), may hold values from -0.109375 to 0.109375
- b_down: float32 [768], replicated, may hold values from -3 to 3
- norm2_gain: float32 [768], replicated, may hold values from 0.25 to 1.75
- norm2_bias: float32 [768], replicated, may hold values from -3 to 3
- key_mask: int32 [8, 4096], P('dp'), may hold values from 0 to 1
- cluster_order: int32 [8, 12, 4096], P('dp', 'mp'), may hold values from 0 to 4095, as said below
- cotangent: bfloat16 [32768, 768], P(('dp', 'mp')), may hold values from -6 to 6
Outputs:
- layer_out: bfloat16 [32768, 768], P(('dp', 'mp'))
- grad_tokens: bfloat16 [32768, 768], P(('dp', 'mp'))
- grad_w_query: float32 [768, 768], P(None, 'mp')
- grad_b_query: float32 [768], P('mp')
- grad_w_key: float32 [768, 768], P(None, 'mp')
- grad_w_value: float32 [768, 768], P(None, 'mp')
- grad_b_value: float32 [768], P('mp')
- grad_w_out: float32 [768, 768], P('mp')
- grad_b_out: float32 [768], replicated
- grad_norm1_gain: float32 [768], replicated
- grad_norm1_bias: float32 [768], replicated
- grad_w_up: float32 [768, 3072], P(None, 'mp')
- grad_b_up: float32 [3072], P('mp')
- grad_w_down: float32 [3072, 768], P('mp')
- grad_b_down: float32 [768], replicated
- grad_norm2_gain: float32 [768], replicated
- grad_norm2_bias: float32 [768], replicated
Inputs may be any that keep to these rules, and one draw needn't show every extreme that they name: `cluster_order`: for each sequence and head a permutation of the 4096 positions; that head's cluster c holds the positions at entries c * 128 to (c + 1) * 128 - 1. The positions whose key_mask is 1 stand first, so that they fill the lowest clusters of every head and the remaining clusters hold masked keys only.
All inputs are finite; a program needn't handle non-finite values.
Results may differ from a plain program's by a relative error of at most 0.02.
The roundings to bfloat16 on the way count: a program that leaves them out, or rounds other values in their place, can miss the bound.
Values may be sent and summed in bfloat16 or wider, within the bound.
A program may use at most 192 MiB of HBM per device.

v0:
```python
import jax
import jax.numpy as jnp
from jax import lax
from jax.sharding import PartitionSpec as P

HD = 64
C = 128
L = 4096


EPS = 1e-12


def matmul(left, right):
    return jnp.dot(left, right, preferred_element_type=jnp.float32)


def contract(left, right, left_dim, right_dim):
    return lax.dot_general(
        left, right, (((left_dim,), (right_dim,)), ((), ())), preferred_element_type=jnp.float32
    )


def layer_norm(hidden, norm_gain, norm_bias):
    average = jnp.mean(hidden, axis=-1, keepdims=True)
    centred = hidden - average
    variance = jnp.mean(centred * centred, axis=-1, keepdims=True)
    return centred * lax.rsqrt(variance + EPS) * norm_gain + norm_bias


def exact_gelu(values):
    return jax.nn.gelu(values, approximate=False)


def body(
    tokens,
    w_query,
    b_query,
    w_key,
    w_value,
    b_value,
    w_out,
    b_out,
    norm1_gain,
    norm1_bias,
    w_up,
    b_up,
    w_down,
    b_down,
    norm2_gain,
    norm2_bias,
    key_mask,
    cluster_order,
    cotangent,
):
    seq_count = cluster_order.shape[0]
    heads_local = cluster_order.shape[1]
    clusters = L // C
    item_count = seq_count * heads_local
    block_shape = (seq_count, heads_local, clusters, C, HD)
    orders = cluster_order.reshape(item_count, L)
    slot_index = lax.broadcasted_iota(jnp.int32, (1, L), 1)

    def permutation(order):
        return (order[:, None] == slot_index).astype(jnp.bfloat16)

    def unsort_rows(rows_items):

        def unsort_one_item(item):
            return contract(permutation(item[0]), item[1], 0, 0).astype(jnp.bfloat16)

        return lax.map(unsort_one_item, (orders, rows_items))

    def to_items(matrices):
        joined = jnp.concatenate(
            [m.reshape(seq_count, L, heads_local, HD) for m in matrices], axis=-1
        )
        return joined.transpose(0, 2, 1, 3).reshape(item_count, L, len(matrices) * HD)

    def from_items(rows_items, count):
        parted = rows_items.reshape(seq_count, heads_local, L, count, HD).transpose(3, 0, 2, 1, 4)
        return tuple(
            (parted[index].reshape(seq_count * L, heads_local * HD) for index in range(count))
        )

    gathered = lax.all_gather(tokens, "mp", axis=0, tiled=True)
    queries = (matmul(gathered, w_query) + b_query).astype(jnp.bfloat16)
    key_rows = matmul(gathered, w_key).astype(jnp.bfloat16)
    value_rows = (matmul(gathered, w_value) + b_value).astype(jnp.bfloat16)
    mask_items = (
        jnp.broadcast_to(key_mask[:, None, :], (seq_count, heads_local, L))
        .reshape(item_count, L, 1)
        .astype(jnp.bfloat16)
    )

    def sort_forward(item):
        table = permutation(item[0])
        return (matmul(table, item[1]).astype(jnp.bfloat16), matmul(table, item[2]))

    sorted_all, keep_sorted = lax.map(
        sort_forward, (orders, to_items((queries, key_rows, value_rows)), mask_items)
    )
    query_blocks = sorted_all[..., :HD].reshape(block_shape)
    key_blocks = sorted_all[..., HD : 2 * HD].reshape(block_shape)
    value_blocks = sorted_all[..., 2 * HD :].reshape(block_shape)
    penalty = (keep_sorted - 1.0).reshape(seq_count, heads_local, clusters, 1, C) * 10000.0

    def block_scores():
        raw_scores = jnp.einsum(
            "shncd,shnkd->shnck", query_blocks, key_blocks, preferred_element_type=jnp.float32
        )
        return raw_scores * 0.125 + penalty

    scores = block_scores()
    row_peak = jnp.max(scores, axis=-1, keepdims=True)
    log_total = row_peak + jnp.log(jnp.sum(jnp.exp(scores - row_peak), axis=-1, keepdims=True))
    probs_low = jnp.exp(scores - log_total).astype(jnp.bfloat16)
    context_sorted = jnp.einsum(
        "shnck,shnkd->shncd", probs_low, value_blocks, preferred_element_type=jnp.float32
    ).astype(jnp.bfloat16)
    context = from_items(unsort_rows(context_sorted.reshape(item_count, L, HD)), 1)[0]
    attended = lax.psum_scatter(
        matmul(context, w_out).astype(jnp.bfloat16), "mp", scatter_dimension=0, tiled=True
    ).astype(jnp.float32)
    residual = tokens.astype(jnp.float32)
    first_norm, first_pull = jax.vjp(
        layer_norm, residual + attended + b_out, norm1_gain, norm1_bias
    )
    first_low = first_norm.astype(jnp.bfloat16)
    up_full, up_bias, down_full = (
        lax.all_gather(w_up, "mp", axis=1, tiled=True),
        lax.all_gather(b_up, "mp", axis=0, tiled=True),
        lax.all_gather(w_down, "mp", axis=0, tiled=True),
    )
    pre_act = matmul(first_low, up_full) + up_bias.astype(jnp.float32)
    activation, gelu_pull = jax.vjp(exact_gelu, pre_act)
    act_low = activation.astype(jnp.bfloat16)
    ffn_out = matmul(act_low, down_full)
    result, second_pull = jax.vjp(layer_norm, first_norm + ffn_out + b_down, norm2_gain, norm2_bias)
    layer_out = result.astype(jnp.bfloat16)
    grad_second, grad_norm2_gain, grad_norm2_bias = second_pull(cotangent.astype(jnp.float32))
    grad_b_down = jnp.sum(grad_second, axis=0)
    grad_ffn = grad_second.astype(jnp.bfloat16)
    grad_pre = gelu_pull(contract(grad_ffn, down_full, 1, 1))[0].astype(jnp.bfloat16)
    grad_first = grad_second + contract(grad_pre, up_full, 1, 1)
    up_rows_full = contract(grad_pre, first_low, 0, 0)
    down_rows_full = contract(act_low, grad_ffn, 0, 0)
    bias_full = jnp.sum(grad_pre, axis=0, dtype=jnp.float32)
    up_share, grad_w_down, grad_b_up = (
        lax.psum_scatter(
            up_rows_full.astype(jnp.bfloat16), "mp", scatter_dimension=0, tiled=True
        ).astype(jnp.float32),
        lax.psum_scatter(
            down_rows_full.astype(jnp.bfloat16), "mp", scatter_dimension=0, tiled=True
        ).astype(jnp.float32),
        lax.psum_scatter(
            bias_full.astype(jnp.bfloat16), "mp", scatter_dimension=0, tiled=True
        ).astype(jnp.float32),
    )
    grad_w_up = up_share.T
    grad_residual, grad_norm1_gain, grad_norm1_bias = first_pull(grad_first)
    grad_b_out = jnp.sum(grad_residual, axis=0)
    grad_att = grad_residual.astype(jnp.bfloat16)
    grad_att_rows = lax.all_gather(grad_att, "mp", axis=0, tiled=True)
    grad_w_out = contract(context, grad_att_rows, 0, 0)
    grad_context = contract(grad_att_rows, w_out, 1, 1).astype(jnp.bfloat16)

    def sort_one_item(item):
        return matmul(permutation(item[0]), item[1]).astype(jnp.bfloat16)

    context_blocks = lax.map(sort_one_item, (orders, to_items((grad_context,)))).reshape(
        block_shape
    )
    attn_probs = jnp.exp(block_scores() - log_total)
    grad_probs = jnp.einsum(
        "shncd,shnkd->shnck", context_blocks, value_blocks, preferred_element_type=jnp.float32
    )
    row_dot = jnp.sum(attn_probs * grad_probs, axis=-1, keepdims=True)
    grad_scores = (attn_probs * (grad_probs - row_dot)).astype(jnp.bfloat16)
    grad_q_blocks = (
        jnp.einsum(
            "shnck,shnkd->shncd", grad_scores, key_blocks, preferred_element_type=jnp.float32
        )
        * 0.125
    ).astype(jnp.bfloat16)
    grad_k_blocks = (
        jnp.einsum(
            "shnck,shncd->shnkd", grad_scores, query_blocks, preferred_element_type=jnp.float32
        )
        * 0.125
    ).astype(jnp.bfloat16)
    grad_v_blocks = jnp.einsum(
        "shnck,shncd->shnkd", probs_low, context_blocks, preferred_element_type=jnp.float32
    ).astype(jnp.bfloat16)
    grad_stack = jnp.concatenate(
        [
            grad_q_blocks.reshape(item_count, L, HD),
            grad_k_blocks.reshape(item_count, L, HD),
            grad_v_blocks.reshape(item_count, L, HD),
        ],
        axis=-1,
    )
    grad_q, grad_k, grad_v = from_items(unsort_rows(grad_stack), 3)
    grad_w_query = contract(gathered, grad_q, 0, 0)
    grad_b_query = jnp.sum(grad_q, axis=0, dtype=jnp.float32)
    grad_w_key = contract(gathered, grad_k, 0, 0)
    grad_w_value = contract(gathered, grad_v, 0, 0)
    grad_b_value = jnp.sum(grad_v, axis=0, dtype=jnp.float32)
    term = contract(grad_q, w_query, 1, 1)
    term = term + contract(grad_k, w_key, 1, 1)
    grad_tokens = (
        grad_residual
        + lax.psum_scatter(
            (term + contract(grad_v, w_value, 1, 1)).astype(jnp.bfloat16),
            "mp",
            scatter_dimension=0,
            tiled=True,
        ).astype(jnp.float32)
    ).astype(jnp.bfloat16)
    grad_norm1_gain, grad_norm1_bias, grad_norm2_gain, grad_norm2_bias, grad_b_out, grad_b_down = (
        lax.psum(
            (
                grad_norm1_gain,
                grad_norm1_bias,
                grad_norm2_gain,
                grad_norm2_bias,
                grad_b_out,
                grad_b_down,
            ),
            ("dp", "mp"),
        )
    )
    (
        grad_w_query,
        grad_b_query,
        grad_w_key,
        grad_w_value,
        grad_b_value,
        grad_w_out,
        grad_w_up,
        grad_b_up,
        grad_w_down,
    ) = lax.psum(
        (
            grad_w_query,
            grad_b_query,
            grad_w_key,
            grad_w_value,
            grad_b_value,
            grad_w_out,
            grad_w_up,
            grad_b_up,
            grad_w_down,
        ),
        "dp",
    )
    return (
        layer_out,
        grad_tokens,
        grad_w_query,
        grad_b_query,
        grad_w_key,
        grad_w_value,
        grad_b_value,
        grad_w_out,
        grad_b_out,
        grad_norm1_gain,
        grad_norm1_bias,
        grad_w_up,
        grad_b_up,
        grad_w_down,
        grad_b_down,
        grad_norm2_gain,
        grad_norm2_bias,
    )


def solution(mesh):
    return jax.shard_map(
        body,
        mesh=mesh,
        in_specs=(
            P(("dp", "mp"), None),
            P(None, "mp"),
            P("mp"),
            P(None, "mp"),
            P(None, "mp"),
            P("mp"),
            P("mp", None),
            P(),
            P(),
            P(),
            P(None, "mp"),
            P("mp"),
            P("mp", None),
            P(),
            P(),
            P(),
            P("dp", None),
            P("dp", "mp", None),
            P(("dp", "mp"), None),
        ),
        out_specs=(
            P(("dp", "mp"), None),
            P(("dp", "mp"), None),
            P(None, "mp"),
            P("mp"),
            P(None, "mp"),
            P(None, "mp"),
            P("mp"),
            P("mp", None),
            P(),
            P(),
            P(),
            P(None, "mp"),
            P("mp"),
            P("mp", None),
            P(),
            P(),
            P(),
        ),
        check_vma=False,
    )
```

profile of v0, /device:TPU:10, one launch (start us, length us, event | category | flops | bytes accessed | tf_op | source)
XLA Modules:
  0.0 1192.2 jit_solution(12186120445890056111)
XLA Ops:
  10.2 113.2 %all-gather.6.cloned.1.call-done = bf16[4096,768]{1,0:T(8,128)(2,1)} async-done(((bf16[1024,768]{1,0:T(8,128)(2,1)}), bf16[4096,768]{1,0:T(8,128)(2,1)}) %all-gather.6.cloned.1.call-update) | async-done | bytes 6291472 | tf_op jit(solution)/shard_map/all_gather | solution.py:86
  164.2 95.3 %while.46 = (s32[]{:T(128)}, bf16[3,4096,192]{1,2,0:T(8,128)(2,1)}, f32[3,4096,1]{1,2,0:T(1,128)S(1)}, s32[3,4096]{1,0:T(4,128)S(1)}, bf16[3,4096,192]{2,1,0:T(8...) while((s32[]{:T(128)}, bf16[3,4096,192]{1,2,0:T(8,128)(2,1)}, ...), condition=%wide.region_1.2_spmd.clone, body=%wide.region_0.1_spmd.clone.sunk | while | flops 6510346240 | bytes 3770449 | solution.py:100
  164.2 18.7 %fusion.159 = bf16[3,4096,192]{1,2,0:T(8,128)(2,1)} fusion(bf16[3,4096,192]{1,2,0:T(8,128)(2,1)} %get-tuple-element.458, s32[]{:T(128)} %get-tuple-element.457, s32[4096]{0:T(1024)S(1)} %bitcast.227, bf16[3,4096,192]{2,1,0:T(8,128)(2,1)} %get-tuple-element.468), kind=kOutput, calls=%fused_computation.11.clone.1 | convolution fusion | flops 6460014592 | bytes 3687424 | tf_op jit(solution)/shard_map/while/body/eval_jaxpr/dot_general | solution.py:15
  182.9 13.0 %fusion.160 = f32[3,4096,1]{1,2,0:T(1,128)S(1)} fusion(f32[3,4096,1]{1,2,0:T(1,128)S(1)} %get-tuple-element.459, s32[]{:T(128)} %get-tuple-element.457, s32[4096]{0:T(1024)S(1)} %bitcast.228, bf16[3,4096,1]{1,0,2:T(4,128)(2,1)S(1)} %get-tuple-element.469), kind=kOutput, calls=%fused_computation.13.clone.1 | convolution fusion | flops 50331648 | bytes 50176 | tf_op jit(solution)/shard_map/while/body/eval_jaxpr/dot_general | solution.py:15
  195.9 18.7 %fusion.159 = bf16[3,4096,192]{1,2,0:T(8,128)(2,1)} fusion(bf16[3,4096,192]{1,2,0:T(8,128)(2,1)} %get-tuple-element.458, s32[]{:T(128)} %get-tuple-element.457, s32[4096]{0:T(1024)S(1)} %bitcast.227, bf16[3,4096,192]{2,1,0:T(8,128)(2,1)} %get-tuple-element.468), kind=kOutput, calls=%fused_computation.11.clone.1 | convolution fusion | flops 6460014592 | bytes 3687424 | tf_op jit(solution)/shard_map/while/body/eval_jaxpr/dot_general | solution.py:15
  214.6 13.0 %fusion.160 = f32[3,4096,1]{1,2,0:T(1,128)S(1)} fusion(f32[3,4096,1]{1,2,0:T(1,128)S(1)} %get-tuple-element.459, s32[]{:T(128)} %get-tuple-element.457, s32[4096]{0:T(1024)S(1)} %bitcast.228, bf16[3,4096,1]{1,0,2:T(4,128)(2,1)S(1)} %get-tuple-element.469), kind=kOutput, calls=%fused_computation.13.clone.1 | convolution fusion | flops 50331648 | bytes 50176 | tf_op jit(solution)/shard_map/while/body/eval_jaxpr/dot_general | solution.py:15
  227.6 18.7 %fusion.159 = bf16[3,4096,192]{1,2,0:T(8,128)(2,1)} fusion(bf16[3,4096,192]{1,2,0:T(8,128)(2,1)} %get-tuple-element.458, s32[]{:T(128)} %get-tuple-element.457, s32[4096]{0:T(1024)S(1)} %bitcast.227, bf16[3,4096,192]{2,1,0:T(8,128)(2,1)} %get-tuple-element.468), kind=kOutput, calls=%fused_computation.11.clone.1 | convolution fusion | flops 6460014592 | bytes 3687424 | tf_op jit(solution)/shard_map/while/body/eval_jaxpr/dot_general | solution.py:15
  246.3 13.0 %fusion.160 = f32[3,4096,1]{1,2,0:T(1,128)S(1)} fusion(f32[3,4096,1]{1,2,0:T(1,128)S(1)} %get-tuple-element.459, s32[]{:T(128)} %get-tuple-element.457, s32[4096]{0:T(1024)S(1)} %bitcast.228, bf16[3,4096,1]{1,0,2:T(4,128)(2,1)S(1)} %get-tuple-element.469), kind=kOutput, calls=%fused_computation.13.clone.1 | convolution fusion | flops 50331648 | bytes 50176 | tf_op jit(solution)/shard_map/while/body/eval_jaxpr/dot_general | solution.py:15
  275.3 45.6 %while.47 = (s32[]{:T(128)}, bf16[3,4096,64]{1,2,0:T(8,128)(2,1)S(1)}, s32[3,4096]{1,0:T(4,128)S(1)}, bf16[3,4096,64]{2,1,0:T(8,128)(2,1)}, s32[]{:T(128)}) while((s32[]{:T(128)}, bf16[3,4096,64]{1,2,0:T(8,128)(2,1)S(1)}, s32[3,4096]{1,0:T(4,128)S(1)}, bf16[3,4096,64]{2,1,0:T(8,128)(2,1)}, s32[]{:T(128)}) %tuple.136), condition=%wide.region_5.6_spmd.clone, body=%wide.region_4.5_spmd.clone.sunk | while | flops 2164523008 | bytes 1623105 | solution.py:72
  275.3 15.2 %fusion.162 = bf16[3,4096,64]{1,2,0:T(8,128)(2,1)S(1)} fusion(bf16[3,4096,64]{1,2,0:T(8,128)(2,1)S(1)} %get-tuple-element.477, s32[]{:T(128)} %get-tuple-element.476, s32[4096]{0:T(1024)S(1)} %bitcast.229, bf16[3,4096,64]{2,1,0:T(8,128)(2,1)} %get-tuple-element.484), kind=kOutput, calls=%fused_computation.26.clone.1 | convolution fusion | flops 2164523008 | bytes 1590272 | tf_op jit(solution)/shard_map/while/body/eval_jaxpr/dot_general | solution.py:19
  290.5 15.2 %fusion.162 = bf16[3,4096,64]{1,2,0:T(8,128)(2,1)S(1)} fusion(bf16[3,4096,64]{1,2,0:T(8,128)(2,1)S(1)} %get-tuple-element.477, s32[]{:T(128)} %get-tuple-element.476, s32[4096]{0:T(1024)S(1)} %bitcast.229, bf16[3,4096,64]{2,1,0:T(8,128)(2,1)} %get-tuple-element.484), kind=kOutput, calls=%fused_computation.26.clone.1 | convolution fusion | flops 2164523008 | bytes 1590272 | tf_op jit(solution)/shard_map/while/body/eval_jaxpr/dot_general | solution.py:19
  305.7 15.2 %fusion.162 = bf16[3,4096,64]{1,2,0:T(8,128)(2,1)S(1)} fusion(bf16[3,4096,64]{1,2,0:T(8,128)(2,1)S(1)} %get-tuple-element.477, s32[]{:T(128)} %get-tuple-element.476, s32[4096]{0:T(1024)S(1)} %bitcast.229, bf16[3,4096,64]{2,1,0:T(8,128)(2,1)} %get-tuple-element.484), kind=kOutput, calls=%fused_computation.26.clone.1 | convolution fusion | flops 2164523008 | bytes 1590272 | tf_op jit(solution)/shard_map/while/body/eval_jaxpr/dot_general | solution.py:19
  326.9 13.5 %all-gather = bf16[4,1,768]{2,1,0:T(2,128)(2,1)S(1)} all-gather(bf16[1,1,768]{2,1,0:T(2,128)(2,1)S(1)} %reshape.296), channel_id=1, replica_groups=mesh['dp'=8,'mp'=4] {'mp'}, dimensions={0}, use_global_device_ids=true | all-gather | bytes 7680 | tf_op jit(solution)/shard_map/all_gather | solution.py:132
  340.5 97.1 %reduce-scatter.5.cloned.1.call-done = bf16[1024,768]{1,0:T(8,128)(2,1)} async-done(((bf16[4096,768]{1,0:T(8,128)(2,1)}), bf16[1024,768]{1,0:T(8,128)(2,1)}) %reduce-scatter.5.cloned.1.call-update) | async-done | bytes 1572880 | tf_op jit(solution)/shard_map/reduce_scatter | solution.py:122
  440.6 85.9 %all-gather.8.cloned.1.call-done = bf16[768,3072]{1,0:T(8,128)(2,1)} async-done(((bf16[768,768]{1,0:T(8,128)(2,1)}), bf16[768,3072]{1,0:T(8,128)(2,1)}) %all-gather.8.cloned.1.call-update) | async-done | bytes 4718608 | tf_op jit(solution)/shard_map/all_gather | solution.py:131
  526.5 38.4 %multiply_convert_fusion = (bf16[1024,3072]{1,0:T(8,128)(2,1)}, f32[1024,3072]{1,0:T(8,128)}, f32[1024,3072]{1,0:T(8,128)}) fusion(f32[3072]{0:T(1024)S(1)} %bitcast.232, bf16[768,3072]{1,0:T(8,128)(2,1)} %all-gather.8.cloned.1.call-done, f32[768]{0:T(1024)S(1)} %copy-done.49, f32[768]{0:T(1024)S(1)} %copy-done.44, f32[1024]{0:T(1024)S(1)} %fusion.93, ...), kind=kOutput, calls=%fused_computation.55 | convolution fusion | flops 5046534144 | bytes 39351296 | tf_op jit(solution)/shard_map/dot_general | solution.py:15
  564.9 50.9 %all-gather.10.cloned.1.call-done = bf16[3072,768]{1,0:T(8,128)(2,1)} async-done(((bf16[768,768]{1,0:T(8,128)(2,1)}), bf16[3072,768]{1,0:T(8,128)(2,1)}) %all-gather.10.cloned.1.call-update) | async-done | bytes 4718608 | tf_op jit(solution)/shard_map/all_gather | solution.py:133
  631.4 19.4 %fusion.107 = (bf16[3072]{0:T(1024)(128)(2,1)}, bf16[1024,3072]{1,0:T(8,128)(2,1)}) fusion(f32[1024,3072]{1,0:T(8,128)} %get-tuple-element.316, bf16[3072,768]{1,0:T(8,128)(2,1)} %all-gather.10.cloned.1.call-done, f32[1024,768]{1,0:T(8,128)} %get-tuple-element.314, f32[1024]{0:T(1024)S(1)} %negate_multiply_fusion.2, f32[1024,3072]{1,0:T(8,128)} %get-tuple-element.328, ...), kind=kOutput, calls=%fused_computation.172 | convolution fusion | flops 4883739648 | bytes 39344128 | tf_op jit(solution)/shard_map/dot_general | solution.py:19
  690.4 90.3 %all-gather.12.cloned.1.call-done = bf16[4096,768]{1,0:T(8,128)(2,1)} async-done(((bf16[1024,768]{1,0:T(8,128)(2,1)}), bf16[4096,768]{1,0:T(8,128)(2,1)}) %all-gather.12.cloned.1.call-update) | async-done | bytes 6291472 | tf_op jit(solution)/shard_map/all_gather | solution.py:164
  788.7 44.7 %while.48 = (s32[]{:T(128)}, bf16[3,4096,64]{1,2,0:T(8,128)(2,1)S(1)}, s32[3,4096]{1,0:T(4,128)S(1)}, bf16[3,4096,64]{2,1,0:T(8,128)(2,1)}, s32[]{:T(128)}) while((s32[]{:T(128)}, bf16[3,4096,64]{1,2,0:T(8,128)(2,1)S(1)}, s32[3,4096]{1,0:T(4,128)S(1)}, bf16[3,4096,64]{2,1,0:T(8,128)(2,1)}, s32[]{:T(128)}) %tuple.137), condition=%wide.region_16.17_spmd.clone, body=%wide.region_15.16_spmd.clone.sunk | while | flops 2164523008 | bytes 1623105 | solution.py:171
  788.7 14.9 %fusion.164 = bf16[3,4096,64]{1,2,0:T(8,128)(2,1)S(1)} fusion(bf16[3,4096,64]{1,2,0:T(8,128)(2,1)S(1)} %get-tuple-element.492, s32[]{:T(128)} %get-tuple-element.491, s32[4096]{0:T(1024)S(1)} %bitcast.230, bf16[3,4096,64]{2,1,0:T(8,128)(2,1)} %get-tuple-element.499), kind=kOutput, calls=%fused_computation.36.clone.1 | convolution fusion | flops 2164523008 | bytes 1590272 | tf_op jit(solution)/shard_map/while/body/eval_jaxpr/dot_general | solution.py:15
  803.7 14.8 %fusion.164 = bf16[3,4096,64]{1,2,0:T(8,128)(2,1)S(1)} fusion(bf16[3,4096,64]{1,2,0:T(8,128)(2,1)S(1)} %get-tuple-element.492, s32[]{:T(128)} %get-tuple-element.491, s32[4096]{0:T(1024)S(1)} %bitcast.230, bf16[3,4096,64]{2,1,0:T(8,128)(2,1)} %get-tuple-element.499), kind=kOutput, calls=%fused_computation.36.clone.1 | convolution fusion | flops 2164523008 | bytes 1590272 | tf_op jit(solution)/shard_map/while/body/eval_jaxpr/dot_general | solution.py:15
  818.5 14.8 %fusion.164 = bf16[3,4096,64]{1,2,0:T(8,128)(2,1)S(1)} fusion(bf16[3,4096,64]{1,2,0:T(8,128)(2,1)S(1)} %get-tuple-element.492, s32[]{:T(128)} %get-tuple-element.491, s32[4096]{0:T(1024)S(1)} %bitcast.230, bf16[3,4096,64]{2,1,0:T(8,128)(2,1)} %get-tuple-element.499), kind=kOutput, calls=%fused_computation.36.clone.1 | convolution fusion | flops 2164523008 | bytes 1590272 | tf_op jit(solution)/shard_map/while/body/eval_jaxpr/dot_general | solution.py:15
  853.6 15.6 %reduce-scatter.9.cloned.1.call-done = bf16[768,768]{1,0:T(8,128)(2,1)} async-done(((bf16[3072,768]{1,0:T(8,128)(2,1)}), bf16[768,768]{1,0:T(8,128)(2,1)}) %reduce-scatter.9.cloned.1.call-update) | async-done | bytes 1179664 | tf_op jit(solution)/shard_map/reduce_scatter | solution.py:150
  877.8 56.9 %while.49 = (s32[]{:T(128)}, bf16[3,4096,192]{1,2,0:T(8,128)(2,1)}, s32[3,4096]{1,0:T(4,128)S(1)}, bf16[3,4096,192]{1,2,0:T(8,128)(2,1)}, s32[]{:T(128)}) while((s32[]{:T(128)}, bf16[3,4096,192]{1,2,0:T(8,128)(2,1)}, s32[3,4096]{1,0:T(4,128)S(1)}, bf16[3,4096,192]{1,2,0:T(8,128)(2,1)}, s32[]{:T(128)}) %tuple.138), condition=%wide.region_19.20_spmd.clone, body=%wide.region_18.19_spmd.clone.sunk | while | flops 6460014592 | bytes 3195969 | solution.py:72
  878.2 18.9 %fusion.166 = bf16[3,4096,192]{1,2,0:T(8,128)(2,1)} fusion(bf16[3,4096,192]{1,2,0:T(8,128)(2,1)} %get-tuple-element.507, s32[]{:T(128)} %get-tuple-element.506, s32[4096]{0:T(1024)S(1)} %bitcast.231, bf16[3,4096,192]{1,2,0:T(8,128)(2,1)} %get-tuple-element.514), kind=kOutput, calls=%fused_computation.46.clone.1 | convolution fusion | flops 6460014592 | bytes 3163136 | tf_op jit(solution)/shard_map/while/body/eval_jaxpr/dot_general | solution.py:19
  897.1 18.8 %fusion.166 = bf16[3,4096,192]{1,2,0:T(8,128)(2,1)} fusion(bf16[3,4096,192]{1,2,0:T(8,128)(2,1)} %get-tuple-element.507, s32[]{:T(128)} %get-tuple-element.506, s32[4096]{0:T(1024)S(1)} %bitcast.231, bf16[3,4096,192]{1,2,0:T(8,128)(2,1)} %get-tuple-element.514), kind=kOutput, calls=%fused_computation.46.clone.1 | convolution fusion | flops 6460014592 | bytes 3163136 | tf_op jit(solution)/shard_map/while/body/eval_jaxpr/dot_general | solution.py:19
  915.9 18.8 %fusion.166 = bf16[3,4096,192]{1,2,0:T(8,128)(2,1)} fusion(bf16[3,4096,192]{1,2,0:T(8,128)(2,1)} %get-tuple-element.507, s32[]{:T(128)} %get-tuple-element.506, s32[4096]{0:T(1024)S(1)} %bitcast.231, bf16[3,4096,192]{1,2,0:T(8,128)(2,1)} %get-tuple-element.514), kind=kOutput, calls=%fused_computation.46.clone.1 | convolution fusion | flops 6460014592 | bytes 3163136 | tf_op jit(solution)/shard_map/while/body/eval_jaxpr/dot_general | solution.py:19
  961.8 13.8 %add_convert_fusion = bf16[4096,768]{1,0:T(8,128)(2,1)} fusion(f32[4096,768]{1,0:T(8,128)} %fusion.108, f32[4096,768]{1,0:T(8,128)} %fusion.109, bf16[4096,192]{0,1:T(8,128)(2,1)S(1)} %bitcast.212, bf16[768,192]{0,1:T(8,128)(2,1)S(1)} %copy-done.30), kind=kOutput, calls=%fused_computation.53 | convolution fusion | flops 1217396736 | bytes 33325056 | tf_op jit(solution)/shard_map/dot_general | solution.py:19
  977.9 41.8 %all-reduce.1 = (f32[768]{0:T(1024)}, f32[768]{0:T(1024)}, f32[768]{0:T(1024)}, f32[768]{0:T(1024)}, f32[768]{0:T(1024)}, /*index=5*/f32[768]{0:T(1024)}) all-reduce(f32[768]{0:T(1024)S(1)} %copy-done.41, f32[768]{0:T(1024)S(1)} %copy-done.45, f32[768]{0:T(1024)S(1)} %copy-done.46, ...), channel_id=1, replica_groups=mesh['dp'=8,'mp'=4] {'dp','mp'}, use_global_device_ids=true, to_apply=%region_30.31 | all-reduce | flops 4608 | bytes 36864 | tf_op jit(solution)/shard_map/psum | solution.py:221
  1032.7 67.3 %all-reduce.8 = (f32[192]{0:T(256)}, f32[192]{0:T(256)}, f32[768]{0:T(1024)}, f32[768,768]{1,0:T(8,128)}) all-reduce(f32[192]{0:T(256)S(1)} %reduce_sum.221, f32[192]{0:T(256)S(1)} %reduce_sum.223, f32[768]{0:T(1024)S(1)} %dynamic-slice_convert_fusion, ...), channel_id=1, replica_groups=mesh['dp'=8,'mp'=4] {'dp'}, use_global_device_ids=true, to_apply=%region_23.24 | all-reduce | flops 590976 | bytes 3548160 | tf_op jit(solution)/shard_map/psum | solution.py:243
  1103.0 76.1 %reduce-scatter.7.cloned.1.call-done = bf16[1024,768]{1,0:T(8,128)(2,1)} async-done(((bf16[4096,768]{1,0:T(8,128)(2,1)}), bf16[1024,768]{1,0:T(8,128)(2,1)}) %reduce-scatter.7.cloned.1.call-update) | async-done | bytes 1572880 | tf_op jit(solution)/shard_map/reduce_scatter | solution.py:213
  (224 shorter events, 211.2 us)
Async XLA Ops:
  7.2 313.8 %copy-start = (bf16[192,768]{1,0:T(8,128)(2,1)S(1)}, bf16[192,768]{1,0:T(8,128)(2,1)}, u32[]{:S(2)}) copy-start(bf16[192,768]{1,0:T(8,128)(2,1)} %param.33) | copy-start | bytes 884740
  7.2 116.2 %all-gather.6.cloned.1.call-start = ((), (), s32[]{:S(2)}) async-start(), calls=%async_computation.4 | async-start | bytes 7864320 | tf_op jit(solution)/shard_map/all_gather | solution.py:86
  7.9 429.7 %reduce-scatter.5.cloned.1.call-start = ((), (), s32[]{:S(2)}) async-start(), calls=%async_computation.5 | async-start | bytes 7864320 | tf_op jit(solution)/shard_map/reduce_scatter | solution.py:122
  153.3 8.0 copy-start.35
  259.5 8.9 copy-start.20
  262.2 6.2 copy-start.7
  325.5 112.1 %copy-start.4 = (bf16[1024,768]{1,0:T(8,128)(2,1)S(1)}, bf16[1024,768]{1,0:T(8,128)(2,1)}, u32[]{:S(2)}) copy-start(bf16[1024,768]{1,0:T(8,128)(2,1)} %param.27) | copy-start | bytes 4718596
  325.5 112.1 %copy-start.32 = (f32[768]{0:T(1024)S(1)}, f32[768]{0:T(1024)}, u32[]{:S(2)}) copy-start(f32[768]{0:T(1024)} %param.34) | copy-start | bytes 9220
  325.5 201.0 %all-gather.8.cloned.1.call-start = ((), (), s32[]{:S(2)}) async-start(), calls=%async_computation.6 | async-start | bytes 5898240 | tf_op jit(solution)/shard_map/all_gather | solution.py:131
  326.3 289.5 %all-gather.10.cloned.1.call-start = ((), (), s32[]{:S(2)}) async-start(), calls=%async_computation.7 | async-start | bytes 5898240 | tf_op jit(solution)/shard_map/all_gather | solution.py:133
  326.9 453.9 %all-gather.12.cloned.1.call-start = ((), (), s32[]{:S(2)}) async-start(), calls=%async_computation.8 | async-start | bytes 7864320 | tf_op jit(solution)/shard_map/all_gather | solution.py:164
  340.5 186.1 %copy-start.44 = (f32[768]{0:T(1024)S(1)}, f32[768]{0:T(1024)}, u32[]{:S(2)}) copy-start(f32[768]{0:T(1024)} %param.35) | copy-start | bytes 9220
  340.5 186.1 %copy-start.49 = (f32[768]{0:T(1024)S(1)}, f32[768]{0:T(1024)}, u32[]{:S(2)}) copy-start(f32[768]{0:T(1024)} %param.36) | copy-start | bytes 9220
  526.5 89.3 %copy-start.48 = (f32[768]{0:T(1024)S(1)}, f32[768]{0:T(1024)}, u32[]{:S(2)}) copy-start(f32[768]{0:T(1024)} %param.40) | copy-start | bytes 9220
  631.4 46.4 %copy-start.37 = (f32[1024]{0:T(1024)}, f32[1024]{0:T(1024)S(1)}, u32[]{:S(2)}) copy-start(f32[1024]{0:T(1024)S(1)} %negate_multiply_fusion.2) | copy-start | bytes 12292
  667.0 202.2 %reduce-scatter.9.cloned.1.call-start = ((), (), s32[]{:S(2)}) async-start(), calls=%async_computation.10 | async-start | bytes 5898240 | tf_op jit(solution)/shard_map/reduce_scatter | solution.py:150
  677.8 354.9 %reduce-scatter.11.cloned.1.call-start = ((), (), s32[]{:S(2)}) async-start(), calls=%async_computation.11 | async-start | bytes 5898240 | tf_op jit(solution)/shard_map/reduce_scatter | solution.py:153
  690.4 409.6 %all-reduce.7.cloned.1.call-start = ((), (), s32[]{:S(2)}) async-start(), calls=%async_computation.12 | async-start | bytes 9437184 | tf_op jit(solution)/shard_map/psum | solution.py:243
  788.7 44.7 %copy-start.8 = (bf16[3,8,32,8,128]{4,3,2,1,0:T(8,128)(2,1)S(1)}, bf16[3,8,32,8,128]{4,3,2,1,0:T(8,128)(2,1)}, u32[]{:S(2)}) copy-start(bf16[3,8,32,8,128]{4,3,2,1,0:T(8,128)(2,1)} %copy-done.7) | copy-start | bytes 4718596
  788.7 44.7 %copy-start.21 = (f32[3,4096,1]{1,2,0:T(1,128)S(1)}, f32[3,4096,1]{1,2,0:T(1,128)}, u32[]{:S(2)}) copy-start(f32[3,4096,1]{1,2,0:T(1,128)} %copy-done.20) | copy-start | bytes 147460
  833.3 6.9 slice-start
  833.4 6.9 slice-start.1
  833.4 6.9 copy-start.25
  844.0 7.2 slice-start.4
  934.7 8.6 slice-start.2
  947.8 231.3 %reduce-scatter.7.cloned.1.call-start = ((), (), s32[]{:S(2)}) async-start(), calls=%async_computation.9 | async-start | bytes 7864320 | tf_op jit(solution)/shard_map/reduce_scatter | solution.py:213
  948.0 7.4 copy-start.31
  955.4 6.4 copy-start.17
  955.4 6.4 copy-start.30
  975.7 44.0 %copy-start.42 = (bf16[3072]{0:T(1024)(128)(2,1)S(1)}, bf16[3072]{0:T(1024)(128)(2,1)}, u32[]{:S(2)}) copy-start(bf16[3072]{0:T(1024)(128)(2,1)} %get-tuple-element.334) | copy-start | bytes 18436
  1032.5 146.6 %copy-start.3 = (f32[1024,768]{1,0:T(8,128)S(1)}, f32[1024,768]{1,0:T(8,128)}, u32[]{:S(2)}) copy-start(f32[1024,768]{1,0:T(8,128)} %copy-done.2) | copy-start | bytes 9437188
  1032.5 146.6 %copy-start.34 = (f32[1024]{0:T(1024)S(1)}, f32[1024]{0:T(1024)}, u32[]{:S(2)}) copy-start(f32[1024]{0:T(1024)} %copy-done.33) | copy-start | bytes 12292
  (34 other events, 95.9 us)
Sparse Core Ops, SparseCore 0:
  9.6 113.7 all-gather.5
  325.7 111.8 reduce-scatter.4
  439.2 87.3 all-gather.7
  528.0 87.8 all-gather.9
  667.1 113.5 all-gather.11
  782.9 86.2 reduce-scatter.8
  871.4 85.7 reduce-scatter.10
  962.2 100.0 all-reduce.6
  1064.7 114.3 reduce-scatter.6
where the time goes:
time: 1200 us; the launch traced here: 1190 us
  waiting for transfers between devices  531 us (44%)
  matrix products  430 us (36%)
  blocking collectives  133 us (11%)
  local copies, waits for them, and re-layouts  43.8 us (4%)
  other arithmetic  37.7 us (3%)
  between operations  15.5 us (1%)
    dot_general x15, matrix products, matmul(): return jnp.dot(left, right, preferred_element_type=jnp.float32)  210 us
    dot_general x18, matrix products, contract(): lax.dot_general(left, right, (((left_dim,), (right_dim,)), ((), ())), pre...  198 us
    all_gather x1, waiting for transfers between devices, body(): gathered = lax.all_gather(tokens, 'mp', axis=0, tiled=True)  113 us
    reduce_scatter x1, waiting for transfers between devices, body(): lax.psum_scatter(matmul(context, w_out).astype(jnp.bfloat16), 'mp', scatt...  97.1 us
    all_gather x1, waiting for transfers between devices, body(): grad_att_rows = lax.all_gather(grad_att, 'mp', axis=0, tiled=True)  90.3 us
    all_gather x1, waiting for transfers between devices, body(): lax.all_gather(w_up, 'mp', axis=1, tiled=True)  85.9 us
    reduce_scatter x1, waiting for transfers between devices, body(): lax.psum_scatter((term + contract(grad_v, w_value, 1, 1)).astype(jnp.bflo...  76.1 us
    psum x1, blocking collectives, body(): lax.psum((grad_w_query, grad_b_query, grad_w_key, grad_w_value, grad_b_va...  67.3 us
  transfers between devices with their start and end apart: 9, of which 7 were waited for; matrix products, arithmetic and copies ran while one was open for 21% of the time, Pallas kernels for 0%

commit v1 on v0

v1 whole, which is shorter than its diff:
```python
import functools
import jax
import jax.numpy as jnp
from jax import lax
from jax.experimental import pallas as pl
from jax.experimental.pallas import tpu as pltpu
from jax.sharding import PartitionSpec as P

L = 4096
C = 128
HD = 64
F32 = jnp.float32
BF16 = jnp.bfloat16
VMEM = pltpu.VMEM


def dot(a, b, da, db):
    return lax.dot_general(a, b, (((da,), (db,)), ((), ())), preferred_element_type=F32)


def attend_kernel(first, ord_ref, qkv_ref, c_ref, ts_ref, pr_ref, src, ctx, buf_a, buf_b, out_a, out_b):
    head = pl.program_id(0) + first
    live = ord_ref[3 * L]
    base = head * L

    src[:, 0, :] = qkv_ref[0, :, :C].astype(F32)
    src[:, 1, :] = qkv_ref[0, :, C:].astype(F32)

    def gather(cluster, buf):
        start = base + cluster * C
        for u in range(C):
            buf[u] = src[ord_ref[start + u]]

    def compute(cluster, buf, out):
        rows = pl.ds(pl.multiple_of(cluster * C, C), C)
        t0 = buf[:, 0, :].astype(BF16)
        t1 = buf[:, 1, :].astype(BF16)
        ts_ref[0, rows, :C] = t0
        ts_ref[0, rows, C:] = t1
        slot = cluster * C + lax.broadcasted_iota(jnp.int32, (1, C), 1)
        penalty = jnp.where(slot < live, 0.0, -10000.0)
        scores = dot(t0, t1, 1, 1) * 0.125 + penalty
        peak = jnp.max(scores, axis=-1, keepdims=True)
        e = jnp.exp(scores - peak)
        probs = e * (1.0 / jnp.sum(e, axis=-1, keepdims=True))
        pr_ref[0, rows, :] = probs
        out[...] = jnp.dot(probs.astype(BF16), t0, preferred_element_type=F32)

    def scatter(cluster, out):
        start = base + cluster * C
        for u in range(C):
            ctx[pl.ds(ord_ref[start + u], 1), :] = out[pl.ds(u, 1), :]

    last = L // C - 1
    gather(0, buf_a)

    def pair(i, _):
        gather(2 * i + 1, buf_b)
        compute(2 * i, buf_a, out_a)
        scatter(jnp.maximum(2 * i - 1, 0), out_b)
        gather(jnp.minimum(2 * i + 2, last), buf_a)
        compute(2 * i + 1, buf_b, out_b)
        scatter(2 * i, out_a)
        return 0

    lax.fori_loop(0, L // C // 2, pair, 0)
    scatter(last, out_b)

    lane = lax.broadcasted_iota(jnp.int32, (1, C), 1)
    if first == 2:
        for k in range(4):
            low = ctx[pl.ds(k * 1024, 512), :]
            high = pltpu.roll(ctx[pl.ds(k * 1024 + 512, 512), :], HD, 1)
            c_ref[pl.ds(k * 512, 512), :] = jnp.where(lane < HD, low, high).astype(BF16)
    else:

        @pl.when(head == 0)
        def _():
            c_ref[...] = ctx[...].astype(BF16)

        @pl.when(head == 1)
        def _():
            c_ref[...] = jnp.where(lane < HD, c_ref[...], ctx[...].astype(BF16))


def attend(first, order, qkv):
    heads = 2 if first == 0 else 1
    whole = lambda shape: pl.BlockSpec(shape, lambda h: (0,) * len(shape), pipeline_mode=pl.Buffered(1))
    in_head = lambda shape: pl.BlockSpec((1,) + shape, lambda h: (h + first, 0, 0))
    per_head = lambda shape: pl.BlockSpec((1,) + shape, lambda h: (h, 0, 0))
    out_rows = L if first == 0 else L // 2
    return pl.pallas_call(
        functools.partial(attend_kernel, first),
        grid=(heads,),
        in_specs=[pl.BlockSpec(memory_space=pltpu.SMEM), in_head((L, 2 * C))],
        out_specs=[whole((out_rows, C)), per_head((L, 2 * C)), per_head((L, C))],
        out_shape=[
            jax.ShapeDtypeStruct((out_rows, C), BF16),
            jax.ShapeDtypeStruct((heads, L, 2 * C), BF16),
            jax.ShapeDtypeStruct((heads, L, C), F32),
        ],
        scratch_shapes=[
            VMEM((L, 2, C), F32), VMEM((L, C), F32),
            VMEM((C, 2, C), F32), VMEM((C, 2, C), F32), VMEM((C, C), F32), VMEM((C, C), F32),
        ],
        compiler_params=pltpu.CompilerParams(vmem_limit_bytes=56 << 20),
        cost_estimate=pl.CostEstimate(flops=heads * 18 * 10**9, bytes_accessed=10 << 20, transcendentals=0),
        name="attend",
    )(order, qkv)


def attend_back_kernel(head, ord_ref, g_ref, ts_ref, pr_ref, d_ref, gsrc, dst, buf_a, buf_b, out_a, out_b):
    base = head * L
    lane = lax.broadcasted_iota(jnp.int32, (1, C), 1)
    if head == 2:
        for k in range(4):
            both = g_ref[pl.ds(k * 512, 512), :].astype(F32)
            gsrc[pl.ds(k * 1024, 512), :] = both
            gsrc[pl.ds(k * 1024 + 512, 512), :] = pltpu.roll(both, HD, 1)
    else:
        gsrc[...] = g_ref[...].astype(F32)

    keep = (lane >= HD) if head == 1 else (lane < HD)

    def gather(cluster, buf):
        start = base + cluster * C
        for u in range(C):
            buf[pl.ds(u, 1), :] = gsrc[pl.ds(ord_ref[start + u], 1), :]

    def compute(cluster, buf, out):
        rows = pl.ds(pl.multiple_of(cluster * C, C), C)
        t0 = ts_ref[0, rows, :C]
        t1 = ts_ref[0, rows, C:]
        probs = pr_ref[0, rows, :]
        g = jnp.where(keep, buf[...], 0.0).astype(BF16)
        dp = dot(g, t0, 1, 1)
        row = jnp.sum(probs * dp, axis=-1, keepdims=True)
        ds = (probs * (dp - row)).astype(BF16)
        out[:, 0, :] = jnp.dot(ds, t1, preferred_element_type=F32) * 0.125 + dot(probs.astype(BF16), g, 0, 0)
        out[:, 1, :] = dot(ds, t0, 0, 0) * 0.125

    def scatter(cluster, out):
        start = base + cluster * C
        for u in range(C):
            dst[ord_ref[start + u]] = out[u]

    last = L // C - 1
    gather(0, buf_a)

    def pair(i, _):
        gather(2 * i + 1, buf_b)
        compute(2 * i, buf_a, out_a)
        scatter(jnp.maximum(2 * i - 1, 0), out_b)
        gather(jnp.minimum(2 * i + 2, last), buf_a)
        compute(2 * i + 1, buf_b, out_b)
        scatter(2 * i, out_a)
        return 0

    lax.fori_loop(0, L // C // 2, pair, 0)
    scatter(last, out_b)

    d_ref[:, :C] = dst[:, 0, :].astype(BF16)
    d_ref[:, C:] = dst[:, 1, :].astype(BF16)


def attend_back(head, order, g, ts, probs):
    i = head % 2
    vm = pl.BlockSpec(memory_space=pltpu.VMEM)
    one = lambda shape: pl.BlockSpec((1,) + shape, lambda h: (i, 0, 0), pipeline_mode=pl.Buffered(1))
    return pl.pallas_call(
        functools.partial(attend_back_kernel, head),
        grid=(1,),
        in_specs=[pl.BlockSpec(memory_space=pltpu.SMEM), vm, one((L, 2 * C)), one((L, C))],
        out_specs=vm,
        out_shape=jax.ShapeDtypeStruct((L, 2 * C), BF16),
        scratch_shapes=[
            VMEM((L, C), F32), VMEM((L, 2, C), F32),
            VMEM((C, C), F32), VMEM((C, C), F32), VMEM((C, 2, C), F32), VMEM((C, 2, C), F32),
        ],
        compiler_params=pltpu.CompilerParams(vmem_limit_bytes=40 << 20),
        cost_estimate=pl.CostEstimate(flops=24 * 10**9, bytes_accessed=10 << 20, transcendentals=0),
        name="attend_back",
    )(order, g, ts, probs)


MESH = pl.DeviceIdType.MESH
WIDTH = 768
ROWS = 1024
SUB = 512
SUBS = ROWS // SUB
SHARE = 224
PACK = 8 * SHARE
OUT_ROW = 1536
BIAS_ROW = 1728
QUARTER = 192
ORDER = 3 * L + 128
DMA = pltpu.SemaphoreType.DMA
ANY = pl.BlockSpec(memory_space=pl.ANY)
VM = pl.BlockSpec(memory_space=pltpu.VMEM)
sds = jax.ShapeDtypeStruct


def place():
    dp, mp = lax.axis_index("dp"), lax.axis_index("mp")
    core = lax.rem(dp, 2)
    return dp, mp, core, jnp.where(core == 0, mp, 3 - mp)


def at(dp, mp):
    return {"dp": dp, "mp": mp}


def signal(barrier, device):
    pl.semaphore_signal(barrier, inc=1, device_id=device, device_id_type=MESH)


def send(src, dst, send_sem, recv_sem, device):
    copy = pltpu.make_async_remote_copy(
        src_ref=src, dst_ref=dst, send_sem=send_sem, recv_sem=recv_sem, device_id=device, device_id_type=MESH
    )
    copy.start()
    return copy


def wait(ref, sem):
    pltpu.make_async_copy(ref, ref, sem).wait()


def mate(dp, rel):
    return dp + 2 * ((lax.rem(dp, 8) // 2 ^ rel) - lax.rem(dp, 8) // 2)


def greet(barrier, both_cores):
    dp, mp, core, t = place()
    step = 1 - 2 * core
    for k in range(4):
        if k:
            signal(barrier, at(dp, lax.rem(mp + k, 4)))
        signal(barrier, at(dp + step, lax.rem(mp + k, 4)))
    for rel in (1, 2, 3):
        signal(barrier, at(mate(dp, rel), mp))
        if both_cores:
            signal(barrier, at(mate(dp, rel) + step, mp))
    pl.semaphore_wait(barrier, 13 if both_cores else 10)


def worker(group, half, dp_base):
    return at(dp_base + group % 2, 2 * half + group // 2)


def chain_device(u, half, dp_base):
    return at(dp_base + half, jnp.where(half == 0, u, 3 - u))


def collect_kernel(x_ref, wsrc_ref, bsrc_ref, osrc_ref, up_ref, down_ref, wout_ref, extra_ref, xs_ref, qkv_ref, w_ref, ord_ref, share_ref,
                   xs, qkv, w, bias, relay,
                   chain_recv, relay_recv, pair_recv, chain_send, relay_send, pair_send, own_sem,
                   wz_recv, wz_send, wp_recv, wp_send, b_recv, b_send, o_recv, o_send, xs_out, qkv_out, w_out, share_sem):
    dp, mp, core, t = place()
    base, half, spot = dp - core, mp // 2, lax.rem(dp, 8) // 2
    step = 1 - 2 * core
    partner, lower, upper = at(dp + step, mp), at(dp, mp - step), at(dp, mp + step)
    group = lax.rem(mp, 2) * 2 + core
    gives = core == lax.rem(mp, 2)
    order_self = worker(mp, core, base)
    order_here = (order_self["dp"] == dp) & (order_self["mp"] == mp)
    cut = lambda s: pl.ds(s * SUB, SUB)
    home = lambda u, s: xs.at[pl.ds(pl.multiple_of(u * ROWS + s * SUB, SUB), SUB)]
    quarter = lambda q: pl.ds(pl.multiple_of(q * QUARTER, QUARTER), QUARTER)

    own = pltpu.make_async_copy(x_ref, xs.at[pl.ds(pl.multiple_of(jnp.minimum(t, 1) * ROWS, ROWS), ROWS)], own_sem)

    @pl.when(t <= 1)
    def _():
        own.start()

    greet(pltpu.get_barrier_semaphore(), False)

    for far in (0, 1):
        target = mp // 2 + 2 * far

        @pl.when(gives & (target != mp))
        def _():
            send(wsrc_ref.at[quarter(spot)], w.at[quarter(spot)], wz_send.at[far], wz_recv, at(dp, target))
            send(bsrc_ref, bias, b_send.at[far], b_recv, at(dp, target))

        @pl.when(gives & (target == mp))
        def _():
            pltpu.make_async_copy(wsrc_ref.at[quarter(spot)], w.at[quarter(spot)], wz_recv).start()
            pltpu.make_async_copy(bsrc_ref, bias, b_recv).start()

    @pl.when(order_here)
    def _():
        pltpu.make_async_copy(osrc_ref, ord_ref, o_recv).start()

    @pl.when(jnp.logical_not(order_here))
    def _():
        send(osrc_ref, ord_ref, o_send, o_recv, order_self)

    @pl.when(t == 3)
    def _():
        for s in range(SUBS):
            send(x_ref.at[cut(s)], relay.at[cut(s)], chain_send.at[0, s], relay_recv.at[s], lower)

    @pl.when((t == 1) | (t == 2))
    def _():
        for s in range(SUBS):
            send(x_ref.at[cut(s)], home(t, s), chain_send.at[0, s], chain_recv.at[t, s], lower)

    @pl.when(t == 0)
    def _():
        for s in range(SUBS):
            send(x_ref.at[cut(s)], home(0, s), chain_send.at[0, s], chain_recv.at[0, s], upper)

    pack = ((0, up_ref), (768, down_ref), (OUT_ROW, wout_ref), (BIAS_ROW, extra_ref))
    for i in range(8):
        @pl.when(lax.rem(dp, 8) == i)
        def _():
            for first, part in pack:
                low, high = max(first, i * SHARE), min(first + part.shape[0], (i + 1) * SHARE)
                if low < high:
                    src = part.at[pl.ds(low - first, high - low)]
                    pltpu.make_async_copy(src, share_ref.at[pl.ds(low - i * SHARE, high - low)], share_sem).start()

    wait(w.at[quarter(spot)], wz_recv)
    for rel in (1, 2, 3):
        send(w.at[quarter(spot)], w.at[quarter(spot)], wp_send.at[rel], wp_recv.at[rel], at(mate(dp, rel), mp))

    @pl.when(t <= 1)
    def _():
        own.wait()
        for s in range(SUBS):
            send(home(t, s), home(t, s), pair_send.at[t, s], pair_recv.at[t, s], partner)

    tt = jnp.minimum(t, 3 - t)

    def rows_of(i, s):
        return pl.ds(pl.multiple_of(lax.rem(tt + i, 4) * ROWS + s * SUB, SUB), SUB)

    def receive(i, s):
        u = lax.rem(tt + i, 4)
        if i == 1:
            @pl.when(t == 2)
            def _():
                wait(relay.at[cut(s)], relay_recv.at[s])
                send(relay.at[cut(s)], home(3, s), relay_send.at[s], chain_recv.at[3, s], lower)

        if i > 0:
            @pl.when(t <= 1)
            def _():
                wait(home(u, s), chain_recv.at[u, s])
                if i < 3:
                    @pl.when(t == 1)
                    def _():
                        send(home(u, s), home(u, s), chain_send.at[i, s], chain_recv.at[u, s], lower)
                send(home(u, s), home(u, s), pair_send.at[u, s], pair_recv.at[u, s], partner)

        @pl.when(t >= 2)
        def _():
            wait(home(u, s), pair_recv.at[u, s])

        rows = rows_of(i, s)
        pltpu.make_async_copy(xs.at[rows], xs_ref.at[rows], xs_out.at[i, s]).start()

    def project(i, s):
        rows = rows_of(i, s)
        row = jnp.concatenate([bias[pl.ds(h, 1), :] for h in range(3)], axis=1)
        qkv[rows, :] = (dot(xs[rows, :], w[...], 1, 1) + row).astype(BF16)
        for h in range(3):
            pltpu.make_async_copy(qkv.at[rows, pl.ds(h * 256, 256)], qkv_ref.at[h, rows], qkv_out.at[i, s, h]).start()

    pieces = [(i, s) for i in range(4) for s in range(SUBS)]
    for i, s in pieces[:4]:
        receive(i, s)
    for rel in (1, 2, 3):
        wait(w.at[quarter(spot ^ rel)], wp_recv.at[rel])
    wait(bias, b_recv)
    pltpu.make_async_copy(w, w_ref, w_out).start()
    for i, s in pieces[:3]:
        project(i, s)
    for k in range(4, len(pieces)):
        receive(*pieces[k])
        project(*pieces[k - 1])
    project(*pieces[-1])

    for i in range(4):
        u = lax.rem(tt + i, 4)
        for s in range(SUBS):
            rows = pl.ds(pl.multiple_of(u * ROWS + s * SUB, SUB), SUB)
            wait(xs.at[rows], xs_out.at[i, s])
            for h in range(3):
                wait(qkv_ref.at[h, rows], qkv_out.at[i, s, h])

            @pl.when(t <= 1)
            def _():
                wait(home(u, s), pair_send.at[u, s])
    for s in range(SUBS):
        wait(x_ref.at[cut(s)], chain_send.at[0, s])

        @pl.when(t == 1)
        def _():
            wait(x_ref.at[cut(s)], chain_send.at[1, s])
            wait(x_ref.at[cut(s)], chain_send.at[2, s])

        @pl.when(t == 2)
        def _():
            wait(relay.at[cut(s)], relay_send.at[s])
    for rel in (1, 2, 3):
        wait(w.at[quarter(spot)], wp_send.at[rel])
    for far in (0, 1):
        @pl.when(gives & (mp // 2 + 2 * far != mp))
        def _():
            wait(wsrc_ref.at[quarter(spot)], wz_send.at[far])
            wait(bsrc_ref, b_send.at[far])
    wait(ord_ref, o_recv)

    @pl.when(jnp.logical_not(order_here))
    def _():
        wait(osrc_ref, o_send)

    wait(w, w_out)
    wait(share_ref, share_sem)


def collect(x, w, b, order, up, down, out, extra):
    return pl.pallas_call(
        collect_kernel,
        out_shape=[sds((4 * ROWS, WIDTH), BF16), sds((3, 4 * ROWS, 256), BF16), sds((WIDTH, WIDTH), BF16), sds((ORDER,), jnp.int32), sds((SHARE, WIDTH), BF16)],
        in_specs=[ANY] * 8,
        out_specs=[ANY] * 5,
        scratch_shapes=[
            VMEM((4 * ROWS, WIDTH), BF16), VMEM((4 * ROWS, WIDTH), BF16), VMEM((WIDTH, WIDTH), BF16), VMEM((8, 256), F32),
            VMEM((ROWS, WIDTH), BF16),
            DMA((4, SUBS)), DMA((SUBS,)), DMA((4, SUBS)), DMA((3, SUBS)), DMA((SUBS,)), DMA((4, SUBS)), DMA,
            DMA, DMA((2,)), DMA((4,)), DMA((4,)), DMA, DMA((2,)), DMA, DMA, DMA((4, SUBS)), DMA((4, SUBS, 3)), DMA, DMA,
        ],
        compiler_params=pltpu.CompilerParams(collective_id=0, has_side_effects=True, vmem_limit_bytes=40 << 20),
        name="collect",
    )(x, w, b, order, up, down, out, extra)


def greet_exchange(barrier):
    dp, mp, core, t = place()
    half, base = mp // 2, dp - core
    mine = lax.rem(mp, 2) * 2 + core
    for u in range(4):
        @pl.when((half != core) | (t != u))
        def _():
            pl.semaphore_signal(barrier, inc=1, device_id=chain_device(u, half, base), device_id_type=MESH)
    for g in range(4):
        @pl.when((half != core) | (mine != g))
        def _():
            pl.semaphore_signal(barrier, inc=1, device_id=worker(g, core, base), device_id_type=MESH)

    @pl.when(half == core)
    def _():
        pl.semaphore_wait(barrier, 6)

    @pl.when(half != core)
    def _():
        pl.semaphore_wait(barrier, 8)


def spread_kernel(a_ref, b_ref, oa_ref, ob_ref, send_sem, recv_sem, local_sem):
    dp, mp, core, t = place()
    half, base = mp // 2, dp - core
    mine = lax.rem(mp, 2) * 2 + core
    greet_exchange(pltpu.get_barrier_semaphore())
    for u in (3, 2, 1, 0):
        pair = ((a_ref.at[pl.ds(u * 1024, 1024)], oa_ref.at[mine]), (b_ref.at[pl.ds(u * 512, 512)], ob_ref.at[mine]))
        for k, (src, dst) in enumerate(pair):
            @pl.when((half != core) | (t != u))
            def _():
                send(src, dst, send_sem.at[u, k], recv_sem.at[mine, k], chain_device(u, half, base))

            @pl.when((half == core) & (t == u))
            def _():
                pltpu.make_async_copy(src, dst, local_sem.at[k]).start()
    for u in range(4):
        for k, src in enumerate((a_ref.at[pl.ds(u * 1024, 1024)], b_ref.at[pl.ds(u * 512, 512)])):
            @pl.when((half != core) | (t != u))
            def _():
                pltpu.make_async_copy(src, src, send_sem.at[u, k]).wait()
    for g in range(4):
        for k, dst in enumerate((oa_ref.at[g], ob_ref.at[g])):
            @pl.when((half != core) | (mine != g))
            def _():
                pltpu.make_async_copy(dst, dst, recv_sem.at[g, k]).wait()

            @pl.when((half == core) & (mine == g))
            def _():
                pltpu.make_async_copy(dst, dst, local_sem.at[k]).wait()


def spread(a, b):
    return pl.pallas_call(
        spread_kernel,
        out_shape=[jax.ShapeDtypeStruct((4, 1024, C), BF16), jax.ShapeDtypeStruct((4, 512, C), BF16)],
        in_specs=[ANY, ANY],
        out_specs=[ANY, ANY],
        scratch_shapes=[DMA((4, 2)), DMA((4, 2)), DMA((2,))],
        compiler_params=pltpu.CompilerParams(collective_id=1, has_side_effects=True),
        name="spread",
    )(a, b)


def regroup_kernel(a_ref, b_ref, oa_ref, ob_ref, send_sem, recv_sem, local_sem):
    dp, mp, core, t = place()
    half, base = mp // 2, dp - core
    mine = lax.rem(mp, 2) * 2 + core
    greet_exchange(pltpu.get_barrier_semaphore())
    big = lambda u: oa_ref.at[pl.ds(u * 1024, 1024)]
    small = lambda u: ob_ref.at[pl.ds(u * 512, 512)]
    for g in (0, 1, 2, 3):
        for k, (src, dst) in enumerate(((a_ref.at[g], big(t)), (b_ref.at[g], small(t)))):
            @pl.when((half != core) | (mine != g))
            def _():
                send(src, dst, send_sem.at[g, k], recv_sem.at[t, k], worker(g, core, base))

            @pl.when((half == core) & (mine == g))
            def _():
                pltpu.make_async_copy(src, dst, local_sem.at[k]).start()
    for g in range(4):
        for k, src in enumerate((a_ref.at[g], b_ref.at[g])):
            @pl.when((half != core) | (mine != g))
            def _():
                pltpu.make_async_copy(src, src, send_sem.at[g, k]).wait()
    for u in range(4):
        for k, dst in enumerate((big(u), small(u))):
            @pl.when((half != core) | (t != u))
            def _():
                pltpu.make_async_copy(dst, dst, recv_sem.at[u, k]).wait()

            @pl.when((half == core) & (t == u))
            def _():
                pltpu.make_async_copy(dst, dst, local_sem.at[k]).wait()


def regroup(a, b):
    return pl.pallas_call(
        regroup_kernel,
        out_shape=[jax.ShapeDtypeStruct((4096, C), BF16), jax.ShapeDtypeStruct((2048, C), BF16)],
        in_specs=[ANY, ANY],
        out_specs=[ANY, ANY],
        scratch_shapes=[DMA((4, 2)), DMA((4, 2)), DMA((2,))],
        compiler_params=pltpu.CompilerParams(collective_id=2, has_side_effects=True),
        name="regroup",
    )(a, b)


def settle_kernel(d0_ref, d1_ref, d2_ref, xs_ref, w_ref, extra_ref, mine_ref, out_ref, heads_ref, grads_ref,
                  stage, pair_in, chain_in, gw, gwl, h_in, z_in, z_out,
                  pair_recv, pair_send, chain_recv, chain_send, relay_send,
                  s_recv, s_send, c_recv, c_send, h_recv, h_send, z_recv, z_send, q_recv, q_send):
    dp, mp, core, t = place()
    base, spot = dp - core, lax.rem(dp, 8) // 2
    step = 1 - 2 * core
    partner, lower, upper = at(dp + step, mp), at(dp, mp - step), at(dp, mp + step)
    group = lax.rem(mp, 2) * 2 + core
    gives = core == lax.rem(mp, 2)
    quarter = lambda q: pl.ds(pl.multiple_of(q * QUARTER, QUARTER), QUARTER)
    share = lambda j, parity: grads_ref.at[pl.ds(pl.multiple_of((2 * j + parity) * SHARE, SHARE), SHARE)]

    greet(pltpu.get_barrier_semaphore(), True)

    grads_ref[pl.ds(pl.multiple_of((2 * spot + core) * SHARE, SHARE), SHARE), :] = mine_ref[...]
    for rel in (1, 2, 3):
        send(mine_ref, share(spot, core), s_send.at[rel], s_recv.at[rel], at(mate(dp, rel), mp))

    def weight_gradients():
        gw[...] = jnp.zeros_like(gw)

        def part(i, sums):
            rows = pl.ds(pl.multiple_of(i * SUB, SUB), SUB)
            x = xs_ref[rows, :]
            new = []
            for h, d_ref in enumerate((d0_ref, d1_ref, d2_ref)):
                d = d_ref[rows, :]
                gw[pl.ds(h * 256, 256), :] += dot(d, x, 0, 0)
                new.append(sums[h] + jnp.sum(d.astype(F32), axis=0, keepdims=True))
            return tuple(new)

        sums = lax.fori_loop(0, 4 * ROWS // SUB, part, tuple(jnp.zeros((1, 256), F32) for _ in range(3)))
        gwl[...] = gw[...].astype(BF16)
        for h in range(3):
            line = jnp.concatenate([sums[h], jnp.zeros((1, WIDTH - 256), F32)], axis=1)
            spare = h * 256 + (192 if h == 1 else 128)
            gwl[pl.ds(spare, 16), :] = jnp.concatenate([line, jnp.zeros((15, WIDTH), F32)], axis=0).astype(BF16)
        for rel in (1, 2, 3):
            send(gwl.at[quarter(spot ^ rel)], h_in.at[rel], h_send.at[rel], h_recv.at[rel], at(mate(dp, rel), mp))

    def plane_sum():
        for rel in (1, 2, 3):
            wait(h_in.at[rel], h_recv.at[rel])
        half_sum = gwl[quarter(spot), :].astype(F32)
        for rel in (1, 2, 3):
            half_sum += h_in[rel].astype(F32)
        z_out[...] = half_sum.astype(BF16)

        @pl.when(mp != group)
        def _():
            send(z_out, z_in.at[mp // 2], z_send, z_recv.at[mp // 2], at(dp, group))

    tt = jnp.minimum(t, 3 - t)
    for i in range(3):
        u = lax.rem(3 - i + tt, 4)
        for s in range(SUBS):
            rows = pl.ds(pl.multiple_of(u * ROWS + s * SUB, SUB), SUB)
            value = jnp.zeros((SUB, WIDTH), F32)
            for h, d_ref in enumerate((d0_ref, d1_ref, d2_ref)):
                value += jnp.dot(d_ref[rows, :], w_ref[pl.ds(h * 256, 256), :], preferred_element_type=F32)

            @pl.when(t >= 2)
            def _():
                stage[rows, :] = value.astype(BF16)
                send(stage.at[rows], pair_in.at[rows], pair_send.at[i, s], pair_recv.at[i, s], partner)

            @pl.when(t <= 1)
            def _():
                wait(pair_in.at[rows], pair_recv.at[i, s])
                here = value + pair_in[rows, :].astype(F32)
                if i == 0:
                    stage[rows, :] = here.astype(BF16)
                else:
                    @pl.when(t == 1)
                    def _():
                        wait(chain_in.at[rows], chain_recv.at[u, s])
                        stage[rows, :] = (here + chain_in[rows, :].astype(F32)).astype(BF16)

                    @pl.when(t == 0)
                    def _():
                        stage[rows, :] = here.astype(BF16)

                @pl.when((t == 0) | (i > 0))
                def _():
                    send(stage.at[rows], chain_in.at[rows], chain_send.at[i, s], chain_recv.at[u, s], upper)

                if i == 0:
                    @pl.when(t == 1)
                    def _():
                        send(stage.at[rows], chain_in.at[rows], chain_send.at[i, s], chain_recv.at[u, s], lower)

        if i < 2:
            @pl.when(t == 1)
            def _():
                (weight_gradients, plane_sum)[i]()

    @pl.when(t != 1)
    def _():
        weight_gradients()

    for rel in (1, 2, 3):
        wait(share(spot ^ rel, core), s_recv.at[rel])
    for j in range(4):
        send(share(j, core), share(j, core), c_send.at[j], c_recv.at[j], partner)

    @pl.when(t == 2)
    def _():
        for s in range(SUBS):
            rows = pl.ds(3 * ROWS + s * SUB, SUB)
            wait(chain_in.at[rows], chain_recv.at[3, s])
            send(chain_in.at[rows], chain_in.at[rows], relay_send.at[s], chain_recv.at[3, s], upper)
            if s == 0:
                plane_sum()

    @pl.when((t == 0) | (t == 3))
    def _():
        plane_sum()

    for s in range(SUBS):
        rows = pl.ds(pl.multiple_of(tt * ROWS + s * SUB, SUB), SUB)
        cut = pl.ds(s * SUB, SUB)
        value = jnp.zeros((SUB, WIDTH), F32)
        for h, d_ref in enumerate((d0_ref, d1_ref, d2_ref)):
            value += jnp.dot(d_ref[rows, :], w_ref[pl.ds(h * 256, 256), :], preferred_element_type=F32)

        @pl.when(t >= 2)
        def _():
            stage[rows, :] = value.astype(BF16)
            send(stage.at[rows], pair_in.at[rows], pair_send.at[3, s], pair_recv.at[3, s], partner)

        @pl.when(t <= 1)
        def _():
            stage[rows, :] = value.astype(BF16)

    @pl.when(gives)
    def _():
        both = jnp.zeros((QUARTER, WIDTH), F32)
        for far in (0, 1):
            source = mp // 2 + 2 * far

            @pl.when(source == mp)
            def _():
                z_in[far] = z_out[...]

            @pl.when(source != mp)
            def _():
                wait(z_in.at[far], z_recv.at[far])

            both += z_in[far].astype(F32)
        heads_ref[quarter(spot), :] = both.astype(BF16)
        mine = heads_ref.at[quarter(spot)]
        send(mine, mine, q_send.at[0], q_recv.at[spot], partner)
        for rel in (1, 2, 3):
            send(mine, mine, q_send.at[rel], q_recv.at[spot], at(mate(dp, rel), mp))
            send(mine, mine, q_send.at[rel + 3], q_recv.at[spot], at(mate(dp, rel) + step, mp))

    for s in range(SUBS):
        cut = pl.ds(s * SUB, SUB)
        rows = pl.ds(pl.multiple_of(t * ROWS + s * SUB, SUB), SUB)
        wait(chain_in.at[rows], chain_recv.at[t, s])
        value = extra_ref[cut, :] + chain_in[rows, :].astype(F32)

        @pl.when(t <= 1)
        def _():
            wait(pair_in.at[rows], pair_recv.at[3, s])
            out_ref[cut, :] = (value + stage[rows, :].astype(F32) + pair_in[rows, :].astype(F32)).astype(BF16)

        @pl.when(t >= 2)
        def _():
            out_ref[cut, :] = value.astype(BF16)

    for q in range(4):
        @pl.when(jnp.logical_not(gives) | (spot != q))
        def _():
            wait(heads_ref.at[quarter(q)], q_recv.at[q])
    for j in range(4):
        wait(share(j, 1 - core), c_recv.at[j])

    for s in range(SUBS):
        piece = stage.at[pl.ds(s * SUB, SUB)]

        @pl.when(t >= 2)
        def _():
            for i in range(4):
                wait(piece, pair_send.at[i, s])

        @pl.when(t <= 1)
        def _():
            for i in range(3):
                wait(piece, chain_send.at[i, s])

        @pl.when(t == 2)
        def _():
            wait(piece, relay_send.at[s])
    for rel in (1, 2, 3):
        wait(mine_ref, s_send.at[rel])
        wait(z_out, h_send.at[rel])
    for j in range(4):
        wait(mine_ref, c_send.at[j])

    @pl.when(mp != group)
    def _():
        wait(z_out, z_send)

    @pl.when(gives)
    def _():
        for k in range(7):
            wait(z_out, q_send.at[k])


def settle(d0, d1, d2, xs, w, extra, mine):
    return pl.pallas_call(
        settle_kernel,
        out_shape=[sds((ROWS, WIDTH), BF16), sds((WIDTH, WIDTH), BF16), sds((PACK, WIDTH), BF16)],
        in_specs=[VM] * 7,
        out_specs=[VM] * 3,
        scratch_shapes=[VMEM((4 * ROWS, WIDTH), BF16)] * 3 + [
            VMEM((WIDTH, WIDTH), F32), VMEM((WIDTH, WIDTH), BF16), VMEM((4, QUARTER, WIDTH), BF16), VMEM((2, QUARTER, WIDTH), BF16),
            VMEM((QUARTER, WIDTH), BF16),
            DMA((4, SUBS)), DMA((4, SUBS)), DMA((4, SUBS)), DMA((3, SUBS)), DMA((SUBS,)),
            DMA((4,)), DMA((4,)), DMA((4,)), DMA((4,)), DMA((4,)), DMA((4,)), DMA((2,)), DMA, DMA((4,)), DMA((7,)),
        ],
        compiler_params=pltpu.CompilerParams(collective_id=3, has_side_effects=True, vmem_limit_bytes=60 << 20),
        name="settle",
    )(d0, d1, d2, xs, w, extra, mine)


EPS = 1e-12
CHUNK = 256
FF_MODEL = 768


def gelu_and_slope(v):
    size = jnp.abs(v)
    u = 1.0 / (1.0 + (0.3275911 * 0.7071067811865476) * size)
    bell = jnp.exp(-0.5 * v * v)
    poly = u * (0.127414796 + u * (-0.142248368 + u * (0.7107068705 + u * (-0.7265760135 + u * 0.5307027145))))
    tail = poly * bell
    cdf = jnp.where(v < 0, tail, 1.0 - tail)
    return v * cdf, cdf + v * (bell * 0.3989422804014327)


def row_mean(v):
    return jnp.sum(v, axis=-1, keepdims=True) * (1.0 / FF_MODEL)


def ffn_kernel(c01_ref, c2_ref, tok_ref, cot_ref, vec_ref, *rest):
    pieces, rest = rest[:4], rest[4:]
    (out_ref, res_ref, g01_ref, g2_ref, sum_ref,
     w, wout, ctx, x, x_t, gf, gf_t, act, slope, zhat, acc, rstd, cols, recv,
     w_local, w_send, w_recv, g_send, g_recv, out_sem) = rest
    dp, mp, core, t = place()
    partner = at(dp + 1 - 2 * core, mp)
    spot = lax.rem(dp, 8) // 2
    barrier = pltpu.get_barrier_semaphore()
    pl.semaphore_signal(barrier, inc=1, device_id=partner, device_id_type=MESH)
    pl.semaphore_wait(barrier, 1)

    def rows_of(shard, j, parity):
        return w.at[shard, pl.ds(pl.multiple_of((2 * j + parity) * SHARE, SHARE), SHARE)]

    first, second = jnp.where(core == 0, 1, 2), jnp.where(core == 0, 2, 1)
    for piece, rel in ((3, 3), (2, second), (1, first), (0, 0)):
        for k in range(4):
            src = pieces[piece].at[k]
            shard = lax.rem(mp - k + 4, 4)
            j = spot ^ rel
            pltpu.make_async_copy(src, rows_of(shard, j, core), w_local.at[j, shard]).start()
            send(src, rows_of(shard, j, core), w_send.at[j, shard], w_recv.at[j, shard], partner)

    lane = lax.broadcasted_iota(jnp.int32, (1, C), 1)
    for g in range(4):
        ctx[:, pl.ds(g * C, C)] = c01_ref[g]
    for g in (0, 2):
        a, b = c2_ref[g].astype(F32), c2_ref[g + 1].astype(F32)
        col = pl.ds(4 * C + g * HD, C)
        ctx[pl.ds(0, 512), col] = jnp.where(lane < HD, a, pltpu.roll(b, HD, 1)).astype(BF16)
        ctx[pl.ds(512, 512), col] = jnp.where(lane < HD, pltpu.roll(a, HD, 1), b).astype(BF16)

    def wait_weights(j):
        for shard in range(4):
            ref = w.at[shard, pl.ds(0, SHARE)]
            pltpu.make_async_copy(ref, ref, w_local.at[j, shard]).wait()
            pltpu.make_async_copy(ref, ref, w_recv.at[j, shard]).wait()

    for j in (3, 0, 1, 2):
        wait_weights(j)

    for m in range(4):
        wout[pl.ds(m * C, C), :] = w[m, pl.ds(OUT_ROW, C), :]
        wout[pl.ds(4 * C + m * HD, HD), :] = w[m, pl.ds(OUT_ROW + C, HD), :]

    cols[...] = jnp.zeros_like(cols)
    b_out, gain1, bias1, b_down, gain2, bias2 = (vec_ref[pl.ds(i, 1), :] for i in range(6))

    def forward(r, _):
        rows = pl.ds(pl.multiple_of(r * CHUNK, CHUNK), CHUNK)
        h = jnp.dot(ctx[rows, :], wout[...], preferred_element_type=F32) + tok_ref[rows, :].astype(F32) + b_out
        h = h - row_mean(h)
        scale = lax.rsqrt(row_mean(h * h) + EPS)
        rstd[rows, :] = scale
        h = h * scale
        zhat[rows, :] = h
        first = h * gain1 + bias1
        acc[rows, :] = first + b_down
        x[rows, :] = first.astype(BF16)
        x_t[:, rows] = first.T.astype(BF16)

        def hidden(m, _):
            total = acc[rows, :]
            up_bias = w[m, pl.ds(BIAS_ROW, 16), :].astype(F32)[0:1, :]
            for f in range(3):
                cut = pl.ds(f * 256, 256)
                pre = jnp.dot(x[rows, :], w[m, pl.ds(0, 768), cut], preferred_element_type=F32) + up_bias[:, f * 256 : f * 256 + 256]
                value, grad = gelu_and_slope(pre)
                value = value.astype(BF16)
                act[m, rows, cut] = value
                slope[m, rows, cut] = grad.astype(BF16)
                total += jnp.dot(value, w[m, pl.ds(768 + f * 256, 256), :], preferred_element_type=F32)
            acc[rows, :] = total
            return 0

        lax.fori_loop(0, 4, hidden, 0)

        z = acc[rows, :]
        z = z - row_mean(z)
        scale = lax.rsqrt(row_mean(z * z) + EPS)
        z = z * scale
        out_ref[rows, :] = (z * gain2 + bias2).astype(BF16)
        cot = cot_ref[rows, :].astype(F32)
        dz = cot * gain2
        gs = scale * (dz - row_mean(dz) - z * row_mean(dz * z))
        cols[pl.ds(2, 1), :] += jnp.sum(cot * z, axis=0, keepdims=True)
        cols[pl.ds(3, 1), :] += jnp.sum(cot, axis=0, keepdims=True)
        cols[pl.ds(5, 1), :] += jnp.sum(gs, axis=0, keepdims=True)
        acc[rows, :] = gs
        gf[rows, :] = gs.astype(BF16)
        gf_t[:, rows] = gs.T.astype(BF16)
        return 0

    lax.fori_loop(0, 1024 // CHUNK, forward, 0)

    def give(m, j):
        cut = pl.ds(pl.multiple_of((2 * j + 1 - core) * SHARE, SHARE), SHARE)
        send(w.at[m, cut], recv.at[m, j], g_send.at[m, j], g_recv.at[m, j], partner)

    for j in range(4):
        for shard in range(4):
            ref = w.at[shard, pl.ds(0, SHARE)]
            pltpu.make_async_copy(ref, ref, w_send.at[j, shard]).wait()

    def backward(m, _):
        def rows_back(r, _):
            rows = pl.ds(pl.multiple_of(r * CHUNK, CHUNK), CHUNK)
            total = acc[rows, :]
            for f in range(3):
                cut = pl.ds(f * 256, 256)
                ga = dot(gf[rows, :], w[m, pl.ds(768 + f * 256, 256), :], 1, 1)
                gp = (ga * slope[m, rows, cut].astype(F32)).astype(BF16)
                slope[m, rows, cut] = gp
                total += dot(gp, w[m, pl.ds(0, 768), cut], 1, 1)
            acc[rows, :] = total
            return 0

        lax.fori_loop(0, 1024 // CHUNK, rows_back, 0)
        bias = []
        for f in range(3):
            cut = pl.ds(f * 256, 256)
            gp = slope[m, :, cut]
            w[m, pl.ds(0, 768), cut] = jnp.dot(x_t[...], gp, preferred_element_type=F32).astype(BF16)
            w[m, pl.ds(768, 768), cut] = jnp.dot(gf_t[...], act[m, :, cut], preferred_element_type=F32).astype(BF16)
            bias.append(jnp.sum(gp.astype(F32), axis=0, keepdims=True))
        cols[pl.ds(8 + m, 1), :] = jnp.concatenate(bias, axis=1)
        for j in range(3):
            give(m, j)
        return 0

    lax.fori_loop(0, 4, backward, 0)

    def first_back(r, _):
        rows = pl.ds(pl.multiple_of(r * CHUNK, CHUNK), CHUNK)
        grad = acc[rows, :]
        z = zhat[rows, :]
        dz = grad * gain1
        gr = rstd[rows, :] * (dz - row_mean(dz) - z * row_mean(dz * z))
        cols[pl.ds(0, 1), :] += jnp.sum(grad * z, axis=0, keepdims=True)
        cols[pl.ds(1, 1), :] += jnp.sum(grad, axis=0, keepdims=True)
        cols[pl.ds(4, 1), :] += jnp.sum(gr, axis=0, keepdims=True)
        res_ref[rows, :] = gr
        low = gr.astype(BF16)
        gf[rows, :] = low
        gc = dot(low, wout[...], 1, 1).astype(BF16)
        for g in range(4):
            g01_ref[g, rows, :] = gc[:, g * C : g * C + C]
        ctx_grad[rows, :] = gc[:, 4 * C :]
        return 0

    ctx_grad = x
    ctx_grad = x.at[:, pl.ds(0, 2 * C)]
    lax.fori_loop(0, 1024 // CHUNK, first_back, 0)
    for g in (0, 2):
        top = ctx_grad[pl.ds(0, 512), pl.ds(g * HD, C)].astype(F32)
        low = ctx_grad[pl.ds(512, 512), pl.ds(g * HD, C)].astype(F32)
        g2_ref[g] = jnp.where(lane < HD, top, pltpu.roll(low, HD, 1)).astype(BF16)
        g2_ref[g + 1] = jnp.where(lane < HD, pltpu.roll(top, HD, 1), low).astype(BF16)

    for n in range(3):
        cut = pl.ds(n * 256, 256)
        part = dot(ctx[:, cut], gf[...], 0, 0).astype(BF16)
        if n < 2:
            for i in range(2):
                w[2 * n + i, pl.ds(OUT_ROW, C), :] = part[i * C : i * C + C, :]
        else:
            for i in range(4):
                w[i, pl.ds(OUT_ROW + C, HD), :] = part[i * HD : i * HD + HD, :]
    for m in range(4):
        w[m, pl.ds(BIAS_ROW, 16), :] = jnp.concatenate(
            [cols[pl.ds(8 + m, 1), :], cols[pl.ds(0, 6), :], jnp.zeros((9, FF_MODEL), F32)], axis=0
        ).astype(BF16)
        give(m, 3)

    for rel in (3, 2, 1, 0):
        j = spot ^ rel
        along = jnp.where(core == 0, rel % 2, rel // 2)
        across = jnp.where(core == 0, rel // 2, rel % 2)
        for m in range(4):
            wait(recv.at[m, j], g_recv.at[m, j])
            cut = pl.ds(pl.multiple_of((2 * j + core) * SHARE, SHARE), SHARE)
            recv[m, j] = (recv[m, j].astype(F32) + w[m, cut, :].astype(F32)).astype(BF16)
            pltpu.make_async_copy(recv.at[m, j], sum_ref.at[along, across, m], out_sem.at[m, rel]).start()
    for m in range(4):
        for j in range(4):
            wait(recv.at[m, j], out_sem.at[m, j])
            wait(recv.at[m, j], g_send.at[m, j])


def ffn(c01, c2, tokens, cot, vecs, pieces):
    dma = pltpu.SemaphoreType.DMA
    vm, any_ = pl.BlockSpec(memory_space=pltpu.VMEM), pl.BlockSpec(memory_space=pl.ANY)
    sds = jax.ShapeDtypeStruct
    return pl.pallas_call(
        ffn_kernel,
        out_shape=[sds((1024, 768), BF16), sds((1024, 768), F32), sds((4, 1024, C), BF16), sds((4, 512, C), BF16),
                   sds((2, 2, 4, SHARE, 768), BF16)],
        in_specs=[vm] * 5 + [any_] * 4,
        out_specs=[vm] * 4 + [any_],
        scratch_shapes=[
            VMEM((4, PACK, 768), BF16), VMEM((768, 768), BF16),
            VMEM((1024, 768), BF16), VMEM((1024, 768), BF16), VMEM((768, 1024), BF16), VMEM((1024, 768), BF16), VMEM((768, 1024), BF16),
            VMEM((4, 1024, 768), BF16), VMEM((4, 1024, 768), BF16),
            VMEM((1024, 768), F32), VMEM((1024, 768), F32), VMEM((1024, 1), F32), VMEM((16, 768), F32),
            VMEM((4, 4, SHARE, 768), BF16),
            dma((4, 4)), dma((4, 4)), dma((4, 4)), dma((4, 4)), dma((4, 4)), dma((4, 4)),
        ],
        compiler_params=pltpu.CompilerParams(collective_id=4, has_side_effects=True, vmem_limit_bytes=63 << 20),
        name="ffn",
    )(c01, c2, tokens, cot, vecs, *pieces)


def swap(value, even_bits, odd_bits, n_dp):
    return lax.ppermute(value, "dp", [(d, d ^ (odd_bits if d % 2 else even_bits)) for d in range(n_dp)])


def pick(value, index, axis):
    return lax.dynamic_index_in_dim(value, index, axis, keepdims=False)


def total(a, b):
    return (a.astype(F32) + b.astype(F32)).astype(BF16)


def tie(*values):
    return lax.optimization_barrier(values)


def body(n_dp, tokens, w_query, b_query, w_key, w_value, b_value, w_out, b_out, norm1_gain, norm1_bias, w_up, b_up, w_down,
         b_down, norm2_gain, norm2_bias, key_mask, cluster_order, cotangent):
    dp, mp, core, t = place()
    ring = lambda k: [(z, (z + k) % 4) for z in range(4)]

    live = jnp.sum(key_mask).astype(jnp.int32)
    order = jnp.where(core == 1, cluster_order ^ 3072, cluster_order).reshape(3 * L)
    order = jnp.concatenate([order, jnp.broadcast_to(live, (128,))])
    q, k, v = (w.T.reshape(3, HD, WIDTH) for w in (w_query, w_key, w_value))
    none = jnp.zeros((HD, WIDTH), BF16)
    w_heads = jnp.concatenate([part for h in range(3) for part in ([q[h], v[h], k[h], none] if h == 1 else [v[h], q[h], none, k[h]])])
    bq, bv, bz = b_query.reshape(3, HD), b_value.reshape(3, HD), jnp.zeros((C,), F32)
    b_heads = jnp.stack([jnp.concatenate([bq[h], bv[h], bz] if h == 1 else [bv[h], bq[h], bz]) for h in range(3)])
    b_heads = jnp.concatenate([b_heads, jnp.zeros((5, 256), F32)])
    extra = jnp.concatenate([b_up.reshape(1, WIDTH), jnp.zeros((PACK - BIAS_ROW - 1, WIDTH), BF16)])

    xs, qkv, w_heads, order, share = collect(tokens, w_heads, b_heads, order, w_up, w_down, w_out, extra)
    qkv, share = tie(qkv, share)
    shares = [share] + [lax.ppermute(share, "mp", ring(i)) for i in (1, 2, 3)]
    c01, ts01, probs01 = attend(0, order, qkv)
    c01, *shares = tie(c01, *shares)
    near = jnp.stack(shares)
    next_to = swap(near, 2, 4, n_dp)
    c2, ts2, probs2 = attend(2, order, qkv)
    c2, near, next_to = tie(c2, near, next_to)
    far = swap(jnp.stack([near, next_to]), 4, 2, n_dp)
    c01, c2 = spread(c01, c2)

    vecs = jnp.stack([b_out, norm1_gain, norm1_bias, b_down, norm2_gain, norm2_bias, b_out, b_out])
    layer_out, grad_residual, g01, g2, sums = ffn(c01, c2, tokens, cotangent, vecs, (near, next_to, far[0], far[1]))

    got = swap(sums[1], 2, 4, n_dp)
    g01, g2 = regroup(g01, g2)
    d0 = attend_back(0, order, g01, ts01, probs01)
    d0, sums, got = tie(d0, sums, got)
    sums = total(sums[0], got)
    got = swap(sums[1], 4, 2, n_dp)
    d1 = attend_back(1, order, g01, ts01, probs01)
    d1, sums, got = tie(d1, sums, got)
    sums = total(sums[0], got)
    for bit in range(3, n_dp.bit_length() - 1):
        sums = total(sums, swap(sums, 1 << bit, 1 << bit, n_dp))
    parts = [pick(sums, mp, 0)]
    for i in (1, 2, 3):
        parts.append(lax.ppermute(pick(sums, (mp + i) % 4, 0), "mp", ring(i)))
    d2 = attend_back(2, order, g2, ts2, probs2)
    d2, *parts = tie(d2, *parts)
    mine = sum(p.astype(F32) for p in parts).astype(BF16)
    grad_tokens, heads, grads = settle(d0, d1, d2, xs, w_heads, grad_residual, mine)
    for bit in range(3, n_dp.bit_length() - 1):
        heads = total(heads, swap(heads, 1 << bit, 1 << bit, n_dp))
    grads, heads = grads.astype(F32), heads.astype(F32).reshape(3, 256, WIDTH)
    at_q, at_v, at_k = (HD, 0, HD), (0, HD, 0), (3 * HD, 2 * HD, 3 * HD)
    spare = (2 * HD, 3 * HD, 2 * HD)
    cols = lambda where: jnp.concatenate([heads[h, where[h] : where[h] + HD] for h in range(3)]).T
    sums_of = lambda where: jnp.concatenate([heads[h, spare[h], where[h] : where[h] + HD] for h in range(3)])

    vec = lambda i: grads[1728 + i]
    return (
        layer_out,
        grad_tokens,
        cols(at_q),
        sums_of(at_q),
        cols(at_k),
        cols(at_v),
        sums_of(at_v),
        grads[1536:1728],
        vec(5),
        vec(1),
        vec(2),
        grads[:768],
        vec(0),
        grads[768:1536].T,
        vec(6),
        vec(3),
        vec(4),
    )


def solution(mesh):
    return jax.shard_map(
        functools.partial(body, mesh.shape["dp"]),
        mesh=mesh,
        in_specs=(
            P(("dp", "mp"), None), P(None, "mp"), P("mp"), P(None, "mp"), P(None, "mp"), P("mp"), P("mp", None), P(), P(), P(),
            P(None, "mp"), P("mp"), P("mp", None), P(), P(), P(), P("dp", None), P("dp", "mp", None), P(("dp", "mp"), None),
        ),
        out_specs=(
            P(("dp", "mp"), None), P(("dp", "mp"), None), P(None, "mp"), P("mp"), P(None, "mp"), P(None, "mp"), P("mp"),
            P("mp", None), P(), P(), P(), P(None, "mp"), P("mp"), P("mp", None), P(), P(), P(),
        ),
        check_vma=False,
    )
```

time: 1200 us -> 496 us (0.41)
  waiting for transfers between devices: 531 us -> 5.91 us
  matrix products: 430 us -> 0 us
  Pallas kernels: 0 us -> 409 us
  blocking collectives: 133 us -> 0 us
  other arithmetic: 37.7 us -> 13.4 us
  starting transfers between devices: 0.53 us -> 17.3 us
  between operations: 15.5 us -> 1.37 us
    dot_general x39 -> x0, matrix products: 430 us -> none  [the longest x15 210 us: matmul(): return jnp.dot(left, right, preferred_element_type=jnp.float32)]
    pallas_call x0 -> x10, Pallas kernels: none -> 409 us  [the longest x1 80.6 us: ffn(): pl.pallas_call(ffn_kernel, out_shape=[sds((1024, 768), BF16), sds((1024,...]
    all_gather x4 -> x0, waiting for transfers between devices: 340 us -> none  [the longest x1 113 us: body(): gathered = lax.all_gather(tokens, 'mp', axis=0, tiled=True)]
    reduce_scatter x4 -> x0, waiting for transfers between devices: 189 us -> none  [the longest x1 97.1 us: body(): lax.psum_scatter(matmul(context, w_out).astype(jnp.bfloat16), 'mp', scatt...]
    psum x2 -> x0, blocking collectives: 109 us -> none  [the longest x1 67.3 us: body(): lax.psum((grad_w_query, grad_b_query, grad_w_key, grad_w_value, grad_b_va...]
    ppermute x0 -> x10, starting transfers between devices: none -> 17.3 us  [the longest x3 7.81 us: body(): shares = [share] + [lax.ppermute(share, 'mp', ring(i)) for i in (1, 2, 3)]]
    reduce_sum x10 -> x1, other arithmetic: 17.3 us -> 1.53 us  [body(): live = jnp.sum(key_mask).astype(jnp.int32)]
    reshape x7 -> x1, local copies, waits for them, and re-layouts: 15.1 us -> 0.68 us  [body(): b_up.reshape(1, WIDTH)]
  transfers between devices with their start and end apart: 9 -> 10, of which waited for: 7 -> 1; matrix products, arithmetic and copies ran while one was open for 21% -> 0% of each run, Pallas kernels for 0% -> 40%
where the time goes in v1:
time: 496 us; the launch traced here: 489 us
  Pallas kernels  409 us (82%)
  local copies, waits for them, and re-layouts  42.1 us (8%)
  starting transfers between devices  17.3 us (3%)
  other arithmetic  13.4 us (3%)
  waiting for transfers between devices  5.91 us (1%)
    pallas_call x1, Pallas kernels, ffn(): pl.pallas_call(ffn_kernel, out_shape=[sds((1024, 768), BF16), sds((1024,...  80.6 us
    pallas_call x1, Pallas kernels, settle(): pl.pallas_call(settle_kernel, out_shape=[sds((ROWS, WIDTH), BF16), sds((W...  72.2 us
    pallas_call x3, Pallas kernels, attend_back(): pl.pallas_call(functools.partial(attend_back_kernel, head), grid=(1,), in...  62.4 us
    pallas_call x2, Pallas kernels, attend(): pl.pallas_call(functools.partial(attend_kernel, first), grid=(heads,), in...  62.2 us
    pallas_call x1, Pallas kernels, collect(): pl.pallas_call(collect_kernel, out_shape=[sds((4 * ROWS, WIDTH), BF16), s...  61.3 us
    pallas_call x1, Pallas kernels, spread(): pl.pallas_call(spread_kernel, out_shape=[jax.ShapeDtypeStruct((4, 1024, C...  36.3 us
    pallas_call x1, Pallas kernels, regroup(): pl.pallas_call(regroup_kernel, out_shape=[jax.ShapeDtypeStruct((4096, C),...  34 us
    unnamed x78, local copies, waits for them, and re-layouts  28.8 us
  transfers between devices with their start and end apart: 10, of which 1 were waited for; matrix products, arithmetic and copies ran while one was open for 0% of the time, Pallas kernels for 40%

profile of v1, /device:TPU:10, one launch (start us, length us, event | category | flops | bytes accessed | tf_op | source)
XLA Modules:
  0.0 489.0 jit_solution(1601031214693260890)
XLA Ops:
  0.7 1.5 reduce_sum.9
  12.1 1.3 copy-done.6
  13.4 1.3 copy-done.7
  14.7 61.3 %collect.1 = (bf16[4096,768]{1,0:T(8,128)(2,1)S(1)}, bf16[3,4096,256]{2,1,0:T(8,128)(2,1)}, bf16[768,768]{1,0:T(8,128)(2,1)S(1)}, s32[12416]{0:T(1024)S(1)}, bf16[224,768]{1,0:T(8,128)(2,1)S(1)}) custom-call(bf16[1024,768]{1,0:T(8,128)(2,1)S(1)} %copy-done.1, bf16[768,768]{1,0:T(8,128)(2,1)S(1)} %slice_dynamic-update-slice_fusion.wsrc_ref, ...), custom_call_target="tpu_custom_call" | custom-call | tf_op jit(solution)/shard_map/collect/pallas_call | solution.py:426
  76.0 2.6 copy-done
  80.2 4.9 collective-permute-start.2
  85.1 2.9 collective-permute-start
  88.0 40.4 %attend.2 = (bf16[4096,128]{1,0:T(8,128)(2,1)}, bf16[2,4096,256]{2,1,0:T(8,128)(2,1)}, f32[2,4096,128]{2,1,0:T(8,128)}) custom-call(s32[12416]{0:T(1024)} %copy-done.11, bf16[3,4096,256]{2,1,0:T(8,128)(2,1)} %get-tuple-element.64.qkv_ref), custom_call_target="tpu_custom_call" | custom-call | flops 35999997952 | bytes 10485760 | tf_op jit(solution)/shard_map/attend/pallas_call | solution.py:92
  129.3 21.8 %attend.3 = (bf16[2048,128]{1,0:T(8,128)(2,1)}, bf16[1,4096,256]{2,1,0:T(8,128)(2,1)}, f32[1,4096,128]{2,1,0:T(8,128)}) custom-call(s32[12416]{0:T(1024)} %copy-done.11, bf16[3,4096,256]{2,1,0:T(8,128)(2,1)} %get-tuple-element.64.qkv_ref), custom_call_target="tpu_custom_call" | custom-call | flops 17999998976 | bytes 10485760 | tf_op jit(solution)/shard_map/attend/pallas_call | solution.py:92
  151.2 1.9 pad_maximum_fusion
  153.0 1.5 collective-permute-start.4
  155.3 36.3 %spread.1 = (bf16[4,1024,128]{2,1,0:T(8,128)(2,1)}, bf16[4,512,128]{2,1,0:T(8,128)(2,1)}) custom-call(bf16[4096,128]{1,0:T(8,128)(2,1)} %get-tuple-element.67.a_ref, bf16[2048,128]{1,0:T(8,128)(2,1)} %get-tuple-element.73.b_ref), custom_call_target="tpu_custom_call" | custom-call | tf_op jit(solution)/shard_map/spread/pallas_call | solution.py:496
  191.6 1.7 slice_bitcast_fusion.3
  193.3 80.6 %ffn.1 = (bf16[1024,768]{1,0:T(8,128)(2,1)}, f32[1024,768]{1,0:T(8,128)}, bf16[4,1024,128]{2,1,0:T(8,128)(2,1)}, bf16[4,512,128]{2,1,0:T(8,128)(2,1)}, bf16[2,2,4,224,768]{4,3,2,1,0:T(8,128)(2,1)}) custom-call(bf16[4,1024,128]{2,1,0:T(8,128)(2,1)} %get-tuple-element.74.c01_ref, bf16[4,512,128]{2,1,0:T(8,128)(2,1)} %get-tuple-element.75.c2_ref, ...), custom_call_target="tpu_custom_call" | custom-call | tf_op jit(solution)/shard_map/ffn/pallas_call | solution.py:992
  274.0 3.6 slice_bitcast_fusion
  277.5 1.7 collective-permute-start.5
  279.2 34.0 %regroup.1 = (bf16[4096,128]{1,0:T(8,128)(2,1)}, bf16[2048,128]{1,0:T(8,128)(2,1)}) custom-call(bf16[4,1024,128]{2,1,0:T(8,128)(2,1)} %get-tuple-element.79.a_ref, bf16[4,512,128]{2,1,0:T(8,128)(2,1)} %get-tuple-element.80.b_ref), custom_call_target="tpu_custom_call" | custom-call | tf_op jit(solution)/shard_map/regroup/pallas_call | solution.py:540
  313.3 1.2 copy-done.9
  314.5 2.2 copy-done.13
  316.7 2.2 copy-done.14
  318.9 20.7 %attend_back.3.d0_ref = bf16[4096,256]{1,0:T(8,128)(2,1)S(1)} custom-call(s32[12416]{0:T(1024)S(1)} %copy-done.12, bf16[4096,128]{1,0:T(8,128)(2,1)S(1)} %copy-done.9, bf16[2,4096,256]{2,1,0:T(8,128)(2,1)S(1)} %copy-done.13, f32[2,4096,128]{2,1,0:T(8,128)S(1)} %copy-done.14), custom_call_target="tpu_custom_call" | custom-call | flops 24000000000 | bytes 10485760 | tf_op jit(solution)/shard_map/attend_back/pallas_call | solution.py:170
  341.4 20.7 %attend_back.4.d1_ref = bf16[4096,256]{1,0:T(8,128)(2,1)S(1)} custom-call(s32[12416]{0:T(1024)S(1)} %copy-done.12, bf16[4096,128]{1,0:T(8,128)(2,1)S(1)} %copy-done.9, bf16[2,4096,256]{2,1,0:T(8,128)(2,1)S(1)} %copy-done.13, f32[2,4096,128]{2,1,0:T(8,128)S(1)} %copy-done.14), custom_call_target="tpu_custom_call" | custom-call | flops 24000000000 | bytes 10485760 | tf_op jit(solution)/shard_map/attend_back/pallas_call | solution.py:170
  363.7 5.2 %collective-permute-start.8 = (bf16[224,768]{1,0:T(8,128)(2,1)S(1)}, bf16[224,768]{1,0:T(8,128)(2,1)S(1)}, u32[]{:S(2)}, u32[]{:S(2)}) collective-permute-start(bf16[224,768]{1,0:T(8,128)(2,1)S(1)} %get-tuple-element.147), channel_id=1, source_target_pairs={{0,2},{1,3},{2,0},{3,1},{4,6},{5,7},{6,4},{7,5},{8,10},{9,11},{10,... | collective-permute-start | bytes 1032200 | tf_op jit(solution)/shard_map/ppermute | solution.py:1071
  369.0 21.0 %attend_back.5.d2_ref = bf16[4096,256]{1,0:T(8,128)(2,1)S(1)} custom-call(s32[12416]{0:T(1024)S(1)} %copy-done.12, bf16[2048,128]{1,0:T(8,128)(2,1)S(1)} %copy-done.10, bf16[1,4096,256]{2,1,0:T(8,128)(2,1)S(1)} %copy-done.15, f32[1,4096,128]{2,1,0:T(8,128)S(1)} %copy-done.16), custom_call_target="tpu_custom_call" | custom-call | flops 24000000000 | bytes 10485760 | tf_op jit(solution)/shard_map/attend_back/pallas_call | solution.py:170
  389.9 1.3 copy-done.4
  391.2 5.9 %collective-permute-done.7 = bf16[224,768]{1,0:T(8,128)(2,1)S(1)} collective-permute-done((bf16[224,768]{1,0:T(8,128)(2,1)S(1)}, bf16[224,768]{1,0:T(8,128)(2,1)S(1)}, u32[]{:S(2)}, u32[]{:S(2)}) %collective-permute-start.7) | collective-permute-done | bytes 344096 | tf_op jit(solution)/shard_map/ppermute | solution.py:1071
  398.0 72.2 %settle.1 = (bf16[1024,768]{1,0:T(8,128)(2,1)}, bf16[768,768]{1,0:T(8,128)(2,1)}, bf16[1792,768]{1,0:T(8,128)(2,1)}) custom-call(bf16[4096,256]{1,0:T(8,128)(2,1)} %copy-done.2, bf16[4096,256]{1,0:T(8,128)(2,1)} %copy-done.3, bf16[4096,256]{1,0:T(8,128)(2,1)} %copy-done.4, bf16[4096,768]{1,0:T(8,128)(2,1)} %copy-done, bf16[768,768]{1,0:T(8,128)(2,1)} %copy-done.5, ...), custom_call_target="tpu_custom_call" | custom-call | tf_op jit(solution)/shard_map/settle/pallas_call | solution.py:763
  470.2 1.5 convert.3
  475.1 1.6 slice.230
  478.0 2.0 copy.36
  479.9 2.0 maximum_bitcast_fusion.2
  481.9 1.4 pad_maximum_fusion.6
  (117 shorter events, 27.3 us)
Async XLA Ops:
  0.7 10.5 %copy-start.30 = (f32[192]{0:T(256)S(1)}, f32[192]{0:T(256)}, u32[]{:S(2)}) copy-start(f32[192]{0:T(256)} %param.24) | copy-start | bytes 2308
  0.7 10.5 %copy-start.31 = (f32[192]{0:T(256)S(1)}, f32[192]{0:T(256)}, u32[]{:S(2)}) copy-start(f32[192]{0:T(256)} %param.21) | copy-start | bytes 2308
  0.7 10.5 %copy-start.23 = (s32[1,3,4096]{2,0,1:T(1,128)S(1)}, s32[1,3,4096]{2,0,1:T(1,128)}, u32[]{:S(2)}) copy-start(s32[1,3,4096]{2,0,1:T(1,128)} %param.36) | copy-start | bytes 147460
  0.7 11.4 %copy-start.1 = (bf16[1024,768]{1,0:T(8,128)(2,1)S(1)}, bf16[1024,768]{1,0:T(8,128)(2,1)}, u32[]{:S(2)}) copy-start(bf16[1024,768]{1,0:T(8,128)(2,1)} %tok_ref.1) | copy-start | bytes 4718596
  0.7 11.4 %copy-start.8 = (bf16[192,768]{1,0:T(8,128)(2,1)S(1)}, bf16[192,768]{1,0:T(8,128)(2,1)}, u32[]{:S(2)}) copy-start(bf16[192,768]{1,0:T(8,128)(2,1)} %wout_ref.1) | copy-start | bytes 884740
  75.9 2.6 copy-start
  80.2 48.3 %collective-permute-start.2 = (bf16[224,768]{1,0:T(8,128)(2,1)S(1)}, bf16[224,768]{1,0:T(8,128)(2,1)S(1)}, u32[]{:S(2)}, u32[]{:S(2)}) collective-permute-start(bf16[224,768]{1,0:T(8,128)(2,1)S(1)} %get-tuple-element.69), channel_id=1, source_target_pairs={{0,3},{1,0},{2,1},{3,2},{4,7},{5,4},{6,5},{7,6},{8,11},{9,8},{10,9... | collective-permute-start | bytes 1032200 | tf_op jit(solution)/shard_map/ppermute | solution.py:1045
  85.1 43.4 %collective-permute-start.1 = (bf16[224,768]{1,0:T(8,128)(2,1)S(1)}, bf16[224,768]{1,0:T(8,128)(2,1)S(1)}, u32[]{:S(2)}, u32[]{:S(2)}) collective-permute-start(bf16[224,768]{1,0:T(8,128)(2,1)S(1)} %get-tuple-element.69), channel_id=1, source_target_pairs={{0,2},{1,3},{2,0},{3,1},{4,6},{5,7},{6,4},{7,5},{8,10},{9,11},{10,... | collective-permute-start | bytes 1032200 | tf_op jit(solution)/shard_map/ppermute | solution.py:1045
  85.1 43.4 %collective-permute-start = (bf16[224,768]{1,0:T(8,128)(2,1)S(1)}, bf16[224,768]{1,0:T(8,128)(2,1)S(1)}, u32[]{:S(2)}, u32[]{:S(2)}) collective-permute-start(bf16[224,768]{1,0:T(8,128)(2,1)S(1)} %get-tuple-element.69), channel_id=1, source_target_pairs={{0,1},{1,2},{2,3},{3,0},{4,5},{5,6},{6,7},{7,4},{8,9},{9,10},{10,1... | collective-permute-start | bytes 1032200 | tf_op jit(solution)/shard_map/ppermute | solution.py:1045
  128.7 22.4 %copy-start.17 = (bf16[4,224,768]{2,1,0:T(8,128)(2,1)}, bf16[4,224,768]{2,1,0:T(8,128)(2,1)S(1)}, u32[]{:S(2)}) copy-start(bf16[4,224,768]{2,1,0:T(8,128)(2,1)S(1)} %pad_maximum_fusion.1.rest_0_) | copy-start | bytes 4128772
  128.7 22.4 %collective-permute-start.3 = (bf16[4,224,768]{2,1,0:T(8,128)(2,1)S(1)}, bf16[4,224,768]{2,1,0:T(8,128)(2,1)S(1)}, u32[]{:S(2)}, u32[]{:S(2)}) collective-permute-start(bf16[4,224,768]{2,1,0:T(8,128)(2,1)S(1)} %pad_maximum_fusion.1.rest_0_), channel_id=1, source_target_pairs={{0,8},{4,20},{8,0},{12,28},{16,24},{20,4},{24,16},{28,12},{1,9},{5... | collective-permute-start | bytes 4128776 | tf_op jit(solution)/shard_map/ppermute | solution.py:1012
  151.1 3.5 copy-start.24
  151.1 3.5 copy-start.25
  151.1 3.5 copy-start.26
  151.1 3.5 copy-start.27
  151.1 3.5 copy-start.28
  151.1 3.5 copy-start.29
  153.0 38.5 %collective-permute-start.4 = (bf16[2,4,224,768]{3,2,1,0:T(8,128)(2,1)}, bf16[2,4,224,768]{3,2,1,0:T(8,128)(2,1)S(1)}, u32[]{:S(2)}, u32[]{:S(2)}) collective-permute-start(bf16[2,4,224,768]{3,2,1,0:T(8,128)(2,1)} %pad_maximum_fusion), channel_id=1, source_target_pairs={{0,16},{4,12},{8,24},{12,4},{16,0},{20,28},{24,8},{28,20},{1,17},{... | collective-permute-start | bytes 8257544 | tf_op jit(solution)/shard_map/ppermute | solution.py:1012
  277.5 35.7 %copy-start.12 = (s32[12416]{0:T(1024)S(1)}, s32[12416]{0:T(1024)}, u32[]{:S(2)}) copy-start(s32[12416]{0:T(1024)} %copy-done.11) | copy-start | bytes 148996
  277.5 62.1 %collective-permute-start.5 = (bf16[2,4,224,768]{3,2,1,0:T(8,128)(2,1)}, bf16[2,4,224,768]{3,2,1,0:T(8,128)(2,1)S(1)}, u32[]{:S(2)}, u32[]{:S(2)}) collective-permute-start(bf16[2,4,224,768]{3,2,1,0:T(8,128)(2,1)} %slice_bitcast_fusion), channel_id=1, source_target_pairs={{0,8},{4,20},{8,0},{12,28},{16,24},{20,4},{24,16},{28,12},{1,9},{5... | collective-permute-start | bytes 8257544 | tf_op jit(solution)/shard_map/ppermute | solution.py:1012
  314.5 2.2 copy-start.13
  316.7 2.2 copy-start.14
  318.9 20.8 %copy-start.19 = (bf16[2,2,4,224,768]{4,3,2,1,0:T(8,128)(2,1)S(1)}, bf16[2,2,4,224,768]{4,3,2,1,0:T(8,128)(2,1)}, u32[]{:S(2)}) copy-start(bf16[2,2,4,224,768]{4,3,2,1,0:T(8,128)(2,1)} %get-tuple-element.86) | copy-start | bytes 16515076
  341.0 21.1 %collective-permute-start.6 = (bf16[4,224,768]{2,1,0:T(8,128)(2,1)S(1)}, bf16[4,224,768]{2,1,0:T(8,128)(2,1)S(1)}, u32[]{:S(2)}, u32[]{:S(2)}) collective-permute-start(bf16[4,224,768]{2,1,0:T(8,128)(2,1)S(1)} %slice_bitcast_fusion.2), channel_id=1, source_target_pairs={{0,16},{4,12},{8,24},{12,4},{16,0},{20,28},{24,8},{28,20},{1,17},{... | collective-permute-start | bytes 4128776 | tf_op jit(solution)/shard_map/ppermute | solution.py:1012
  362.1 6.8 %copy-start.16 = (f32[1,4096,128]{2,1,0:T(8,128)S(1)}, f32[1,4096,128]{2,1,0:T(8,128)}, u32[]{:S(2)}) copy-start(f32[1,4096,128]{2,1,0:T(8,128)} %get-tuple-element.91.pr_ref) | copy-start | bytes 6291460
  363.6 5.4 %copy-start.10 = (bf16[2048,128]{1,0:T(8,128)(2,1)S(1)}, bf16[2048,128]{1,0:T(8,128)(2,1)}, u32[]{:S(2)}) copy-start(bf16[2048,128]{1,0:T(8,128)(2,1)} %get-tuple-element.89.g_ref) | copy-start | bytes 1572868
  363.6 5.4 %copy-start.15 = (bf16[1,4096,256]{2,1,0:T(8,128)(2,1)S(1)}, bf16[1,4096,256]{2,1,0:T(8,128)(2,1)}, u32[]{:S(2)}) copy-start(bf16[1,4096,256]{2,1,0:T(8,128)(2,1)} %get-tuple-element.90.ts_ref) | copy-start | bytes 6291460
  363.6 27.6 %collective-permute-start.9 = (bf16[224,768]{1,0:T(8,128)(2,1)S(1)}, bf16[224,768]{1,0:T(8,128)(2,1)S(1)}, u32[]{:S(2)}, u32[]{:S(2)}) collective-permute-start(bf16[224,768]{1,0:T(8,128)(2,1)S(1)} %get-tuple-element.146), channel_id=1, source_target_pairs={{0,3},{1,0},{2,1},{3,2},{4,7},{5,4},{6,5},{7,6},{8,11},{9,8},{10,9... | collective-permute-start | bytes 1032200 | tf_op jit(solution)/shard_map/ppermute | solution.py:1071
  363.7 27.5 %collective-permute-start.8 = (bf16[224,768]{1,0:T(8,128)(2,1)S(1)}, bf16[224,768]{1,0:T(8,128)(2,1)S(1)}, u32[]{:S(2)}, u32[]{:S(2)}) collective-permute-start(bf16[224,768]{1,0:T(8,128)(2,1)S(1)} %get-tuple-element.147), channel_id=1, source_target_pairs={{0,2},{1,3},{2,0},{3,1},{4,6},{5,7},{6,4},{7,5},{8,10},{9,11},{10,... | collective-permute-start | bytes 1032200 | tf_op jit(solution)/shard_map/ppermute | solution.py:1071
  368.9 28.2 %collective-permute-start.7 = (bf16[224,768]{1,0:T(8,128)(2,1)S(1)}, bf16[224,768]{1,0:T(8,128)(2,1)S(1)}, u32[]{:S(2)}, u32[]{:S(2)}) collective-permute-start(bf16[224,768]{1,0:T(8,128)(2,1)S(1)} %get-tuple-element.148), channel_id=1, source_target_pairs={{0,1},{1,2},{2,3},{3,0},{4,5},{5,6},{6,7},{7,4},{8,9},{9,10},{10,1... | collective-permute-start | bytes 1032200 | tf_op jit(solution)/shard_map/ppermute | solution.py:1071
  472.3 2.0 copy-start.18
  481.9 3.8 copy-start.21
  (10 other events, 13.4 us)

commit v2 on v1

--- a/solution.py
+++ b/solution.py
@@ -9,6 +9,9 @@
 L = 4096
 C = 128
 HD = 64
+GROUP = 2
+STEP = 1024
+GROUPS = STEP // (GROUP * C)
 F32 = jnp.float32
 BF16 = jnp.bfloat16
 VMEM = pltpu.VMEM
@@ -18,167 +21,165 @@
     return lax.dot_general(a, b, (((da,), (db,)), ((), ())), preferred_element_type=F32)
 
 
-def attend_kernel(first, ord_ref, qkv_ref, c_ref, ts_ref, pr_ref, src, ctx, buf_a, buf_b, out_a, out_b):
-    head = pl.program_id(0) + first
-    live = ord_ref[3 * L]
-    base = head * L
-
-    src[:, 0, :] = qkv_ref[0, :, :C].astype(F32)
-    src[:, 1, :] = qkv_ref[0, :, C:].astype(F32)
-
-    def gather(cluster, buf):
-        start = base + cluster * C
-        for u in range(C):
-            buf[u] = src[ord_ref[start + u]]
-
-    def compute(cluster, buf, out):
-        rows = pl.ds(pl.multiple_of(cluster * C, C), C)
-        t0 = buf[:, 0, :].astype(BF16)
-        t1 = buf[:, 1, :].astype(BF16)
-        ts_ref[0, rows, :C] = t0
-        ts_ref[0, rows, C:] = t1
-        slot = cluster * C + lax.broadcasted_iota(jnp.int32, (1, C), 1)
-        penalty = jnp.where(slot < live, 0.0, -10000.0)
-        scores = dot(t0, t1, 1, 1) * 0.125 + penalty
-        peak = jnp.max(scores, axis=-1, keepdims=True)
-        e = jnp.exp(scores - peak)
-        probs = e * (1.0 / jnp.sum(e, axis=-1, keepdims=True))
-        pr_ref[0, rows, :] = probs
-        out[...] = jnp.dot(probs.astype(BF16), t0, preferred_element_type=F32)
-
-    def scatter(cluster, out):
-        start = base + cluster * C
-        for u in range(C):
-            ctx[pl.ds(ord_ref[start + u], 1), :] = out[pl.ds(u, 1), :]
-
-    last = L // C - 1
-    gather(0, buf_a)
-
-    def pair(i, _):
-        gather(2 * i + 1, buf_b)
-        compute(2 * i, buf_a, out_a)
-        scatter(jnp.maximum(2 * i - 1, 0), out_b)
-        gather(jnp.minimum(2 * i + 2, last), buf_a)
-        compute(2 * i + 1, buf_b, out_b)
-        scatter(2 * i, out_a)
-        return 0
-
-    lax.fori_loop(0, L // C // 2, pair, 0)
-    scatter(last, out_b)
-
-    lane = lax.broadcasted_iota(jnp.int32, (1, C), 1)
-    if first == 2:
-        for k in range(4):
-            low = ctx[pl.ds(k * 1024, 512), :]
-            high = pltpu.roll(ctx[pl.ds(k * 1024 + 512, 512), :], HD, 1)
-            c_ref[pl.ds(k * 512, 512), :] = jnp.where(lane < HD, low, high).astype(BF16)
-    else:
-
-        @pl.when(head == 0)
-        def _():
-            c_ref[...] = ctx[...].astype(BF16)
-
-        @pl.when(head == 1)
-        def _():
-            c_ref[...] = jnp.where(lane < HD, c_ref[...], ctx[...].astype(BF16))
-
-
-def attend(first, order, qkv):
+def in_turn(gather, compute, scatter, bufs, outs):
+    gather(0, bufs[0])
+    for group in range(GROUPS):
+        if group + 1 < GROUPS:
+            gather(group + 1, bufs[(group + 1) % 2])
+        compute(group, bufs[group % 2], outs[group % 2])
+        if group:
+            scatter(group - 1, outs[(group - 1) % 2])
+    scatter(GROUPS - 1, outs[(GROUPS - 1) % 2])
+
+
+def attend_kernel(first, ord_ref, mask_ref, qkv_ref, c_ref, ts_ref, pr_ref, src, ctx, *slots):
+    head, step = pl.program_id(0) + first, pl.program_id(1)
+    live = jnp.sum(mask_ref[...].astype(F32), axis=1, keepdims=True).astype(jnp.int32)
+
+    @pl.when(step == 0)
+    def _():
+        src[pl.ds(0, L, stride=2), :] = qkv_ref[0, :, :C].astype(F32)
+        src[pl.ds(1, L, stride=2), :] = qkv_ref[0, :, C:].astype(F32)
+
+    def gather(group, buf):
+        for u in range(GROUP * C):
+            buf[pl.ds(2 * u, 2), :] = src[pl.ds(pl.multiple_of(ord_ref[group * GROUP * C + u], 2), 2), :]
+
+    def compute(group, buf, out):
+        each = range(GROUP)
+        rows = [pl.ds((group * GROUP + i) * C, C) for i in each]
+        t0 = [buf[pl.ds(2 * i * C, C, stride=2), :].astype(BF16) for i in each]
+        t1 = [buf[pl.ds(2 * i * C + 1, C, stride=2), :].astype(BF16) for i in each]
+        for i in each:
+            ts_ref[0, rows[i], :C] = t0[i]
+            ts_ref[0, rows[i], C:] = t1[i]
+        slot = [step * STEP + (group * GROUP + i) * C + lax.broadcasted_iota(jnp.int32, (C, C), 0) for i in each]
+        scores = [dot(t1[i], t0[i], 1, 1) * 0.125 + jnp.where(slot[i] < live, 0.0, -10000.0) for i in each]
+        e = [jnp.exp(scores[i] - jnp.max(scores[i], axis=0, keepdims=True)) for i in each]
+        probs = [e[i] * (1.0 / jnp.sum(e[i], axis=0, keepdims=True)) for i in each]
+        for i in each:
+            pr_ref[0, rows[i], :] = probs[i]
+        for i in each:
+            out[pl.ds(i * C, C), :] = dot(probs[i].astype(BF16), t0[i], 0, 0)
+
+    def scatter(group, out):
+        for u in range(GROUP * C):
+            ctx[pl.ds(ord_ref[group * GROUP * C + u], 1), :] = out[pl.ds(u, 1), :]
+
+    in_turn(gather, compute, scatter, slots[:2], slots[2:])
+
+    @pl.when(step == L // STEP - 1)
+    def _():
+        lane = lax.broadcasted_iota(jnp.int32, (1, C), 1)
+        if first == 2:
+            for k in range(4):
+                low = ctx[pl.ds(k * 2048, 512, stride=2), :]
+                high = pltpu.roll(ctx[pl.ds(k * 2048 + 1024, 512, stride=2), :], HD, 1)
+                c_ref[pl.ds(k * 512, 512), :] = jnp.where(lane < HD, low, high).astype(BF16)
+        else:
+            rows = ctx[pl.ds(0, L, stride=2), :].astype(BF16)
+
+            @pl.when(head == 0)
+            def _():
+                c_ref[...] = rows
+
+            @pl.when(head == 1)
+            def _():
+                c_ref[...] = jnp.where(lane < HD, c_ref[...], rows)
+
+
+def attend(first, order, mask, qkv):
     heads = 2 if first == 0 else 1
-    whole = lambda shape: pl.BlockSpec(shape, lambda h: (0,) * len(shape), pipeline_mode=pl.Buffered(1))
-    in_head = lambda shape: pl.BlockSpec((1,) + shape, lambda h: (h + first, 0, 0))
-    per_head = lambda shape: pl.BlockSpec((1,) + shape, lambda h: (h, 0, 0))
+    whole = lambda shape: pl.BlockSpec(shape, lambda h, i: (0,) * len(shape), pipeline_mode=pl.Buffered(1))
+    per_step = lambda width: pl.BlockSpec((1, STEP, width), lambda h, i: (h, i, 0))
+    steps = L // STEP
     out_rows = L if first == 0 else L // 2
     return pl.pallas_call(
         functools.partial(attend_kernel, first),
-        grid=(heads,),
-        in_specs=[pl.BlockSpec(memory_space=pltpu.SMEM), in_head((L, 2 * C))],
-        out_specs=[whole((out_rows, C)), per_head((L, 2 * C)), per_head((L, C))],
+        grid=(heads, steps),
+        in_specs=[
+            pl.BlockSpec((STEP,), lambda h, i: ((h + first) * steps + i,), memory_space=pltpu.SMEM),
+            whole((1, L)),
+            pl.BlockSpec((1, L, 2 * C), lambda h, i: (h + first, 0, 0)),
+        ],
+        out_specs=[whole((out_rows, C)), per_step(2 * C), per_step(C)],
         out_shape=[
             jax.ShapeDtypeStruct((out_rows, C), BF16),
             jax.ShapeDtypeStruct((heads, L, 2 * C), BF16),
             jax.ShapeDtypeStruct((heads, L, C), F32),
         ],
-        scratch_shapes=[
-            VMEM((L, 2, C), F32), VMEM((L, C), F32),
-            VMEM((C, 2, C), F32), VMEM((C, 2, C), F32), VMEM((C, C), F32), VMEM((C, C), F32),
-        ],
-        compiler_params=pltpu.CompilerParams(vmem_limit_bytes=56 << 20),
-        cost_estimate=pl.CostEstimate(flops=heads * 18 * 10**9, bytes_accessed=10 << 20, transcendentals=0),
+        scratch_shapes=[VMEM((2 * L, C), F32), VMEM((2 * L, C), F32)]
+        + [VMEM((2 * GROUP * C, C), F32)] * 2 + [VMEM((GROUP * C, C), F32)] * 2,
+        compiler_params=pltpu.CompilerParams(vmem_limit_bytes=60 << 20),
+        cost_estimate=pl.CostEstimate(flops=heads * 9 * 10**9, bytes_accessed=10 << 20, transcendentals=0),
         name="attend",
-    )(order, qkv)
-
-
-def attend_back_kernel(head, ord_ref, g_ref, ts_ref, pr_ref, d_ref, gsrc, dst, buf_a, buf_b, out_a, out_b):
-    base = head * L
+    )(order, mask, qkv)
+
+
+def attend_back_kernel(head, ord_ref, g_ref, ts_ref, pr_ref, d_ref, gsrc, dst, *slots):
+    step = pl.program_id(0)
     lane = lax.broadcasted_iota(jnp.int32, (1, C), 1)
-    if head == 2:
-        for k in range(4):
-            both = g_ref[pl.ds(k * 512, 512), :].astype(F32)
-            gsrc[pl.ds(k * 1024, 512), :] = both
-            gsrc[pl.ds(k * 1024 + 512, 512), :] = pltpu.roll(both, HD, 1)
-    else:
-        gsrc[...] = g_ref[...].astype(F32)
+
+    @pl.when(step == 0)
+    def _():
+        if head == 2:
+            for k in range(4):
+                both = g_ref[pl.ds(k * 512, 512), :].astype(F32)
+                gsrc[pl.ds(k * 2048, 512, stride=2), :] = both
+                gsrc[pl.ds(k * 2048 + 1024, 512, stride=2), :] = pltpu.roll(both, HD, 1)
+        else:
+            gsrc[pl.ds(0, L, stride=2), :] = g_ref[...].astype(F32)
 
     keep = (lane >= HD) if head == 1 else (lane < HD)
 
-    def gather(cluster, buf):
-        start = base + cluster * C
-        for u in range(C):
-            buf[pl.ds(u, 1), :] = gsrc[pl.ds(ord_ref[start + u], 1), :]
-
-    def compute(cluster, buf, out):
-        rows = pl.ds(pl.multiple_of(cluster * C, C), C)
-        t0 = ts_ref[0, rows, :C]
-        t1 = ts_ref[0, rows, C:]
-        probs = pr_ref[0, rows, :]
-        g = jnp.where(keep, buf[...], 0.0).astype(BF16)
-        dp = dot(g, t0, 1, 1)
-        row = jnp.sum(probs * dp, axis=-1, keepdims=True)
-        ds = (probs * (dp - row)).astype(BF16)
-        out[:, 0, :] = jnp.dot(ds, t1, preferred_element_type=F32) * 0.125 + dot(probs.astype(BF16), g, 0, 0)
-        out[:, 1, :] = dot(ds, t0, 0, 0) * 0.125
-
-    def scatter(cluster, out):
-        start = base + cluster * C
-        for u in range(C):
-            dst[ord_ref[start + u]] = out[u]
-
-    last = L // C - 1
-    gather(0, buf_a)
-
-    def pair(i, _):
-        gather(2 * i + 1, buf_b)
-        compute(2 * i, buf_a, out_a)
-        scatter(jnp.maximum(2 * i - 1, 0), out_b)
-        gather(jnp.minimum(2 * i + 2, last), buf_a)
-        compute(2 * i + 1, buf_b, out_b)
-        scatter(2 * i, out_a)
-        return 0
-
-    lax.fori_loop(0, L // C // 2, pair, 0)
-    scatter(last, out_b)
-
-    d_ref[:, :C] = dst[:, 0, :].astype(BF16)
-    d_ref[:, C:] = dst[:, 1, :].astype(BF16)
+    def gather(group, buf):
+        for u in range(GROUP * C):
+            buf[pl.ds(u, 1), :] = gsrc[pl.ds(ord_ref[group * GROUP * C + u], 1), :]
+
+    def compute(group, buf, out):
+        each = range(GROUP)
+        rows = [pl.ds((group * GROUP + i) * C, C) for i in each]
+        t0 = [ts_ref[0, rows[i], :C] for i in each]
+        t1 = [ts_ref[0, rows[i], C:] for i in each]
+        probs = [pr_ref[0, rows[i], :] for i in each]
+        g = [jnp.where(keep, buf[pl.ds(i * C, C), :], 0.0).astype(BF16) for i in each]
+        dp = [dot(t0[i], g[i], 1, 1) for i in each]
+        ds = [(probs[i] * (dp[i] - jnp.sum(probs[i] * dp[i], axis=0, keepdims=True))).astype(BF16) for i in each]
+        for i in each:
+            grad = dot(ds[i], t1[i], 0, 0) * 0.125 + jnp.dot(probs[i].astype(BF16), g[i], preferred_element_type=F32)
+            out[pl.ds(2 * i * C, C, stride=2), :] = grad
+        for i in each:
+            out[pl.ds(2 * i * C + 1, C, stride=2), :] = jnp.dot(ds[i], t0[i], preferred_element_type=F32) * 0.125
+
+    def scatter(group, out):
+        for u in range(GROUP * C):
+            dst[pl.ds(pl.multiple_of(ord_ref[group * GROUP * C + u], 2), 2), :] = out[pl.ds(2 * u, 2), :]
+
+    in_turn(gather, compute, scatter, slots[:2], slots[2:])
+
+    @pl.when(step == L // STEP - 1)
+    def _():
+        d_ref[:, :C] = dst[pl.ds(0, L, stride=2), :].astype(BF16)
+        d_ref[:, C:] = dst[pl.ds(1, L, stride=2), :].astype(BF16)
 
 
 def attend_back(head, order, g, ts, probs):
-    i = head % 2
-    vm = pl.BlockSpec(memory_space=pltpu.VMEM)
-    one = lambda shape: pl.BlockSpec((1,) + shape, lambda h: (i, 0, 0), pipeline_mode=pl.Buffered(1))
+    steps = L // STEP
+    whole = lambda shape: pl.BlockSpec(shape, lambda i: (0,) * len(shape), pipeline_mode=pl.Buffered(1))
+    per_step = lambda width: pl.BlockSpec((1, STEP, width), lambda i: (head % 2, i, 0))
     return pl.pallas_call(
         functools.partial(attend_back_kernel, head),
-        grid=(1,),
-        in_specs=[pl.BlockSpec(memory_space=pltpu.SMEM), vm, one((L, 2 * C)), one((L, C))],
-        out_specs=vm,
+        grid=(steps,),
+        in_specs=[
+            pl.BlockSpec((STEP,), lambda i: (head * steps + i,), memory_space=pltpu.SMEM),
+            whole(g.shape), per_step(2 * C), per_step(C),
+        ],
+        out_specs=whole((L, 2 * C)),
         out_shape=jax.ShapeDtypeStruct((L, 2 * C), BF16),
-        scratch_shapes=[
-            VMEM((L, C), F32), VMEM((L, 2, C), F32),
-            VMEM((C, C), F32), VMEM((C, C), F32), VMEM((C, 2, C), F32), VMEM((C, 2, C), F32),
-        ],
-        compiler_params=pltpu.CompilerParams(vmem_limit_bytes=40 << 20),
-        cost_estimate=pl.CostEstimate(flops=24 * 10**9, bytes_accessed=10 << 20, transcendentals=0),
+        scratch_shapes=[VMEM((2 * L, C), F32), VMEM((2 * L, C), F32)]
+        + [VMEM((GROUP * C, C), F32)] * 2 + [VMEM((2 * GROUP * C, C), F32)] * 2,
+        compiler_params=pltpu.CompilerParams(vmem_limit_bytes=60 << 20),
+        cost_estimate=pl.CostEstimate(flops=9 * 10**9, bytes_accessed=10 << 20, transcendentals=0),
         name="attend_back",
     )(order, g, ts, probs)
 
@@ -193,7 +194,6 @@
 OUT_ROW = 1536
 BIAS_ROW = 1728
 QUARTER = 192
-ORDER = 3 * L + 128
 DMA = pltpu.SemaphoreType.DMA
 ANY = pl.BlockSpec(memory_space=pl.ANY)
 VM = pl.BlockSpec(memory_space=pltpu.VMEM)
@@ -252,10 +252,11 @@
     return at(dp_base + half, jnp.where(half == 0, u, 3 - u))
 
 
-def collect_kernel(x_ref, wsrc_ref, bsrc_ref, osrc_ref, up_ref, down_ref, wout_ref, extra_ref, xs_ref, qkv_ref, w_ref, ord_ref, share_ref,
-                   xs, qkv, w, bias, relay,
+def collect_kernel(x_ref, wq_ref, wk_ref, wv_ref, bsrc_ref, osrc_ref, msrc_ref, up_ref, down_ref, wout_ref, extra_ref,
+                   xs_ref, qkv_ref, w_ref, ord_ref, mask_ref, share_ref,
+                   xs, qkv, w, wsrc, bias, relay,
                    chain_recv, relay_recv, pair_recv, chain_send, relay_send, pair_send, own_sem,
-                   wz_recv, wz_send, wp_recv, wp_send, b_recv, b_send, o_recv, o_send, xs_out, qkv_out, w_out, share_sem):
+                   wz_recv, wz_send, wp_recv, wp_send, b_recv, b_send, o_recv, o_send, m_recv, m_send, xs_out, qkv_out, w_out, share_sem, build_sem):
     dp, mp, core, t = place()
     base, half, spot = dp - core, mp // 2, lax.rem(dp, 8) // 2
     step = 1 - 2 * core
@@ -274,6 +275,19 @@
     def _():
         own.start()
 
+    parts = []
+    for h in range(3):
+        for n, part in enumerate((wq_ref, wv_ref, wk_ref, None) if h == 1 else (wv_ref, wq_ref, None, wk_ref)):
+            rows = pl.ds((4 * h + n) * HD, HD)
+            if part is None:
+                wsrc[rows, :] = jnp.zeros((HD, WIDTH), BF16)
+            else:
+                copy = pltpu.make_async_copy(part.at[pl.ds(h * HD, HD)], wsrc.at[rows], build_sem.at[4 * h + n])
+                copy.start()
+                parts.append(copy)
+    for copy in parts:
+        copy.wait()
+
     greet(pltpu.get_barrier_semaphore(), False)
 
     for far in (0, 1):
@@ -281,21 +295,23 @@
 
         @pl.when(gives & (target != mp))
         def _():
-            send(wsrc_ref.at[quarter(spot)], w.at[quarter(spot)], wz_send.at[far], wz_recv, at(dp, target))
+            send(wsrc.at[quarter(spot)], w.at[quarter(spot)], wz_send.at[far], wz_recv, at(dp, target))
             send(bsrc_ref, bias, b_send.at[far], b_recv, at(dp, target))
 
         @pl.when(gives & (target == mp))
         def _():
-            pltpu.make_async_copy(wsrc_ref.at[quarter(spot)], w.at[quarter(spot)], wz_recv).start()
+            pltpu.make_async_copy(wsrc.at[quarter(spot)], w.at[quarter(spot)], wz_recv).start()
             pltpu.make_async_copy(bsrc_ref, bias, b_recv).start()
 
     @pl.when(order_here)
     def _():
         pltpu.make_async_copy(osrc_ref, ord_ref, o_recv).start()
+        pltpu.make_async_copy(msrc_ref, mask_ref, m_recv).start()
 
     @pl.when(jnp.logical_not(order_here))
     def _():
         send(osrc_ref, ord_ref, o_send, o_recv, order_self)
+        send(msrc_ref, mask_ref, m_send, m_recv, order_self)
 
     @pl.when(t == 3)
     def _():
@@ -410,33 +426,37 @@
     for far in (0, 1):
         @pl.when(gives & (mp // 2 + 2 * far != mp))
         def _():
-            wait(wsrc_ref.at[quarter(spot)], wz_send.at[far])
+            wait(wsrc.at[quarter(spot)], wz_send.at[far])
             wait(bsrc_ref, b_send.at[far])
     wait(ord_ref, o_recv)
+    wait(mask_ref, m_recv)
 
     @pl.when(jnp.logical_not(order_here))
     def _():
         wait(osrc_ref, o_send)
+        wait(msrc_ref, m_send)
 
     wait(w, w_out)
     wait(share_ref, share_sem)
 
 
-def collect(x, w, b, order, up, down, out, extra):
+def collect(x, wq, wk, wv, b, order, mask, up, down, out, extra):
     return pl.pallas_call(
         collect_kernel,
-        out_shape=[sds((4 * ROWS, WIDTH), BF16), sds((3, 4 * ROWS, 256), BF16), sds((WIDTH, WIDTH), BF16), sds((ORDER,), jnp.int32), sds((SHARE, WIDTH), BF16)],
-        in_specs=[ANY] * 8,
-        out_specs=[ANY] * 5,
+        out_shape=[sds((4 * ROWS, WIDTH), BF16), sds((3, 4 * ROWS, 256), BF16), sds((WIDTH, WIDTH), BF16), sds((3 * L,), jnp.int32),
+                   sds((1, L), jnp.int32), sds((SHARE, WIDTH), BF16)],
+        in_specs=[ANY] * 11,
+        out_specs=[ANY] * 6,
         scratch_shapes=[
-            VMEM((4 * ROWS, WIDTH), BF16), VMEM((4 * ROWS, WIDTH), BF16), VMEM((WIDTH, WIDTH), BF16), VMEM((8, 256), F32),
-            VMEM((ROWS, WIDTH), BF16),
+            VMEM((4 * ROWS, WIDTH), BF16), VMEM((4 * ROWS, WIDTH), BF16), VMEM((WIDTH, WIDTH), BF16), VMEM((WIDTH, WIDTH), BF16),
+            VMEM((8, 256), F32), VMEM((ROWS, WIDTH), BF16),
             DMA((4, SUBS)), DMA((SUBS,)), DMA((4, SUBS)), DMA((3, SUBS)), DMA((SUBS,)), DMA((4, SUBS)), DMA,
-            DMA, DMA((2,)), DMA((4,)), DMA((4,)), DMA, DMA((2,)), DMA, DMA, DMA((4, SUBS)), DMA((4, SUBS, 3)), DMA, DMA,
+            DMA, DMA((2,)), DMA((4,)), DMA((4,)), DMA, DMA((2,)), DMA, DMA, DMA, DMA,
+            DMA((4, SUBS)), DMA((4, SUBS, 3)), DMA, DMA, DMA((12,)),
         ],
-        compiler_params=pltpu.CompilerParams(collective_id=0, has_side_effects=True, vmem_limit_bytes=40 << 20),
+        compiler_params=pltpu.CompilerParams(collective_id=0, has_side_effects=True, vmem_limit_bytes=60 << 20),
         name="collect",
-    )(x, w, b, order, up, down, out, extra)
+    )(x, wq, wk, wv, b, order, mask, up, down, out, extra)
 
 
 def greet_exchange(barrier):
@@ -548,10 +568,11 @@
     )(a, b)
 
 
-def settle_kernel(d0_ref, d1_ref, d2_ref, xs_ref, w_ref, extra_ref, mine_ref, out_ref, heads_ref, grads_ref,
-                  stage, pair_in, chain_in, gw, gwl, h_in, z_in, z_out,
+def settle_kernel(d0_ref, d1_ref, d2_ref, xs_ref, w_ref, extra_ref, mine_ref, out_ref, *rest):
+    pieces_out, rest = rest[:8], rest[8:]
+    (heads_ref, grads_ref, stage, pair_in, chain_in, gw, gwl, h_in, z_in, z_out,
                   pair_recv, pair_send, chain_recv, chain_send, relay_send,
-                  s_recv, s_send, c_recv, c_send, h_recv, h_send, z_recv, z_send, q_recv, q_send):
+                  s_recv, s_send, c_recv, c_send, h_recv, h_send, z_recv, z_send, q_recv, q_send, out_sem) = rest
     dp, mp, core, t = place()
     base, spot = dp - core, lax.rem(dp, 8) // 2
     step = 1 - 2 * core
@@ -726,6 +747,17 @@
             wait(heads_ref.at[quarter(q)], q_recv.at[q])
     for j in range(4):
         wait(share(j, 1 - core), c_recv.at[j])
+    copies = []
+    for first, rows, n in ((0, 768, 3), (768, 768, 4), (OUT_ROW, 192, 5), (BIAS_ROW, 64, 6)):
+        copies.append(pltpu.make_async_copy(grads_ref.at[pl.ds(first, rows)], pieces_out[n], out_sem.at[n]))
+    for h in range(3):
+        for n, where in enumerate((0, 2, 1) if h == 1 else (1, 3, 0)):
+            src = heads_ref.at[pl.ds((4 * h + where) * HD, HD)]
+            copies.append(pltpu.make_async_copy(src, pieces_out[n].at[pl.ds(h * HD, HD)], out_sem.at[8 + 3 * h + n]))
+        src = heads_ref.at[pl.ds(h * 256 + (192 if h == 1 else 128), 16)]
+        copies.append(pltpu.make_async_copy(src, pieces_out[7].at[h], out_sem.at[17 + h]))
+    for copy in copies:
+        copy.start()
 
     for s in range(SUBS):
         piece = stage.at[pl.ds(s * SUB, SUB)]
@@ -758,18 +790,22 @@
         for k in range(7):
             wait(z_out, q_send.at[k])
 
+    for copy in copies:
+        copy.wait()
+
 
 def settle(d0, d1, d2, xs, w, extra, mine):
     return pl.pallas_call(
         settle_kernel,
-        out_shape=[sds((ROWS, WIDTH), BF16), sds((WIDTH, WIDTH), BF16), sds((PACK, WIDTH), BF16)],
+        out_shape=[sds((ROWS, WIDTH), BF16)] + [sds((rows, WIDTH), BF16) for rows in (192, 192, 192, 768, 768, 192, 64)]
+        + [sds((3, 16, WIDTH), BF16)],
         in_specs=[VM] * 7,
-        out_specs=[VM] * 3,
-        scratch_shapes=[VMEM((4 * ROWS, WIDTH), BF16)] * 3 + [
+        out_specs=[VM] + [ANY] * 8,
+        scratch_shapes=[VMEM((WIDTH, WIDTH), BF16), VMEM((PACK, WIDTH), BF16)] + [VMEM((4 * ROWS, WIDTH), BF16)] * 3 + [
             VMEM((WIDTH, WIDTH), F32), VMEM((WIDTH, WIDTH), BF16), VMEM((4, QUARTER, WIDTH), BF16), VMEM((2, QUARTER, WIDTH), BF16),
             VMEM((QUARTER, WIDTH), BF16),
             DMA((4, SUBS)), DMA((4, SUBS)), DMA((4, SUBS)), DMA((3, SUBS)), DMA((SUBS,)),
-            DMA((4,)), DMA((4,)), DMA((4,)), DMA((4,)), DMA((4,)), DMA((4,)), DMA((2,)), DMA, DMA((4,)), DMA((7,)),
+            DMA((4,)), DMA((4,)), DMA((4,)), DMA((4,)), DMA((4,)), DMA((4,)), DMA((2,)), DMA, DMA((4,)), DMA((7,)), DMA((20,)),
         ],
         compiler_params=pltpu.CompilerParams(collective_id=3, has_side_effects=True, vmem_limit_bytes=60 << 20),
         name="settle",
@@ -777,7 +813,7 @@
 
 
 EPS = 1e-12
-CHUNK = 256
+CHUNK = 512
 FF_MODEL = 768
 
 
@@ -796,9 +832,9 @@
 
 
 def ffn_kernel(c01_ref, c2_ref, tok_ref, cot_ref, vec_ref, *rest):
-    pieces, rest = rest[:4], rest[4:]
-    (out_ref, res_ref, g01_ref, g2_ref, sum_ref,
-     w, wout, ctx, x, x_t, gf, gf_t, act, slope, zhat, acc, rstd, cols, recv,
+    pieces, rest = (rest[0], rest[1], rest[2].at[0], rest[2].at[1]), rest[3:]
+    (out_ref, res_ref, g01_ref, g2_ref, keep_ref, give_ref,
+     w, wout, ctx, x, x_t, gf, act, slope, zhat, acc, rstd, cols, recv,
      w_local, w_send, w_recv, g_send, g_recv, out_sem) = rest
     dp, mp, core, t = place()
     partner = at(dp + 1 - 2 * core, mp)
@@ -810,14 +846,20 @@
     def rows_of(shard, j, parity):
         return w.at[shard, pl.ds(pl.multiple_of((2 * j + parity) * SHARE, SHARE), SHARE)]
 
-    first, second = jnp.where(core == 0, 1, 2), jnp.where(core == 0, 2, 1)
-    for piece, rel in ((3, 3), (2, second), (1, first), (0, 0)):
+    def bring(j, piece):
         for k in range(4):
             src = pieces[piece].at[k]
             shard = lax.rem(mp - k + 4, 4)
-            j = spot ^ rel
             pltpu.make_async_copy(src, rows_of(shard, j, core), w_local.at[j, shard]).start()
             send(src, rows_of(shard, j, core), w_send.at[j, shard], w_recv.at[j, shard], partner)
+
+    for own in range(4):
+        for c in range(2):
+            @pl.when((spot == own) & (core == c))
+            def _():
+                for j in (3, 0, 1, 2):
+                    rel = j ^ own
+                    bring(j, rel if rel in (0, 3) or c == 0 else 3 - rel)
 
     lane = lax.broadcasted_iota(jnp.int32, (1, C), 1)
     for g in range(4):
@@ -834,9 +876,7 @@
             pltpu.make_async_copy(ref, ref, w_local.at[j, shard]).wait()
             pltpu.make_async_copy(ref, ref, w_recv.at[j, shard]).wait()
 
-    for j in (3, 0, 1, 2):
-        wait_weights(j)
-
+    wait_weights(3)
     for m in range(4):
         wout[pl.ds(m * C, C), :] = w[m, pl.ds(OUT_ROW, C), :]
         wout[pl.ds(4 * C + m * HD, HD), :] = w[m, pl.ds(OUT_ROW + C, HD), :]
@@ -844,7 +884,7 @@
     cols[...] = jnp.zeros_like(cols)
     b_out, gain1, bias1, b_down, gain2, bias2 = (vec_ref[pl.ds(i, 1), :] for i in range(6))
 
-    def forward(r, _):
+    def first_norm(r, _):
         rows = pl.ds(pl.multiple_of(r * CHUNK, CHUNK), CHUNK)
         h = jnp.dot(ctx[rows, :], wout[...], preferred_element_type=F32) + tok_ref[rows, :].astype(F32) + b_out
         h = h - row_mean(h)
@@ -857,21 +897,32 @@
         x[rows, :] = first.astype(BF16)
         x_t[:, rows] = first.T.astype(BF16)
 
-        def hidden(m, _):
-            total = acc[rows, :]
-            up_bias = w[m, pl.ds(BIAS_ROW, 16), :].astype(F32)[0:1, :]
+        return 0
+
+    lax.fori_loop(0, 1024 // CHUNK, first_norm, 0)
+    for j in range(3):
+        wait_weights(j)
+
+    def forward(r, _):
+        rows = pl.ds(pl.multiple_of(r * CHUNK, CHUNK), CHUNK)
+
+        def up(m, f):
+            cut = pl.ds(f * 256, 256)
+            bias = w[m, pl.ds(BIAS_ROW, 16), cut].astype(F32)[0:1, :]
+            pre = jnp.dot(x[rows, :], w[m, pl.ds(0, 768), cut], preferred_element_type=F32) + bias
+            value, grad = gelu_and_slope(pre)
+            act[m, rows, cut] = value.astype(BF16)
+            slope[m, rows, cut] = grad.astype(BF16)
+
+        def down(m):
+            acc[rows, :] += jnp.dot(act[m, rows, :], w[m, pl.ds(768, 768), :], preferred_element_type=F32)
+
+        for m in range(4):
             for f in range(3):
-                cut = pl.ds(f * 256, 256)
-                pre = jnp.dot(x[rows, :], w[m, pl.ds(0, 768), cut], preferred_element_type=F32) + up_bias[:, f * 256 : f * 256 + 256]
-                value, grad = gelu_and_slope(pre)
-                value = value.astype(BF16)
-                act[m, rows, cut] = value
-                slope[m, rows, cut] = grad.astype(BF16)
-                total += jnp.dot(value, w[m, pl.ds(768 + f * 256, 256), :], preferred_element_type=F32)
-            acc[rows, :] = total
-            return 0
-
-        lax.fori_loop(0, 4, hidden, 0)
+                up(m, f)
+                if m and f == 0:
+                    down(m - 1)
+        down(3)
 
         z = acc[rows, :]
         z = z - row_mean(z)
@@ -886,7 +937,6 @@
         cols[pl.ds(5, 1), :] += jnp.sum(gs, axis=0, keepdims=True)
         acc[rows, :] = gs
         gf[rows, :] = gs.astype(BF16)
-        gf_t[:, rows] = gs.T.astype(BF16)
         return 0
 
     lax.fori_loop(0, 1024 // CHUNK, forward, 0)
@@ -903,14 +953,11 @@
     def backward(m, _):
         def rows_back(r, _):
             rows = pl.ds(pl.multiple_of(r * CHUNK, CHUNK), CHUNK)
-            total = acc[rows, :]
             for f in range(3):
                 cut = pl.ds(f * 256, 256)
                 ga = dot(gf[rows, :], w[m, pl.ds(768 + f * 256, 256), :], 1, 1)
-                gp = (ga * slope[m, rows, cut].astype(F32)).astype(BF16)
-                slope[m, rows, cut] = gp
-                total += dot(gp, w[m, pl.ds(0, 768), cut], 1, 1)
-            acc[rows, :] = total
+                slope[m, rows, cut] = (ga * slope[m, rows, cut].astype(F32)).astype(BF16)
+            acc[rows, :] += dot(slope[m, rows, :], w[m, pl.ds(0, 768), :], 1, 1)
             return 0
 
         lax.fori_loop(0, 1024 // CHUNK, rows_back, 0)
@@ -919,7 +966,7 @@
             cut = pl.ds(f * 256, 256)
             gp = slope[m, :, cut]
             w[m, pl.ds(0, 768), cut] = jnp.dot(x_t[...], gp, preferred_element_type=F32).astype(BF16)
-            w[m, pl.ds(768, 768), cut] = jnp.dot(gf_t[...], act[m, :, cut], preferred_element_type=F32).astype(BF16)
+            w[m, pl.ds(768 + f * 256, 256), :] = dot(act[m, :, cut], gf[...], 0, 0).astype(BF16)
             bias.append(jnp.sum(gp.astype(F32), axis=0, keepdims=True))
         cols[pl.ds(8 + m, 1), :] = jnp.concatenate(bias, axis=1)
         for j in range(3):
@@ -978,7 +1025,10 @@
             wait(recv.at[m, j], g_recv.at[m, j])
             cut = pl.ds(pl.multiple_of((2 * j + core) * SHARE, SHARE), SHARE)
             recv[m, j] = (recv[m, j].astype(F32) + w[m, cut, :].astype(F32)).astype(BF16)
-            pltpu.make_async_copy(recv.at[m, j], sum_ref.at[along, across, m], out_sem.at[m, rel]).start()
+            for side, ref in enumerate((keep_ref, give_ref)):
+                @pl.when(along == side)
+                def _():
+                    pltpu.make_async_copy(recv.at[m, j], ref.at[across, m], out_sem.at[m, rel]).start()
     for m in range(4):
         for j in range(4):
             wait(recv.at[m, j], out_sem.at[m, j])
@@ -992,12 +1042,12 @@
     return pl.pallas_call(
         ffn_kernel,
         out_shape=[sds((1024, 768), BF16), sds((1024, 768), F32), sds((4, 1024, C), BF16), sds((4, 512, C), BF16),
-                   sds((2, 2, 4, SHARE, 768), BF16)],
-        in_specs=[vm] * 5 + [any_] * 4,
-        out_specs=[vm] * 4 + [any_],
+                   sds((2, 4, SHARE, 768), BF16), sds((2, 4, SHARE, 768), BF16)],
+        in_specs=[vm] * 5 + [any_] * 3,
+        out_specs=[vm] * 4 + [any_] * 2,
         scratch_shapes=[
             VMEM((4, PACK, 768), BF16), VMEM((768, 768), BF16),
-            VMEM((1024, 768), BF16), VMEM((1024, 768), BF16), VMEM((768, 1024), BF16), VMEM((1024, 768), BF16), VMEM((768, 1024), BF16),
+            VMEM((1024, 768), BF16), VMEM((1024, 768), BF16), VMEM((768, 1024), BF16), VMEM((1024, 768), BF16),
             VMEM((4, 1024, 768), BF16), VMEM((4, 1024, 768), BF16),
             VMEM((1024, 768), F32), VMEM((1024, 768), F32), VMEM((1024, 1), F32), VMEM((16, 768), F32),
             VMEM((4, 4, SHARE, 768), BF16),
@@ -1029,41 +1079,38 @@
     dp, mp, core, t = place()
     ring = lambda k: [(z, (z + k) % 4) for z in range(4)]
 
-    live = jnp.sum(key_mask).astype(jnp.int32)
-    order = jnp.where(core == 1, cluster_order ^ 3072, cluster_order).reshape(3 * L)
-    order = jnp.concatenate([order, jnp.broadcast_to(live, (128,))])
-    q, k, v = (w.T.reshape(3, HD, WIDTH) for w in (w_query, w_key, w_value))
-    none = jnp.zeros((HD, WIDTH), BF16)
-    w_heads = jnp.concatenate([part for h in range(3) for part in ([q[h], v[h], k[h], none] if h == 1 else [v[h], q[h], none, k[h]])])
+    order = 2 * jnp.where(core == 1, cluster_order ^ 3072, cluster_order).reshape(3 * L)
     bq, bv, bz = b_query.reshape(3, HD), b_value.reshape(3, HD), jnp.zeros((C,), F32)
     b_heads = jnp.stack([jnp.concatenate([bq[h], bv[h], bz] if h == 1 else [bv[h], bq[h], bz]) for h in range(3)])
     b_heads = jnp.concatenate([b_heads, jnp.zeros((5, 256), F32)])
     extra = jnp.concatenate([b_up.reshape(1, WIDTH), jnp.zeros((PACK - BIAS_ROW - 1, WIDTH), BF16)])
 
-    xs, qkv, w_heads, order, share = collect(tokens, w_heads, b_heads, order, w_up, w_down, w_out, extra)
+    xs, qkv, w_heads, order, mask, share = collect(
+        tokens, w_query.T, w_key.T, w_value.T, b_heads, order, key_mask, w_up, w_down, w_out, extra
+    )
     qkv, share = tie(qkv, share)
     shares = [share] + [lax.ppermute(share, "mp", ring(i)) for i in (1, 2, 3)]
-    c01, ts01, probs01 = attend(0, order, qkv)
+    c01, ts01, probs01 = attend(0, order, mask, qkv)
     c01, *shares = tie(c01, *shares)
     near = jnp.stack(shares)
     next_to = swap(near, 2, 4, n_dp)
-    c2, ts2, probs2 = attend(2, order, qkv)
+    c2, ts2, probs2 = attend(2, order, mask, qkv)
     c2, near, next_to = tie(c2, near, next_to)
     far = swap(jnp.stack([near, next_to]), 4, 2, n_dp)
     c01, c2 = spread(c01, c2)
 
     vecs = jnp.stack([b_out, norm1_gain, norm1_bias, b_down, norm2_gain, norm2_bias, b_out, b_out])
-    layer_out, grad_residual, g01, g2, sums = ffn(c01, c2, tokens, cotangent, vecs, (near, next_to, far[0], far[1]))
-
-    got = swap(sums[1], 2, 4, n_dp)
+    layer_out, grad_residual, g01, g2, keep, give = ffn(c01, c2, tokens, cotangent, vecs, (near, next_to, far))
+
+    got = swap(give, 2, 4, n_dp)
     g01, g2 = regroup(g01, g2)
     d0 = attend_back(0, order, g01, ts01, probs01)
-    d0, sums, got = tie(d0, sums, got)
-    sums = total(sums[0], got)
-    got = swap(sums[1], 4, 2, n_dp)
+    d0, keep, got = tie(d0, keep, got)
+    keep, give = total(keep[0], got[0]), total(keep[1], got[1])
+    got = swap(give, 4, 2, n_dp)
     d1 = attend_back(1, order, g01, ts01, probs01)
-    d1, sums, got = tie(d1, sums, got)
-    sums = total(sums[0], got)
+    d1, keep, got = tie(d1, keep, got)
+    sums = total(keep, got)
     for bit in range(3, n_dp.bit_length() - 1):
         sums = total(sums, swap(sums, 1 << bit, 1 << bit, n_dp))
     parts = [pick(sums, mp, 0)]
@@ -1072,31 +1119,27 @@
     d2 = attend_back(2, order, g2, ts2, probs2)
     d2, *parts = tie(d2, *parts)
     mine = sum(p.astype(F32) for p in parts).astype(BF16)
-    grad_tokens, heads, grads = settle(d0, d1, d2, xs, w_heads, grad_residual, mine)
+    grad_tokens, *sums = settle(d0, d1, d2, xs, w_heads, grad_residual, mine)
+    hq, hk, hv, g_up, g_down, g_out, small, spare = (s.astype(F32) for s in sums)
     for bit in range(3, n_dp.bit_length() - 1):
-        heads = total(heads, swap(heads, 1 << bit, 1 << bit, n_dp))
-    grads, heads = grads.astype(F32), heads.astype(F32).reshape(3, 256, WIDTH)
-    at_q, at_v, at_k = (HD, 0, HD), (0, HD, 0), (3 * HD, 2 * HD, 3 * HD)
-    spare = (2 * HD, 3 * HD, 2 * HD)
-    cols = lambda where: jnp.concatenate([heads[h, where[h] : where[h] + HD] for h in range(3)]).T
-    sums_of = lambda where: jnp.concatenate([heads[h, spare[h], where[h] : where[h] + HD] for h in range(3)])
-
-    vec = lambda i: grads[1728 + i]
+        hq, hk, hv, spare = (s + swap(s, 1 << bit, 1 << bit, n_dp) for s in (hq, hk, hv, spare))
+    sums_of = lambda where: jnp.concatenate([spare[h, 0, where[h] : where[h] + HD] for h in range(3)])
+    vec = lambda i: small[i]
     return (
         layer_out,
         grad_tokens,
-        cols(at_q),
-        sums_of(at_q),
-        cols(at_k),
-        cols(at_v),
-        sums_of(at_v),
-        grads[1536:1728],
+        hq.T,
+        sums_of((HD, 0, HD)),
+        hk.T,
+        hv.T,
+        sums_of((0, HD, 0)),
+        g_out,
         vec(5),
         vec(1),
         vec(2),
-        grads[:768],
+        g_up,
         vec(0),
-        grads[768:1536].T,
+        g_down,
         vec(6),
         vec(3),
         vec(4),

time: 496 us -> 431 us (0.87)
  Pallas kernels: 409 us -> 350 us
  local copies, waits for them, and re-layouts: 42.1 us -> 8.65 us
  waiting for transfers between devices: 5.91 us -> 29.8 us
  other arithmetic: 13.4 us -> 19.8 us
    pallas_call x6, Pallas kernels: 197 us -> 149 us  [the longest x1 73.9 us: settle(): pl.pallas_call(settle_kernel, out_shape=[sds((ROWS, WIDTH), BF16)] + [sds...]
    unnamed x78 -> x38, local copies, waits for them, and re-layouts: 28.8 us -> 4.87 us
    pallas_call x1, Pallas kernels: 80.6 us -> 68.9 us  [ffn(): pl.pallas_call(ffn_kernel, out_shape=[sds((1024, 768), BF16), sds((1024,...]
    ppermute x4, waiting for transfers between devices: 0.01 us -> 9.26 us  [swap(): lax.ppermute(value, 'dp', [(d, d ^ (odd_bits if d % 2 else even_bits)) fo...]
    ppermute x3, waiting for transfers between devices: 5.89 us -> 14.8 us  [body(): parts.append(lax.ppermute(pick(sums, (mp + i) % 4, 0), 'mp', ring(i)))]
    squeeze x5 -> x1, local copies, waits for them, and re-layouts: 6.83 us -> 0.07 us  [body(): spare[h, 0, where[h]:where[h] + HD]]
    convert_element_type x1 -> x5, other arithmetic: 0.42 us -> 6.28 us  [body(): s.astype(F32)]
    ppermute x3, waiting for transfers between devices: 0.01 us -> 5.76 us  [body(): shares = [share] + [lax.ppermute(share, 'mp', ring(i)) for i in (1, 2, 3)]]
  transfers between devices with their start and end apart: 10 -> 10, of which waited for: 1 -> 5; matrix products, arithmetic and copies ran while one was open for 0% -> 0% of each run, Pallas kernels for 40% -> 34%
where the time goes in v2:
time: 431 us; the launch traced here: 426 us
  Pallas kernels  350 us (81%)
  waiting for transfers between devices  29.8 us (7%)
  other arithmetic  19.8 us (5%)
  starting transfers between devices  16.8 us (4%)
  local copies, waits for them, and re-layouts  8.65 us (2%)
    pallas_call x1, Pallas kernels, settle(): pl.pallas_call(settle_kernel, out_shape=[sds((ROWS, WIDTH), BF16)] + [sds...  73.9 us
    pallas_call x1, Pallas kernels, ffn(): pl.pallas_call(ffn_kernel, out_shape=[sds((1024, 768), BF16), sds((1024,...  68.9 us
    pallas_call x1, Pallas kernels, collect(): pl.pallas_call(collect_kernel, out_shape=[sds((4 * ROWS, WIDTH), BF16), s...  63.2 us
    pallas_call x3, Pallas kernels, attend_back(): pl.pallas_call(functools.partial(attend_back_kernel, head), grid=(steps,)...  38.5 us
    pallas_call x2, Pallas kernels, attend(): pl.pallas_call(functools.partial(attend_kernel, first), grid=(heads, step...  36.5 us
    pallas_call x1, Pallas kernels, spread(): pl.pallas_call(spread_kernel, out_shape=[jax.ShapeDtypeStruct((4, 1024, C...  35.1 us
    pallas_call x1, Pallas kernels, regroup(): pl.pallas_call(regroup_kernel, out_shape=[jax.ShapeDtypeStruct((4096, C),...  33.6 us
    ppermute x3, waiting for transfers between devices, body(): parts.append(lax.ppermute(pick(sums, (mp + i) % 4, 0), 'mp', ring(i)))  14.8 us
  transfers between devices with their start and end apart: 10, of which 5 were waited for; matrix products, arithmetic and copies ran while one was open for 0% of the time, Pallas kernels for 34%

profile of v2, /device:TPU:10, one launch (start us, length us, event | category | flops | bytes accessed | tf_op | source)
XLA Modules:
  0.0 426.0 jit_solution(8524064528907849825)
XLA Ops:
  1.3 0.9 fusion.3
  2.3 1.5 fusion.2
  5.2 63.2 %collect.1 = (bf16[4096,768]{1,0:T(8,128)(2,1)}, bf16[3,4096,256]{2,1,0:T(8,128)(2,1)}, bf16[768,768]{1,0:T(8,128)(2,1)}, s32[12288]{0:T(1024)}, s32[1,4096]{1,0:T(1,128)}, /*index=5*/bf16[224,768]{1,0:T(8,128)(2,1)}) custom-call(bf16[1024,768]{1,0:T(8,128)(2,1)} %tok_ref.1, bf16[192,768]{1,0:T(8,128)(2,1)} %bitcast.49, bf16[192,768]{1,0:T(8,128)(2,1)} %bitcast.50, ...), custom_call_target="tpu_custom_call" | custom-call | tf_op jit(solution)/shard_map/collect/pallas_call | solution.py:444
  68.5 7.3 %collective-permute-start.1 = (bf16[224,768]{1,0:T(8,128)(2,1)}, bf16[224,768]{1,0:T(8,128)(2,1)S(1)}, u32[]{:S(2)}, u32[]{:S(2)}) collective-permute-start(bf16[224,768]{1,0:T(8,128)(2,1)} %get-tuple-element.78), channel_id=1, source_target_pairs={{0,2},{1,3},{2,0},{3,1},{4,6},{5,7},{6,4},{7,5},{8,10},{9,11},{10,... | collective-permute-start | bytes 1032200 | tf_op jit(solution)/shard_map/ppermute | solution.py:1092
  76.0 23.6 %attend.2 = (bf16[4096,128]{1,0:T(8,128)(2,1)}, bf16[2,4096,256]{2,1,0:T(8,128)(2,1)}, f32[2,4096,128]{2,1,0:T(8,128)}) custom-call(s32[12288]{0:T(1024)} %get-tuple-element.69.ord_ref, s32[1,4096]{1,0:T(1,128)} %get-tuple-element.70.mask_ref, bf16[3,4096,256]{2,1,0:T(8,128)(2,1)} %get-tuple-element.73.qkv_ref), custom_call_target="tpu_custom_call" | custom-call | flops 17999998976 | bytes 10485760 | tf_op jit(solution)/shard_map/attend/pallas_call | solution.py:97
  99.5 5.8 %collective-permute-done.2 = bf16[224,768]{1,0:T(8,128)(2,1)S(1)} collective-permute-done((bf16[224,768]{1,0:T(8,128)(2,1)}, bf16[224,768]{1,0:T(8,128)(2,1)S(1)}, u32[]{:S(2)}, u32[]{:S(2)}) %collective-permute-start.2) | collective-permute-done | bytes 344096 | tf_op jit(solution)/shard_map/ppermute | solution.py:1092
  105.5 1.5 collective-permute-start.3
  107.0 12.9 %attend.3 = (bf16[2048,128]{1,0:T(8,128)(2,1)}, bf16[1,4096,256]{2,1,0:T(8,128)(2,1)}, f32[1,4096,128]{2,1,0:T(8,128)}) custom-call(s32[12288]{0:T(1024)} %get-tuple-element.69.ord_ref, s32[1,4096]{1,0:T(1,128)} %get-tuple-element.70.mask_ref, bf16[3,4096,256]{2,1,0:T(8,128)(2,1)} %get-tuple-element.73.qkv_ref), custom_call_target="tpu_custom_call" | custom-call | flops 8999999488 | bytes 10485760 | tf_op jit(solution)/shard_map/attend/pallas_call | solution.py:97
  119.9 3.9 collective-permute-done.3.rest_1_
  123.9 1.8 pad_maximum_fusion
  125.8 1.0 collective-permute-start.4
  127.6 35.1 %spread.1 = (bf16[4,1024,128]{2,1,0:T(8,128)(2,1)}, bf16[4,512,128]{2,1,0:T(8,128)(2,1)}) custom-call(bf16[4096,128]{1,0:T(8,128)(2,1)} %get-tuple-element.76.a_ref, bf16[2048,128]{1,0:T(8,128)(2,1)} %get-tuple-element.82.b_ref), custom_call_target="tpu_custom_call" | custom-call | tf_op jit(solution)/shard_map/spread/pallas_call | solution.py:516
  162.7 68.9 %ffn.1 = (bf16[1024,768]{1,0:T(8,128)(2,1)}, f32[1024,768]{1,0:T(8,128)}, bf16[4,1024,128]{2,1,0:T(8,128)(2,1)}, bf16[4,512,128]{2,1,0:T(8,128)(2,1)}, bf16[2,4,...) custom-call(bf16[4,1024,128]{2,1,0:T(8,128)(2,1)} %get-tuple-element.83.c01_ref, ...), custom_call_target="tpu_custom_call" | custom-call | tf_op jit(solution)/shard_map/ffn/pallas_call | solution.py:1042
  231.7 1.0 collective-permute-start.5
  232.7 33.6 %regroup.1 = (bf16[4096,128]{1,0:T(8,128)(2,1)}, bf16[2048,128]{1,0:T(8,128)(2,1)}) custom-call(bf16[4,1024,128]{2,1,0:T(8,128)(2,1)} %get-tuple-element.88.a_ref, bf16[4,512,128]{2,1,0:T(8,128)(2,1)} %get-tuple-element.89.b_ref), custom_call_target="tpu_custom_call" | custom-call | tf_op jit(solution)/shard_map/regroup/pallas_call | solution.py:560
  266.3 13.0 %attend_back.3.d0_ref = bf16[4096,256]{1,0:T(8,128)(2,1)} custom-call(s32[12288]{0:T(1024)} %get-tuple-element.69.ord_ref, bf16[4096,128]{1,0:T(8,128)(2,1)} %get-tuple-element.90.g_ref, bf16[2,4096,256]{2,1,0:T(8,128)(2,1)} %get-tuple-element.91.ts_ref, f32[2,4096,128]{2,1,0:T(8,128)} %get-tuple-element.92.pr_ref), custom_call_target="tpu_custom_call" | custom-call | flops 8999999488 | bytes 10485760 | tf_op jit(solution)/shard_map/attend_back/pallas_call | solution.py:170
  279.3 1.6 copy-done.2
  280.9 4.3 %fusion.1 = (bf16[4,224,768]{2,1,0:T(8,128)(2,1)}, bf16[4,224,768]{2,1,0:T(8,128)(2,1)S(1)}) fusion(bf16[2,4,224,768]{3,2,1,0:T(8,128)(2,1)} %copy-done.2, bf16[2,4,224,768]{3,2,1,0:T(8,128)(2,1)} %get-tuple-element.96), kind=kLoop, calls=%fused_computation.5 | loop fusion | flops 5505024 | bytes 8257536 | tf_op jit(solution)/shard_map/convert_element_type | solution.py:1070
  285.6 12.8 %attend_back.4.d1_ref = bf16[4096,256]{1,0:T(8,128)(2,1)} custom-call(s32[12288]{0:T(1024)} %get-tuple-element.69.ord_ref, bf16[4096,128]{1,0:T(8,128)(2,1)} %get-tuple-element.90.g_ref, bf16[2,4096,256]{2,1,0:T(8,128)(2,1)} %get-tuple-element.91.ts_ref, f32[2,4096,128]{2,1,0:T(8,128)} %get-tuple-element.92.pr_ref), custom_call_target="tpu_custom_call" | custom-call | flops 8999999488 | bytes 10485760 | tf_op jit(solution)/shard_map/attend_back/pallas_call | solution.py:170
  298.4 5.4 %collective-permute-done.6 = bf16[4,224,768]{2,1,0:T(8,128)(2,1)S(1)} collective-permute-done((bf16[4,224,768]{2,1,0:T(8,128)(2,1)}, bf16[4,224,768]{2,1,0:T(8,128)(2,1)S(1)}, u32[]{:S(2)}, u32[]{:S(2)}) %collective-permute-start.6) | collective-permute-done | bytes 1376288 | tf_op jit(solution)/shard_map/ppermute | solution.py:1062
  304.2 3.8 collective-permute-start.7
  308.0 1.5 collective-permute-start.9
  309.5 12.7 %attend_back.5.d2_ref = bf16[4096,256]{1,0:T(8,128)(2,1)} custom-call(s32[12288]{0:T(1024)} %get-tuple-element.69.ord_ref, bf16[2048,128]{1,0:T(8,128)(2,1)} %get-tuple-element.99.g_ref, bf16[1,4096,256]{2,1,0:T(8,128)(2,1)} %get-tuple-element.100.ts_ref, f32[1,4096,128]{2,1,0:T(8,128)} %get-tuple-element.101.pr_ref), custom_call_target="tpu_custom_call" | custom-call | flops 8999999488 | bytes 10485760 | tf_op jit(solution)/shard_map/attend_back/pallas_call | solution.py:170
  322.2 9.1 %collective-permute-done.7 = bf16[224,768]{1,0:T(8,128)(2,1)S(1)} collective-permute-done((bf16[224,768]{1,0:T(8,128)(2,1)S(1)}, bf16[224,768]{1,0:T(8,128)(2,1)S(1)}, u32[]{:S(2)}, u32[]{:S(2)}) %collective-permute-start.7) | collective-permute-done | bytes 344096 | tf_op jit(solution)/shard_map/ppermute | solution.py:1118
  331.2 5.7 %collective-permute-done.8 = bf16[224,768]{1,0:T(8,128)(2,1)S(1)} collective-permute-done((bf16[224,768]{1,0:T(8,128)(2,1)S(1)}, bf16[224,768]{1,0:T(8,128)(2,1)S(1)}, u32[]{:S(2)}, u32[]{:S(2)}) %collective-permute-start.8) | collective-permute-done | bytes 344096 | tf_op jit(solution)/shard_map/ppermute | solution.py:1118
  337.0 0.9 add_convert_fusion.3.mine_ref
  337.9 73.9 %settle.1 = (bf16[1024,768]{1,0:T(8,128)(2,1)}, bf16[192,768]{1,0:T(8,128)(2,1)}, bf16[192,768]{1,0:T(8,128)(2,1)}, bf16[192,768]{1,0:T(8,128)(2,1)}, bf16[768,7...) custom-call(bf16[4096,256]{1,0:T(8,128)(2,1)} %attend_back.3.d0_ref,, ...), custom_call_target="tpu_custom_call" | custom-call | tf_op jit(solution)/shard_map/settle/pallas_call | solution.py:798
  411.7 0.9 convert_element_type.86
  412.7 2.9 convert_element_type.89
  415.7 1.6 convert_element_type.90
  422.6 1.1 copy.38
  424.6 1.1 copy.39
  (70 shorter events, 10.5 us)
Async XLA Ops:
  68.4 31.1 %collective-permute-start = (bf16[224,768]{1,0:T(8,128)(2,1)}, bf16[224,768]{1,0:T(8,128)(2,1)S(1)}, u32[]{:S(2)}, u32[]{:S(2)}) collective-permute-start(bf16[224,768]{1,0:T(8,128)(2,1)} %get-tuple-element.78), channel_id=1, source_target_pairs={{0,1},{1,2},{2,3},{3,0},{4,5},{5,6},{6,7},{7,4},{8,9},{9,10},{10,1... | collective-permute-start | bytes 1032200 | tf_op jit(solution)/shard_map/ppermute | solution.py:1092
  68.5 31.1 %collective-permute-start.1 = (bf16[224,768]{1,0:T(8,128)(2,1)}, bf16[224,768]{1,0:T(8,128)(2,1)S(1)}, u32[]{:S(2)}, u32[]{:S(2)}) collective-permute-start(bf16[224,768]{1,0:T(8,128)(2,1)} %get-tuple-element.78), channel_id=1, source_target_pairs={{0,2},{1,3},{2,0},{3,1},{4,6},{5,7},{6,4},{7,5},{8,10},{9,11},{10,... | collective-permute-start | bytes 1032200 | tf_op jit(solution)/shard_map/ppermute | solution.py:1092
  75.8 29.5 %collective-permute-start.2 = (bf16[224,768]{1,0:T(8,128)(2,1)}, bf16[224,768]{1,0:T(8,128)(2,1)S(1)}, u32[]{:S(2)}, u32[]{:S(2)}) collective-permute-start(bf16[224,768]{1,0:T(8,128)(2,1)} %get-tuple-element.78), channel_id=1, source_target_pairs={{0,3},{1,0},{2,1},{3,2},{4,7},{5,4},{6,5},{7,6},{8,11},{9,8},{10,9... | collective-permute-start | bytes 1032200 | tf_op jit(solution)/shard_map/ppermute | solution.py:1092
  76.0 29.3 %copy-start.6 = (bf16[224,768]{1,0:T(8,128)(2,1)S(1)}, bf16[224,768]{1,0:T(8,128)(2,1)}, u32[]{:S(2)}) copy-start(bf16[224,768]{1,0:T(8,128)(2,1)} %get-tuple-element.78) | copy-start | bytes 1032196
  105.5 18.4 %copy-start = (bf16[4,224,768]{2,1,0:T(8,128)(2,1)}, bf16[4,224,768]{2,1,0:T(8,128)(2,1)S(1)}, u32[]{:S(2)}) copy-start(bf16[4,224,768]{2,1,0:T(8,128)(2,1)S(1)} %pad_maximum_fusion.1.rest_0_) | copy-start | bytes 4128772
  105.5 18.4 %collective-permute-start.3 = (bf16[4,224,768]{2,1,0:T(8,128)(2,1)S(1)}, bf16[4,224,768]{2,1,0:T(8,128)(2,1)S(1)}, u32[]{:S(2)}, u32[]{:S(2)}) collective-permute-start(bf16[4,224,768]{2,1,0:T(8,128)(2,1)S(1)} %pad_maximum_fusion.1.rest_0_), channel_id=1, source_target_pairs={{0,8},{4,20},{8,0},{12,28},{16,24},{20,4},{24,16},{28,12},{1,9},{5... | collective-permute-start | bytes 4128776 | tf_op jit(solution)/shard_map/ppermute | solution.py:1062
  123.9 2.0 copy-start.1
  123.9 2.9 copy-start.12
  123.9 2.9 copy-start.13
  123.9 3.0 copy-start.14
  123.9 3.0 copy-start.15
  123.9 3.0 copy-start.16
  123.9 3.0 copy-start.17
  125.8 36.9 %collective-permute-start.4 = (bf16[2,4,224,768]{3,2,1,0:T(8,128)(2,1)}, bf16[2,4,224,768]{3,2,1,0:T(8,128)(2,1)}, u32[]{:S(2)}, u32[]{:S(2)}) collective-permute-start(bf16[2,4,224,768]{3,2,1,0:T(8,128)(2,1)} %pad_maximum_fusion), channel_id=1, source_target_pairs={{0,16},{4,12},{8,24},{12,4},{16,0},{20,28},{24,8},{28,20},{1,17},{... | collective-permute-start | bytes 8257544 | tf_op jit(solution)/shard_map/ppermute | solution.py:1062
  231.7 47.6 %collective-permute-start.5 = (bf16[2,4,224,768]{3,2,1,0:T(8,128)(2,1)}, bf16[2,4,224,768]{3,2,1,0:T(8,128)(2,1)S(1)}, u32[]{:S(2)}, u32[]{:S(2)}) collective-permute-start(bf16[2,4,224,768]{3,2,1,0:T(8,128)(2,1)} %get-tuple-element.94), channel_id=1, source_target_pairs={{0,8},{4,20},{8,0},{12,28},{16,24},{20,4},{24,16},{28,12},{1,9},{5... | collective-permute-start | bytes 8257544 | tf_op jit(solution)/shard_map/ppermute | solution.py:1062
  279.3 1.6 copy-start.2
  285.2 18.5 %collective-permute-start.6 = (bf16[4,224,768]{2,1,0:T(8,128)(2,1)}, bf16[4,224,768]{2,1,0:T(8,128)(2,1)S(1)}, u32[]{:S(2)}, u32[]{:S(2)}) collective-permute-start(bf16[4,224,768]{2,1,0:T(8,128)(2,1)} %get-tuple-element.128), channel_id=1, source_target_pairs={{0,16},{4,12},{8,24},{12,4},{16,0},{20,28},{24,8},{28,20},{1,17},{... | collective-permute-start | bytes 4128776 | tf_op jit(solution)/shard_map/ppermute | solution.py:1062
  304.2 27.1 %collective-permute-start.7 = (bf16[224,768]{1,0:T(8,128)(2,1)S(1)}, bf16[224,768]{1,0:T(8,128)(2,1)S(1)}, u32[]{:S(2)}, u32[]{:S(2)}) collective-permute-start(bf16[224,768]{1,0:T(8,128)(2,1)S(1)} %get-tuple-element.132), channel_id=1, source_target_pairs={{0,1},{1,2},{2,3},{3,0},{4,5},{5,6},{6,7},{7,4},{8,9},{9,10},{10,1... | collective-permute-start | bytes 1032200 | tf_op jit(solution)/shard_map/ppermute | solution.py:1118
  308.0 29.0 %collective-permute-start.8 = (bf16[224,768]{1,0:T(8,128)(2,1)S(1)}, bf16[224,768]{1,0:T(8,128)(2,1)S(1)}, u32[]{:S(2)}, u32[]{:S(2)}) collective-permute-start(bf16[224,768]{1,0:T(8,128)(2,1)S(1)} %get-tuple-element.131), channel_id=1, source_target_pairs={{0,2},{1,3},{2,0},{3,1},{4,6},{5,7},{6,4},{7,5},{8,10},{9,11},{10,... | collective-permute-start | bytes 1032200 | tf_op jit(solution)/shard_map/ppermute | solution.py:1118
  308.0 29.0 %collective-permute-start.9 = (bf16[224,768]{1,0:T(8,128)(2,1)S(1)}, bf16[224,768]{1,0:T(8,128)(2,1)S(1)}, u32[]{:S(2)}, u32[]{:S(2)}) collective-permute-start(bf16[224,768]{1,0:T(8,128)(2,1)S(1)} %get-tuple-element.130), channel_id=1, source_target_pairs={{0,3},{1,0},{2,1},{3,2},{4,7},{5,4},{6,5},{7,6},{8,11},{9,8},{10,9... | collective-permute-start | bytes 1032200 | tf_op jit(solution)/shard_map/ppermute | solution.py:1118
  412.7 2.9 copy-start.5
  415.7 1.6 copy-start.10
  415.7 2.4 copy-start.9
  417.2 1.7 copy-start.8
  417.2 2.6 copy-start.7
  417.2 3.4 copy-start.11
  418.1 4.5 %copy-start.3 = (bf16[1024,768]{1,0:T(8,128)(2,1)S(1)}, bf16[1024,768]{1,0:T(8,128)(2,1)}, u32[]{:S(2)}) copy-start(bf16[1024,768]{1,0:T(8,128)(2,1)} %get-tuple-element.169) | copy-start | bytes 4718596
  422.6 2.0 copy-start.4

commit v3 on v2

--- a/solution.py
+++ b/solution.py
@@ -189,10 +189,8 @@
 ROWS = 1024
 SUB = 512
 SUBS = ROWS // SUB
-SHARE = 224
-PACK = 8 * SHARE
-OUT_ROW = 1536
-BIAS_ROW = 1728
+SHARE = 208
+SHARE_ALL = SHARE + 32
 QUARTER = 192
 DMA = pltpu.SemaphoreType.DMA
 ANY = pl.BlockSpec(memory_space=pl.ANY)
@@ -252,11 +250,11 @@
     return at(dp_base + half, jnp.where(half == 0, u, 3 - u))
 
 
-def collect_kernel(x_ref, wq_ref, wk_ref, wv_ref, bsrc_ref, osrc_ref, msrc_ref, up_ref, down_ref, wout_ref, extra_ref,
-                   xs_ref, qkv_ref, w_ref, ord_ref, mask_ref, share_ref,
+def collect_kernel(x_ref, wq_ref, wk_ref, wv_ref, bsrc_ref, osrc_ref, msrc_ref,
+                   xs_ref, qkv_ref, w_ref, ord_ref, mask_ref,
                    xs, qkv, w, wsrc, bias, relay,
                    chain_recv, relay_recv, pair_recv, chain_send, relay_send, pair_send, own_sem,
-                   wz_recv, wz_send, wp_recv, wp_send, b_recv, b_send, o_recv, o_send, m_recv, m_send, xs_out, qkv_out, w_out, share_sem, build_sem):
+                   wz_recv, wz_send, wp_recv, wp_send, b_recv, b_send, o_recv, o_send, m_recv, m_send, xs_out, qkv_out, w_out, build_sem):
     dp, mp, core, t = place()
     base, half, spot = dp - core, mp // 2, lax.rem(dp, 8) // 2
     step = 1 - 2 * core
@@ -327,16 +325,6 @@
     def _():
         for s in range(SUBS):
             send(x_ref.at[cut(s)], home(0, s), chain_send.at[0, s], chain_recv.at[0, s], upper)
-
-    pack = ((0, up_ref), (768, down_ref), (OUT_ROW, wout_ref), (BIAS_ROW, extra_ref))
-    for i in range(8):
-        @pl.when(lax.rem(dp, 8) == i)
-        def _():
-            for first, part in pack:
-                low, high = max(first, i * SHARE), min(first + part.shape[0], (i + 1) * SHARE)
-                if low < high:
-                    src = part.at[pl.ds(low - first, high - low)]
-                    pltpu.make_async_copy(src, share_ref.at[pl.ds(low - i * SHARE, high - low)], share_sem).start()
 
     wait(w.at[quarter(spot)], wz_recv)
     for rel in (1, 2, 3):
@@ -437,26 +425,25 @@
         wait(msrc_ref, m_send)
 
     wait(w, w_out)
-    wait(share_ref, share_sem)
-
-
-def collect(x, wq, wk, wv, b, order, mask, up, down, out, extra):
+
+
+def collect(x, wq, wk, wv, b, order, mask):
     return pl.pallas_call(
         collect_kernel,
         out_shape=[sds((4 * ROWS, WIDTH), BF16), sds((3, 4 * ROWS, 256), BF16), sds((WIDTH, WIDTH), BF16), sds((3 * L,), jnp.int32),
-                   sds((1, L), jnp.int32), sds((SHARE, WIDTH), BF16)],
-        in_specs=[ANY] * 11,
-        out_specs=[ANY] * 6,
+                   sds((1, L), jnp.int32)],
+        in_specs=[ANY] * 7,
+        out_specs=[ANY] * 5,
         scratch_shapes=[
             VMEM((4 * ROWS, WIDTH), BF16), VMEM((4 * ROWS, WIDTH), BF16), VMEM((WIDTH, WIDTH), BF16), VMEM((WIDTH, WIDTH), BF16),
             VMEM((8, 256), F32), VMEM((ROWS, WIDTH), BF16),
             DMA((4, SUBS)), DMA((SUBS,)), DMA((4, SUBS)), DMA((3, SUBS)), DMA((SUBS,)), DMA((4, SUBS)), DMA,
             DMA, DMA((2,)), DMA((4,)), DMA((4,)), DMA, DMA((2,)), DMA, DMA, DMA, DMA,
-            DMA((4, SUBS)), DMA((4, SUBS, 3)), DMA, DMA, DMA((12,)),
+            DMA((4, SUBS)), DMA((4, SUBS, 3)), DMA, DMA((12,)),
         ],
         compiler_params=pltpu.CompilerParams(collective_id=0, has_side_effects=True, vmem_limit_bytes=60 << 20),
         name="collect",
-    )(x, wq, wk, wv, b, order, mask, up, down, out, extra)
+    )(x, wq, wk, wv, b, order, mask)
 
 
 def greet_exchange(barrier):
@@ -569,7 +556,7 @@
 
 
 def settle_kernel(d0_ref, d1_ref, d2_ref, xs_ref, w_ref, extra_ref, mine_ref, out_ref, *rest):
-    pieces_out, rest = rest[:8], rest[8:]
+    pieces_out, rest = rest[:9], rest[9:]
     (heads_ref, grads_ref, stage, pair_in, chain_in, gw, gwl, h_in, z_in, z_out,
                   pair_recv, pair_send, chain_recv, chain_send, relay_send,
                   s_recv, s_send, c_recv, c_send, h_recv, h_send, z_recv, z_send, q_recv, q_send, out_sem) = rest
@@ -580,11 +567,11 @@
     group = lax.rem(mp, 2) * 2 + core
     gives = core == lax.rem(mp, 2)
     quarter = lambda q: pl.ds(pl.multiple_of(q * QUARTER, QUARTER), QUARTER)
-    share = lambda j, parity: grads_ref.at[pl.ds(pl.multiple_of((2 * j + parity) * SHARE, SHARE), SHARE)]
+    share = lambda j, parity: grads_ref.at[2 * j + parity]
 
     greet(pltpu.get_barrier_semaphore(), True)
 
-    grads_ref[pl.ds(pl.multiple_of((2 * spot + core) * SHARE, SHARE), SHARE), :] = mine_ref[...]
+    grads_ref[2 * spot + core] = mine_ref[...]
     for rel in (1, 2, 3):
         send(mine_ref, share(spot, core), s_send.at[rel], s_recv.at[rel], at(mate(dp, rel), mp))
 
@@ -748,8 +735,13 @@
     for j in range(4):
         wait(share(j, 1 - core), c_recv.at[j])
     copies = []
-    for first, rows, n in ((0, 768, 3), (768, 768, 4), (OUT_ROW, 192, 5), (BIAS_ROW, 64, 6)):
-        copies.append(pltpu.make_async_copy(grads_ref.at[pl.ds(first, rows)], pieces_out[n], out_sem.at[n]))
+    for i in range(8):
+        for n, (first, rows) in enumerate(((0, 96), (96, 96), (192, 32), (224, 16))):
+            if n == 2 and i >= 6:
+                continue
+            dst = pieces_out[3 + n].at[pl.ds(i * rows, rows)]
+            copies.append(pltpu.make_async_copy(grads_ref.at[i, pl.ds(first, rows)], dst, out_sem.at[20 + 4 * i + n]))
+    copies.append(pltpu.make_async_copy(grads_ref.at[6, pl.ds(192, 16)], pieces_out[8], out_sem.at[0]))
     for h in range(3):
         for n, where in enumerate((0, 2, 1) if h == 1 else (1, 3, 0)):
             src = heads_ref.at[pl.ds((4 * h + where) * HD, HD)]
@@ -797,15 +789,15 @@
 def settle(d0, d1, d2, xs, w, extra, mine):
     return pl.pallas_call(
         settle_kernel,
-        out_shape=[sds((ROWS, WIDTH), BF16)] + [sds((rows, WIDTH), BF16) for rows in (192, 192, 192, 768, 768, 192, 64)]
-        + [sds((3, 16, WIDTH), BF16)],
+        out_shape=[sds((ROWS, WIDTH), BF16)] + [sds((rows, WIDTH), BF16) for rows in (192, 192, 192, 768, 768, 192, 128)]
+        + [sds((3, 16, WIDTH), BF16), sds((16, WIDTH), BF16)],
         in_specs=[VM] * 7,
-        out_specs=[VM] + [ANY] * 8,
-        scratch_shapes=[VMEM((WIDTH, WIDTH), BF16), VMEM((PACK, WIDTH), BF16)] + [VMEM((4 * ROWS, WIDTH), BF16)] * 3 + [
+        out_specs=[VM] + [ANY] * 9,
+        scratch_shapes=[VMEM((WIDTH, WIDTH), BF16), VMEM((8, SHARE_ALL, WIDTH), BF16)] + [VMEM((4 * ROWS, WIDTH), BF16)] * 3 + [
             VMEM((WIDTH, WIDTH), F32), VMEM((WIDTH, WIDTH), BF16), VMEM((4, QUARTER, WIDTH), BF16), VMEM((2, QUARTER, WIDTH), BF16),
             VMEM((QUARTER, WIDTH), BF16),
             DMA((4, SUBS)), DMA((4, SUBS)), DMA((4, SUBS)), DMA((3, SUBS)), DMA((SUBS,)),
-            DMA((4,)), DMA((4,)), DMA((4,)), DMA((4,)), DMA((4,)), DMA((4,)), DMA((2,)), DMA, DMA((4,)), DMA((7,)), DMA((20,)),
+            DMA((4,)), DMA((4,)), DMA((4,)), DMA((4,)), DMA((4,)), DMA((4,)), DMA((2,)), DMA, DMA((4,)), DMA((7,)), DMA((52,)),
         ],
         compiler_params=pltpu.CompilerParams(collective_id=3, has_side_effects=True, vmem_limit_bytes=60 << 20),
         name="settle",
@@ -820,46 +812,62 @@
 def gelu_and_slope(v):
     size = jnp.abs(v)
     u = 1.0 / (1.0 + (0.3275911 * 0.7071067811865476) * size)
-    bell = jnp.exp(-0.5 * v * v)
-    poly = u * (0.127414796 + u * (-0.142248368 + u * (0.7107068705 + u * (-0.7265760135 + u * 0.5307027145))))
+    bell = jnp.exp2(v * v * -0.7213475204444817 - 1.3257480647361595)
+    poly = u * (0.3193815306 + u * (-0.3565637784 + u * (1.7814779345 + u * (-1.8212559786 + u * 1.3302744294))))
     tail = poly * bell
     cdf = jnp.where(v < 0, tail, 1.0 - tail)
-    return v * cdf, cdf + v * (bell * 0.3989422804014327)
+    return v * cdf, cdf + v * bell
 
 
 def row_mean(v):
     return jnp.sum(v, axis=-1, keepdims=True) * (1.0 / FF_MODEL)
 
 
-def ffn_kernel(c01_ref, c2_ref, tok_ref, cot_ref, vec_ref, *rest):
-    pieces, rest = (rest[0], rest[1], rest[2].at[0], rest[2].at[1]), rest[3:]
-    (out_ref, res_ref, g01_ref, g2_ref, keep_ref, give_ref,
-     w, wout, ctx, x, x_t, gf, act, slope, zhat, acc, rstd, cols, recv,
-     w_local, w_send, w_recv, g_send, g_recv, out_sem) = rest
+def ffn_kernel(c01_ref, c2_ref, tok_ref, cot_ref, vec_ref, near_ref, a_ref, b_ref,
+               out_ref, res_ref, g01_ref, g2_ref, keep_ref, next_ref, give_ref, keep_tail_ref, give_tail_ref,
+               w, wout, ctx, x, gf, act, slope, zhat, acc, rstd, cols, recv, recv2, tail, tail_in,
+               o_local, o_send, o_recv, f_send, f_recv, w_local, w_send, w_recv, d_send, d_recv,
+               g_send, g_recv, m_send, m_recv, t_send, t_recv, out_sem, tail_sem):
     dp, mp, core, t = place()
-    partner = at(dp + 1 - 2 * core, mp)
+    step = 1 - 2 * core
+    partner = at(dp + step, mp)
     spot = lax.rem(dp, 8) // 2
+    one, two = jnp.where(core == 0, 1, 2), jnp.where(core == 0, 2, 1)
+    mate_a, mate_b = at(dp + 2 * ((spot ^ one) - spot), mp), at(dp + 2 * ((spot ^ two) - spot), mp)
+    shard = lambda k: lax.rem(mp - k + 4, 4)
     barrier = pltpu.get_barrier_semaphore()
-    pl.semaphore_signal(barrier, inc=1, device_id=partner, device_id_type=MESH)
-    pl.semaphore_wait(barrier, 1)
-
-    def rows_of(shard, j, parity):
-        return w.at[shard, pl.ds(pl.multiple_of((2 * j + parity) * SHARE, SHARE), SHARE)]
-
-    def bring(j, piece):
+    for device in (partner, mate_a, mate_b):
+        signal(barrier, device)
+    pl.semaphore_wait(barrier, 3)
+
+    def out_rows(m, i):
+        first = jnp.where(i < 4, m * C + 32 * i, 4 * C + m * HD + 32 * (i - 4))
+        return wout.at[pl.ds(pl.multiple_of(first, 32), 32)]
+
+    sources = ((0, near_ref), (one, a_ref), (two, b_ref))
+    far = spot ^ 3
+    for k in range(4):
+        @pl.when(spot ^ one < 3)
+        def _():
+            send(a_ref.at[k, pl.ds(SHARE, 32)], out_rows(shard(k), 2 * (spot ^ one) + core), f_send.at[k], f_recv.at[k], mate_b)
+    for rel, ref in sources:
+        j = spot ^ rel
         for k in range(4):
-            src = pieces[piece].at[k]
-            shard = lax.rem(mp - k + 4, 4)
-            pltpu.make_async_copy(src, rows_of(shard, j, core), w_local.at[j, shard]).start()
-            send(src, rows_of(shard, j, core), w_send.at[j, shard], w_recv.at[j, shard], partner)
-
-    for own in range(4):
-        for c in range(2):
-            @pl.when((spot == own) & (core == c))
-            def _():
-                for j in (3, 0, 1, 2):
-                    rel = j ^ own
-                    bring(j, rel if rel in (0, 3) or c == 0 else 3 - rel)
+            src = ref.at[k, pl.ds(SHARE, 32)]
+
+            @pl.when(j < 3)
+            def _():
+                pltpu.make_async_copy(src, out_rows(shard(k), 2 * j + core), o_local.at[j, k]).start()
+                send(src, out_rows(shard(k), 2 * j + core), o_send.at[j, k], o_recv.at[j, k], partner)
+
+    body = pl.ds(0, SHARE)
+    for k in range(4):
+        send(a_ref.at[k, body], w.at[2 * (spot ^ one) + core, shard(k)], d_send.at[k], d_recv.at[k], mate_b)
+    for rel, ref in sources:
+        for k in range(4):
+            mine = w.at[2 * (spot ^ rel) + core, shard(k)]
+            pltpu.make_async_copy(ref.at[k, body], mine, w_local.at[rel, k]).start()
+            send(ref.at[k, body], mine, w_send.at[rel, k], w_recv.at[rel, k], partner)
 
     lane = lax.broadcasted_iota(jnp.int32, (1, C), 1)
     for g in range(4):
@@ -869,23 +877,26 @@
         col = pl.ds(4 * C + g * HD, C)
         ctx[pl.ds(0, 512), col] = jnp.where(lane < HD, a, pltpu.roll(b, HD, 1)).astype(BF16)
         ctx[pl.ds(512, 512), col] = jnp.where(lane < HD, pltpu.roll(a, HD, 1), b).astype(BF16)
-
-    def wait_weights(j):
-        for shard in range(4):
-            ref = w.at[shard, pl.ds(0, SHARE)]
-            pltpu.make_async_copy(ref, ref, w_local.at[j, shard]).wait()
-            pltpu.make_async_copy(ref, ref, w_recv.at[j, shard]).wait()
-
-    wait_weights(3)
-    for m in range(4):
-        wout[pl.ds(m * C, C), :] = w[m, pl.ds(OUT_ROW, C), :]
-        wout[pl.ds(4 * C + m * HD, HD), :] = w[m, pl.ds(OUT_ROW + C, HD), :]
-
     cols[...] = jnp.zeros_like(cols)
     b_out, gain1, bias1, b_down, gain2, bias2 = (vec_ref[pl.ds(i, 1), :] for i in range(6))
-
-    def first_norm(r, _):
-        rows = pl.ds(pl.multiple_of(r * CHUNK, CHUNK), CHUNK)
+    row_chunks = [pl.ds(r * CHUNK, CHUNK) for r in range(1024 // CHUNK)]
+
+    part = wout.at[pl.ds(0, 32)]
+    for k in range(4):
+        @pl.when(far < 3)
+        def _():
+            mine = out_rows(shard(k), 2 * far + core)
+            wait(mine, f_recv.at[k])
+            send(mine, mine, o_send.at[far, k], o_recv.at[far, k], partner)
+    for j in range(3):
+        for k in range(4):
+            @pl.when(far != j)
+            def _():
+                wait(part, o_local.at[j, k])
+
+            wait(part, o_recv.at[j, k])
+
+    for rows in row_chunks:
         h = jnp.dot(ctx[rows, :], wout[...], preferred_element_type=F32) + tok_ref[rows, :].astype(F32) + b_out
         h = h - row_mean(h)
         scale = lax.rsqrt(row_mean(h * h) + EPS)
@@ -895,35 +906,41 @@
         first = h * gain1 + bias1
         acc[rows, :] = first + b_down
         x[rows, :] = first.astype(BF16)
-        x_t[:, rows] = first.T.astype(BF16)
-
-        return 0
-
-    lax.fori_loop(0, 1024 // CHUNK, first_norm, 0)
-    for j in range(3):
-        wait_weights(j)
-
-    def forward(r, _):
-        rows = pl.ds(pl.multiple_of(r * CHUNK, CHUNK), CHUNK)
-
-        def up(m, f):
-            cut = pl.ds(f * 256, 256)
-            bias = w[m, pl.ds(BIAS_ROW, 16), cut].astype(F32)[0:1, :]
-            pre = jnp.dot(x[rows, :], w[m, pl.ds(0, 768), cut], preferred_element_type=F32) + bias
-            value, grad = gelu_and_slope(pre)
-            act[m, rows, cut] = value.astype(BF16)
-            slope[m, rows, cut] = grad.astype(BF16)
-
-        def down(m):
-            acc[rows, :] += jnp.dot(act[m, rows, :], w[m, pl.ds(768, 768), :], preferred_element_type=F32)
-
-        for m in range(4):
-            for f in range(3):
-                up(m, f)
-                if m and f == 0:
-                    down(m - 1)
-        down(3)
-
+
+    whole = w.at[0, 0]
+    up_pair = lambda j: w[pl.ds(2 * j, 2), :, pl.ds(0, 96), :].reshape(768, FF_MODEL)
+    down_pair = lambda j: w[pl.ds(2 * j, 2), :, pl.ds(96, 96), :].reshape(768, FF_MODEL)
+
+    def up(j, rel, rows):
+        bias = [jnp.sum(w[2 * j + f, :, pl.ds(192, 16), :].astype(F32), axis=0)[0:1, :384] for f in range(2)]
+        pre = dot(x[rows, :], up_pair(j), 1, 1) + jnp.concatenate(bias, axis=1)
+        value, grad = gelu_and_slope(pre)
+        act[rel, rows, :] = value.astype(BF16)
+        slope[rel, rows, :] = grad.astype(BF16)
+
+    def down(j, rel, rows):
+        acc[rows, :] += jnp.dot(act[rel, rows, :], down_pair(j), preferred_element_type=F32)
+
+    for rel in range(4):
+        j = spot ^ rel
+        if rel == 2:
+            for k in range(4):
+                mine = w.at[2 * (spot ^ 3) + core, shard(k)]
+                wait(mine, d_recv.at[k])
+                send(mine, mine, w_send.at[3, k], w_recv.at[3, k], partner)
+        for k in range(4):
+            if rel < 3:
+                wait(whole, w_local.at[rel, k])
+            wait(whole, w_recv.at[rel, k])
+        before = None
+        for rows in row_chunks:
+            up(j, rel, rows)
+            if before is not None:
+                down(j, rel, before)
+            before = rows
+        down(j, rel, before)
+
+    for rows in row_chunks:
         z = acc[rows, :]
         z = z - row_mean(z)
         scale = lax.rsqrt(row_mean(z * z) + EPS)
@@ -937,46 +954,49 @@
         cols[pl.ds(5, 1), :] += jnp.sum(gs, axis=0, keepdims=True)
         acc[rows, :] = gs
         gf[rows, :] = gs.astype(BF16)
-        return 0
-
-    lax.fori_loop(0, 1024 // CHUNK, forward, 0)
-
-    def give(m, j):
-        cut = pl.ds(pl.multiple_of((2 * j + 1 - core) * SHARE, SHARE), SHARE)
-        send(w.at[m, cut], recv.at[m, j], g_send.at[m, j], g_recv.at[m, j], partner)
-
-    for j in range(4):
-        for shard in range(4):
-            ref = w.at[shard, pl.ds(0, SHARE)]
-            pltpu.make_async_copy(ref, ref, w_send.at[j, shard]).wait()
-
-    def backward(m, _):
-        def rows_back(r, _):
-            rows = pl.ds(pl.multiple_of(r * CHUNK, CHUNK), CHUNK)
-            for f in range(3):
-                cut = pl.ds(f * 256, 256)
-                ga = dot(gf[rows, :], w[m, pl.ds(768 + f * 256, 256), :], 1, 1)
-                slope[m, rows, cut] = (ga * slope[m, rows, cut].astype(F32)).astype(BF16)
-            acc[rows, :] += dot(slope[m, rows, :], w[m, pl.ds(0, 768), :], 1, 1)
-            return 0
-
-        lax.fori_loop(0, 1024 // CHUNK, rows_back, 0)
-        bias = []
-        for f in range(3):
-            cut = pl.ds(f * 256, 256)
-            gp = slope[m, :, cut]
-            w[m, pl.ds(0, 768), cut] = jnp.dot(x_t[...], gp, preferred_element_type=F32).astype(BF16)
-            w[m, pl.ds(768 + f * 256, 256), :] = dot(act[m, :, cut], gf[...], 0, 0).astype(BF16)
-            bias.append(jnp.sum(gp.astype(F32), axis=0, keepdims=True))
-        cols[pl.ds(8 + m, 1), :] = jnp.concatenate(bias, axis=1)
-        for j in range(3):
-            give(m, j)
-        return 0
-
-    lax.fori_loop(0, 4, backward, 0)
-
-    def first_back(r, _):
-        rows = pl.ds(pl.multiple_of(r * CHUNK, CHUNK), CHUNK)
+
+    for rel in range(4):
+        for k in range(4):
+            wait(whole, w_send.at[rel, k])
+    for k in range(4):
+        wait(whole, d_send.at[k])
+
+    grads = pl.ds(0, 192)
+    order = (3, 1, 2, 0)
+    place_of = {rel: q for q, rel in enumerate(order)}
+
+    def add_cores(rel):
+        q, i = place_of[rel], 2 * (spot ^ rel) + core
+        wait(recv.at[q], g_recv.at[q])
+        for m in range(4):
+            recv[q, m] = (recv[q, m].astype(F32) + w[i, m, grads, :].astype(F32)).astype(BF16)
+        if rel == 3:
+            send(recv.at[q], recv2, m_send, m_recv, mate_a)
+        elif rel == 0:
+            pltpu.make_async_copy(recv.at[q], keep_ref, out_sem.at[0]).start()
+        else:
+            @pl.when(one == rel)
+            def _():
+                pltpu.make_async_copy(recv.at[q], next_ref, out_sem.at[1]).start()
+
+    for q, rel in enumerate(order):
+        j = spot ^ rel
+        for rows in row_chunks:
+            ga = dot(gf[rows, :], down_pair(j), 1, 1)
+            slope[rel, rows, :] = (ga * slope[rel, rows, :].astype(F32)).astype(BF16)
+            acc[rows, :] += jnp.dot(slope[rel, rows, :], up_pair(j), preferred_element_type=F32)
+        for f in range(2):
+            cut = pl.ds(f * 384, 384)
+            gp = slope[rel, :, cut]
+            w[2 * j + f, :, pl.ds(0, 96), :] = dot(gp, x[...], 0, 0).astype(BF16).reshape(4, 96, FF_MODEL)
+            w[2 * j + f, :, pl.ds(96, 96), :] = dot(act[rel, :, cut], gf[...], 0, 0).astype(BF16).reshape(4, 96, FF_MODEL)
+            cols[pl.ds(8 + 2 * j + f, 1), pl.ds(0, 384)] = jnp.sum(gp.astype(F32), axis=0, keepdims=True)
+        send(w.at[2 * j + 1 - core, :, grads], recv.at[q], g_send.at[q], g_recv.at[q], partner)
+        if q:
+            add_cores(order[q - 1])
+
+    ctx_grad = x.at[:, pl.ds(0, 2 * C)]
+    for rows in row_chunks:
         grad = acc[rows, :]
         z = zhat[rows, :]
         dz = grad * gain1
@@ -991,11 +1011,6 @@
         for g in range(4):
             g01_ref[g, rows, :] = gc[:, g * C : g * C + C]
         ctx_grad[rows, :] = gc[:, 4 * C :]
-        return 0
-
-    ctx_grad = x
-    ctx_grad = x.at[:, pl.ds(0, 2 * C)]
-    lax.fori_loop(0, 1024 // CHUNK, first_back, 0)
     for g in (0, 2):
         top = ctx_grad[pl.ds(0, 512), pl.ds(g * HD, C)].astype(F32)
         low = ctx_grad[pl.ds(512, 512), pl.ds(g * HD, C)].astype(F32)
@@ -1003,59 +1018,74 @@
         g2_ref[g + 1] = jnp.where(lane < HD, pltpu.roll(top, HD, 1), low).astype(BF16)
 
     for n in range(3):
-        cut = pl.ds(n * 256, 256)
-        part = dot(ctx[:, cut], gf[...], 0, 0).astype(BF16)
-        if n < 2:
-            for i in range(2):
-                w[2 * n + i, pl.ds(OUT_ROW, C), :] = part[i * C : i * C + C, :]
-        else:
-            for i in range(4):
-                w[i, pl.ds(OUT_ROW + C, HD), :] = part[i * HD : i * HD + HD, :]
-    for m in range(4):
-        w[m, pl.ds(BIAS_ROW, 16), :] = jnp.concatenate(
-            [cols[pl.ds(8 + m, 1), :], cols[pl.ds(0, 6), :], jnp.zeros((9, FF_MODEL), F32)], axis=0
-        ).astype(BF16)
-        give(m, 3)
-
-    for rel in (3, 2, 1, 0):
+        got = dot(ctx[:, pl.ds(n * 256, 256)], gf[...], 0, 0).astype(BF16)
+        for i in range(8):
+            piece = got[i * 32 : i * 32 + 32, :]
+            m, share = (2 * n + i // 4, i % 4) if n < 2 else (i // 2, 4 + i % 2)
+            tail[share % 2, share // 2, m, pl.ds(0, 32), :] = piece
+    vectors = jnp.concatenate([cols[pl.ds(0, 6), :], jnp.zeros((26, FF_MODEL), F32)], axis=0).astype(BF16)
+    for i in range(8):
+        line = jnp.concatenate([cols[pl.ds(8 + i, 1), :], jnp.zeros((15, FF_MODEL), F32)], axis=0).astype(BF16)
+        for m in range(4):
+            tail[i % 2, i // 2, m, pl.ds(32, 16), :] = line
+            if i >= 6:
+                tail[i % 2, i // 2, m, pl.ds(0, 32), :] = vectors if i == 6 else jnp.zeros((32, FF_MODEL), BF16)
+    send(tail.at[1 - core], tail_in, t_send, t_recv, partner)
+    add_cores(0)
+
+    wait(recv2, m_recv)
+    for rel in (1, 2):
+        @pl.when(two == rel)
+        def _():
+            for m in range(4):
+                recv2[m] = (recv2[m].astype(F32) + recv[place_of[rel], m].astype(F32)).astype(BF16)
+    give = pltpu.make_async_copy(recv2, give_ref, out_sem.at[2])
+    give.start()
+    wait(tail_in, t_recv)
+    for rel in range(4):
         j = spot ^ rel
-        along = jnp.where(core == 0, rel % 2, rel // 2)
-        across = jnp.where(core == 0, rel // 2, rel % 2)
         for m in range(4):
-            wait(recv.at[m, j], g_recv.at[m, j])
-            cut = pl.ds(pl.multiple_of((2 * j + core) * SHARE, SHARE), SHARE)
-            recv[m, j] = (recv[m, j].astype(F32) + w[m, cut, :].astype(F32)).astype(BF16)
-            for side, ref in enumerate((keep_ref, give_ref)):
-                @pl.when(along == side)
-                def _():
-                    pltpu.make_async_copy(recv.at[m, j], ref.at[across, m], out_sem.at[m, rel]).start()
-    for m in range(4):
-        for j in range(4):
-            wait(recv.at[m, j], out_sem.at[m, j])
-            wait(recv.at[m, j], g_send.at[m, j])
-
-
-def ffn(c01, c2, tokens, cot, vecs, pieces):
-    dma = pltpu.SemaphoreType.DMA
-    vm, any_ = pl.BlockSpec(memory_space=pltpu.VMEM), pl.BlockSpec(memory_space=pl.ANY)
-    sds = jax.ShapeDtypeStruct
+            tail_in[j, m] = (tail_in[j, m].astype(F32) + tail[core, j, m].astype(F32)).astype(BF16)
+        along, across = jnp.where(core == 0, rel % 2, rel // 2), jnp.where(core == 0, rel // 2, rel % 2)
+        for side, ref in enumerate((keep_tail_ref, give_tail_ref)):
+            @pl.when(along == side)
+            def _():
+                pltpu.make_async_copy(tail_in.at[j], ref.at[across], tail_sem.at[rel]).start()
+    give.wait()
+    wait(recv2, out_sem.at[0])
+    wait(recv2, out_sem.at[1])
+    for rel in range(4):
+        wait(tail_in.at[0], tail_sem.at[rel])
+    for q in range(4):
+        wait(recv.at[q], g_send.at[q])
+    wait(recv2, m_send)
+    wait(tail_in, t_send)
+    for k in range(4):
+        @pl.when(spot ^ one < 3)
+        def _():
+            wait(part, f_send.at[k])
+
+        for j in range(3):
+            wait(part, o_send.at[j, k])
+
+
+def ffn(c01, c2, tokens, cot, vecs, near, a, b):
+    main, rest = sds((4, 192, WIDTH), BF16), sds((2, 4, 48, WIDTH), BF16)
+    rows = lambda dtype: VMEM((1024, WIDTH), dtype)
+    four = lambda *shape: VMEM((4,) + shape, BF16)
     return pl.pallas_call(
         ffn_kernel,
-        out_shape=[sds((1024, 768), BF16), sds((1024, 768), F32), sds((4, 1024, C), BF16), sds((4, 512, C), BF16),
-                   sds((2, 4, SHARE, 768), BF16), sds((2, 4, SHARE, 768), BF16)],
-        in_specs=[vm] * 5 + [any_] * 3,
-        out_specs=[vm] * 4 + [any_] * 2,
+        out_shape=[sds((1024, WIDTH), BF16), sds((1024, WIDTH), F32), sds((4, 1024, C), BF16), sds((4, 512, C), BF16), main, main, main, rest, rest],
+        in_specs=[VM] * 5 + [ANY] * 3,
+        out_specs=[VM] * 4 + [ANY] * 5,
         scratch_shapes=[
-            VMEM((4, PACK, 768), BF16), VMEM((768, 768), BF16),
-            VMEM((1024, 768), BF16), VMEM((1024, 768), BF16), VMEM((768, 1024), BF16), VMEM((1024, 768), BF16),
-            VMEM((4, 1024, 768), BF16), VMEM((4, 1024, 768), BF16),
-            VMEM((1024, 768), F32), VMEM((1024, 768), F32), VMEM((1024, 1), F32), VMEM((16, 768), F32),
-            VMEM((4, 4, SHARE, 768), BF16),
-            dma((4, 4)), dma((4, 4)), dma((4, 4)), dma((4, 4)), dma((4, 4)), dma((4, 4)),
-        ],
+            VMEM((8, 4, SHARE, WIDTH), BF16), VMEM((WIDTH, WIDTH), BF16), rows(BF16), rows(BF16), rows(BF16), four(1024, WIDTH), four(1024, WIDTH),
+            rows(F32), rows(F32), VMEM((1024, 1), F32), VMEM((16, WIDTH), F32), four(4, 192, WIDTH), four(192, WIDTH),
+            VMEM((2, 4, 4, 48, WIDTH), BF16), four(4, 48, WIDTH),
+        ] + [DMA((4, 4))] * 3 + [DMA((4,))] * 2 + [DMA((4, 4))] * 3 + [DMA((4,))] * 4 + [DMA] * 4 + [DMA((3,)), DMA((4,))],
         compiler_params=pltpu.CompilerParams(collective_id=4, has_side_effects=True, vmem_limit_bytes=63 << 20),
         name="ffn",
-    )(c01, c2, tokens, cot, vecs, *pieces)
+    )(c01, c2, tokens, cot, vecs, near, a, b)
 
 
 def swap(value, even_bits, odd_bits, n_dp):
@@ -1083,48 +1113,54 @@
     bq, bv, bz = b_query.reshape(3, HD), b_value.reshape(3, HD), jnp.zeros((C,), F32)
     b_heads = jnp.stack([jnp.concatenate([bq[h], bv[h], bz] if h == 1 else [bv[h], bq[h], bz]) for h in range(3)])
     b_heads = jnp.concatenate([b_heads, jnp.zeros((5, 256), F32)])
-    extra = jnp.concatenate([b_up.reshape(1, WIDTH), jnp.zeros((PACK - BIAS_ROW - 1, WIDTH), BF16)])
-
-    xs, qkv, w_heads, order, mask, share = collect(
-        tokens, w_query.T, w_key.T, w_value.T, b_heads, order, key_mask, w_up, w_down, w_out, extra
-    )
+    i = dp % 8
+    bias_row = lax.dynamic_update_slice(jnp.zeros((16, WIDTH), BF16), lax.dynamic_slice(b_up, (96 * i,), (96,)).reshape(1, 96), (0, 96 * mp))
+    share = jnp.concatenate([
+        lax.dynamic_slice(w_up, (0, 96 * i), (WIDTH, 96)).T,
+        lax.dynamic_slice(w_down, (96 * i, 0), (96, WIDTH)),
+        bias_row,
+        lax.dynamic_slice(w_out, (jnp.minimum(32 * i, 160), 0), (32, WIDTH)),
+    ])
+
+    xs, qkv, w_heads, order, mask = collect(tokens, w_query.T, w_key.T, w_value.T, b_heads, order, key_mask)
     qkv, share = tie(qkv, share)
     shares = [share] + [lax.ppermute(share, "mp", ring(i)) for i in (1, 2, 3)]
     c01, ts01, probs01 = attend(0, order, mask, qkv)
     c01, *shares = tie(c01, *shares)
     near = jnp.stack(shares)
-    next_to = swap(near, 2, 4, n_dp)
+    along, across = swap(near, 2, 4, n_dp), swap(near, 4, 2, n_dp)
     c2, ts2, probs2 = attend(2, order, mask, qkv)
-    c2, near, next_to = tie(c2, near, next_to)
-    far = swap(jnp.stack([near, next_to]), 4, 2, n_dp)
     c01, c2 = spread(c01, c2)
 
     vecs = jnp.stack([b_out, norm1_gain, norm1_bias, b_down, norm2_gain, norm2_bias, b_out, b_out])
-    layer_out, grad_residual, g01, g2, keep, give = ffn(c01, c2, tokens, cotangent, vecs, (near, next_to, far))
-
-    got = swap(give, 2, 4, n_dp)
+    layer_out, grad_residual, g01, g2, keep, nearer, give, keep_tail, give_tail = ffn(
+        c01, c2, tokens, cotangent, vecs, near, along, across
+    )
+
+    got, got_nearer, got_tail = swap(give, 4, 2, n_dp), swap(nearer, 2, 4, n_dp), swap(give_tail, 2, 4, n_dp)
     g01, g2 = regroup(g01, g2)
+    g01, keep, got, got_nearer, keep_tail, got_tail = tie(g01, keep, got, got_nearer, keep_tail, got_tail)
+    keep = total(keep, got_nearer)
+    keep_tail, give_tail = total(keep_tail[0], got_tail[0]), total(keep_tail[1], got_tail[1])
+    got_tail = swap(give_tail, 4, 2, n_dp)
     d0 = attend_back(0, order, g01, ts01, probs01)
-    d0, keep, got = tie(d0, keep, got)
-    keep, give = total(keep[0], got[0]), total(keep[1], got[1])
-    got = swap(give, 4, 2, n_dp)
-    d1 = attend_back(1, order, g01, ts01, probs01)
-    d1, keep, got = tie(d1, keep, got)
-    sums = total(keep, got)
+    d0, order, keep, got, keep_tail, got_tail = tie(d0, order, keep, got, keep_tail, got_tail)
+    sums = jnp.concatenate([total(keep, got), total(keep_tail, got_tail)], axis=1)
     for bit in range(3, n_dp.bit_length() - 1):
         sums = total(sums, swap(sums, 1 << bit, 1 << bit, n_dp))
     parts = [pick(sums, mp, 0)]
     for i in (1, 2, 3):
         parts.append(lax.ppermute(pick(sums, (mp + i) % 4, 0), "mp", ring(i)))
+    d1 = attend_back(1, order, g01, ts01, probs01)
     d2 = attend_back(2, order, g2, ts2, probs2)
     d2, *parts = tie(d2, *parts)
     mine = sum(p.astype(F32) for p in parts).astype(BF16)
     grad_tokens, *sums = settle(d0, d1, d2, xs, w_heads, grad_residual, mine)
-    hq, hk, hv, g_up, g_down, g_out, small, spare = (s.astype(F32) for s in sums)
+    hq, hk, hv, g_up, g_down, g_out, units, spare, vectors = (s.astype(F32) for s in sums)
     for bit in range(3, n_dp.bit_length() - 1):
         hq, hk, hv, spare = (s + swap(s, 1 << bit, 1 << bit, n_dp) for s in (hq, hk, hv, spare))
     sums_of = lambda where: jnp.concatenate([spare[h, 0, where[h] : where[h] + HD] for h in range(3)])
-    vec = lambda i: small[i]
+    g_b_up = lax.dynamic_slice(units.reshape(8, 16, WIDTH)[:, 0], (0, 96 * mp), (8, 96)).reshape(WIDTH)
     return (
         layer_out,
         grad_tokens,
@@ -1134,15 +1170,15 @@
         hv.T,
         sums_of((0, HD, 0)),
         g_out,
-        vec(5),
-        vec(1),
-        vec(2),
-        g_up,
-        vec(0),
+        vectors[4],
+        vectors[0],
+        vectors[1],
+        g_up.T,
+        g_b_up,
         g_down,
-        vec(6),
-        vec(3),
-        vec(4),
+        vectors[5],
+        vectors[2],
+        vectors[3],
     )
 
 

time: 431 us -> 414 us (0.961)
  waiting for transfers between devices: 29.8 us -> 8.72 us
  other arithmetic: 19.8 us -> 15 us
  local copies, waits for them, and re-layouts: 8.65 us -> 13.4 us
    ppermute x3, waiting for transfers between devices: 14.8 us -> 1.29 us  [body(): parts.append(lax.ppermute(pick(sums, (mp + i) % 4, 0), 'mp', ring(i)))]
    ppermute x4 -> x6, waiting for transfers between devices: 9.26 us -> 0.02 us  [swap(): lax.ppermute(value, 'dp', [(d, d ^ (odd_bits if d % 2 else even_bits)) fo...]
  transfers between devices with their start and end apart: 10 -> 12, of which waited for: 5 -> 2; matrix products, arithmetic and copies ran while one was open for 0% -> 0% of each run, Pallas kernels for 34% -> 35%
where the time goes in v3:
time: 414 us; the launch traced here: 408 us
  Pallas kernels  350 us (85%)
  starting transfers between devices  19.4 us (5%)
  other arithmetic  15 us (4%)
  local copies, waits for them, and re-layouts  13.4 us (3%)
  waiting for transfers between devices  8.72 us (2%)
    pallas_call x1, Pallas kernels, settle(): pl.pallas_call(settle_kernel, out_shape=[sds((ROWS, WIDTH), BF16)] + [sds...  73.3 us
    pallas_call x1, Pallas kernels, ffn(): pl.pallas_call(ffn_kernel, out_shape=[sds((1024, WIDTH), BF16), sds((1024...  69.2 us
    pallas_call x1, Pallas kernels, collect(): pl.pallas_call(collect_kernel, out_shape=[sds((4 * ROWS, WIDTH), BF16), s...  63.2 us
    pallas_call x3, Pallas kernels, attend_back(): pl.pallas_call(functools.partial(attend_back_kernel, head), grid=(steps,)...  38.4 us
    pallas_call x2, Pallas kernels, attend(): pl.pallas_call(functools.partial(attend_kernel, first), grid=(heads, step...  36.5 us
    pallas_call x1, Pallas kernels, spread(): pl.pallas_call(spread_kernel, out_shape=[jax.ShapeDtypeStruct((4, 1024, C...  35.2 us
    pallas_call x1, Pallas kernels, regroup(): pl.pallas_call(regroup_kernel, out_shape=[jax.ShapeDtypeStruct((4096, C),...  33.8 us
  transfers between devices with their start and end apart: 12, of which 2 were waited for; matrix products, arithmetic and copies ran while one was open for 0% of the time, Pallas kernels for 35%

profile of v3, /device:TPU:10, one launch (start us, length us, event | category | flops | bytes accessed | tf_op | source)
XLA Modules:
  0.0 407.5 jit_solution(13456350000689112345)
XLA Ops:
  0.7 1.2 constant_dynamic-slice_fusion.2
  2.0 0.9 constant_dynamic-slice_fusion.1
  4.7 1.5 fusion.10
  7.2 63.2 %collect.1 = (bf16[4096,768]{1,0:T(8,128)(2,1)}, bf16[3,4096,256]{2,1,0:T(8,128)(2,1)}, bf16[768,768]{1,0:T(8,128)(2,1)}, s32[12288]{0:T(1024)}, s32[1,4096]{1,0:T(1,128)}) custom-call(bf16[1024,768]{1,0:T(8,128)(2,1)} %tok_ref.1, bf16[192,768]{1,0:T(8,128)(2,1)} %bitcast.52, bf16[192,768]{1,0:T(8,128)(2,1)} %bitcast.53, bf16[192,768]{1,0:T(8,128)(2,1)} %bitcast.54, ...), custom_call_target="tpu_custom_call" | custom-call | tf_op jit(solution)/shard_map/collect/pallas_call | solution.py:431
  70.5 7.3 %collective-permute-start.1 = (bf16[240,768]{1,0:T(8,128)(2,1)S(1)}, bf16[240,768]{1,0:T(8,128)(2,1)S(1)}, u32[]{:S(2)}, u32[]{:S(2)}) collective-permute-start(bf16[240,768]{1,0:T(8,128)(2,1)S(1)} %pad_maximum_fusion.1), channel_id=1, source_target_pairs={{0,2},{1,3},{2,0},{3,1},{4,6},{5,7},{6,4},{7,5},{8,10},{9,11},{10,... | collective-permute-start | bytes 1105928 | tf_op jit(solution)/shard_map/ppermute | solution.py:1127
  78.3 23.5 %attend.2 = (bf16[4096,128]{1,0:T(8,128)(2,1)}, bf16[2,4096,256]{2,1,0:T(8,128)(2,1)}, f32[2,4096,128]{2,1,0:T(8,128)}) custom-call(s32[12288]{0:T(1024)} %get-tuple-element.107.ord_ref, s32[1,4096]{1,0:T(1,128)} %get-tuple-element.76.mask_ref, bf16[3,4096,256]{2,1,0:T(8,128)(2,1)} %get-tuple-element.78.qkv_ref), custom_call_target="tpu_custom_call" | custom-call | flops 17999998976 | bytes 10485760 | tf_op jit(solution)/shard_map/attend/pallas_call | solution.py:97
  101.8 7.4 %collective-permute-done.2 = bf16[240,768]{1,0:T(8,128)(2,1)S(1)} collective-permute-done((bf16[240,768]{1,0:T(8,128)(2,1)S(1)}, bf16[240,768]{1,0:T(8,128)(2,1)S(1)}, u32[]{:S(2)}, u32[]{:S(2)}) %collective-permute-start.2) | collective-permute-done | bytes 368672 | tf_op jit(solution)/shard_map/ppermute | solution.py:1127
  109.4 1.5 collective-permute-start.3
  112.3 12.9 %attend.3 = (bf16[2048,128]{1,0:T(8,128)(2,1)}, bf16[1,4096,256]{2,1,0:T(8,128)(2,1)}, f32[1,4096,128]{2,1,0:T(8,128)}) custom-call(s32[12288]{0:T(1024)} %get-tuple-element.107.ord_ref, s32[1,4096]{1,0:T(1,128)} %get-tuple-element.76.mask_ref, bf16[3,4096,256]{2,1,0:T(8,128)(2,1)} %get-tuple-element.78.qkv_ref), custom_call_target="tpu_custom_call" | custom-call | flops 8999999488 | bytes 10485760 | tf_op jit(solution)/shard_map/attend/pallas_call | solution.py:97
  125.2 35.2 %spread.1 = (bf16[4,1024,128]{2,1,0:T(8,128)(2,1)}, bf16[4,512,128]{2,1,0:T(8,128)(2,1)}) custom-call(bf16[4096,128]{1,0:T(8,128)(2,1)} %get-tuple-element.81.a_ref, bf16[2048,128]{1,0:T(8,128)(2,1)} %get-tuple-element.82.b_ref), custom_call_target="tpu_custom_call" | custom-call | tf_op jit(solution)/shard_map/spread/pallas_call | solution.py:503
  160.5 1.1 copy-done.5
  161.6 69.2 %ffn.1 = (bf16[1024,768]{1,0:T(8,128)(2,1)}, f32[1024,768]{1,0:T(8,128)}, bf16[4,1024,128]{2,1,0:T(8,128)(2,1)}, bf16[4,512,128]{2,1,0:T(8,128)(2,1)}, bf16[4,19...) custom-call(bf16[4,1024,128]{2,1,0:T(8,128)(2,1)} %get-tuple-element, ...), custom_call_target="tpu_custom_call" | custom-call | tf_op jit(solution)/shard_map/ffn/pallas_call | solution.py:1076
  230.8 1.2 collective-permute-start.5
  232.6 1.5 collective-permute-start.7
  234.0 33.8 %regroup.1 = (bf16[4096,128]{1,0:T(8,128)(2,1)}, bf16[2048,128]{1,0:T(8,128)(2,1)}) custom-call(bf16[4,1024,128]{2,1,0:T(8,128)(2,1)} %get-tuple-element.90.a_ref, bf16[4,512,128]{2,1,0:T(8,128)(2,1)} %get-tuple-element.91.b_ref), custom_call_target="tpu_custom_call" | custom-call | tf_op jit(solution)/shard_map/regroup/pallas_call | solution.py:547
  267.9 1.2 fusion.9
  269.0 0.9 collective-permute-start.8
  270.0 12.8 %attend_back.3.d0_ref = bf16[4096,256]{1,0:T(8,128)(2,1)} custom-call(s32[12288]{0:T(1024)} %get-tuple-element.107.ord_ref, bf16[4096,128]{1,0:T(8,128)(2,1)} %get-tuple-element.98.g_ref, bf16[2,4096,256]{2,1,0:T(8,128)(2,1)} %get-tuple-element.99.ts_ref, f32[2,4096,128]{2,1,0:T(8,128)} %get-tuple-element.100.pr_ref), custom_call_target="tpu_custom_call" | custom-call | flops 8999999488 | bytes 10485760 | tf_op jit(solution)/shard_map/attend_back/pallas_call | solution.py:170
  283.1 1.0 add_convert_fusion.3
  284.6 1.4 collective-permute-start.10
  286.0 3.9 collective-permute-start.11
  289.9 12.8 %attend_back.4.d1_ref = bf16[4096,256]{1,0:T(8,128)(2,1)} custom-call(s32[12288]{0:T(1024)} %get-tuple-element.107.ord_ref, bf16[4096,128]{1,0:T(8,128)(2,1)} %get-tuple-element.98.g_ref, bf16[2,4096,256]{2,1,0:T(8,128)(2,1)} %get-tuple-element.99.ts_ref, f32[2,4096,128]{2,1,0:T(8,128)} %get-tuple-element.100.pr_ref), custom_call_target="tpu_custom_call" | custom-call | flops 8999999488 | bytes 10485760 | tf_op jit(solution)/shard_map/attend_back/pallas_call | solution.py:170
  302.7 12.8 %attend_back.5.d2_ref = bf16[4096,256]{1,0:T(8,128)(2,1)} custom-call(s32[12288]{0:T(1024)} %get-tuple-element.107.ord_ref, bf16[2048,128]{1,0:T(8,128)(2,1)} %get-tuple-element.108.g_ref, bf16[1,4096,256]{2,1,0:T(8,128)(2,1)} %get-tuple-element.109.ts_ref, f32[1,4096,128]{2,1,0:T(8,128)} %get-tuple-element.110.pr_ref), custom_call_target="tpu_custom_call" | custom-call | flops 8999999488 | bytes 10485760 | tf_op jit(solution)/shard_map/attend_back/pallas_call | solution.py:170
  315.5 1.3 collective-permute-done.11
  316.8 0.9 add_convert_fusion.2.mine_ref
  317.7 73.3 %settle.1 = (bf16[1024,768]{1,0:T(8,128)(2,1)}, bf16[192,768]{1,0:T(8,128)(2,1)}, bf16[192,768]{1,0:T(8,128)(2,1)}, bf16[192,768]{1,0:T(8,128)(2,1)}, bf16[768,7...) custom-call(bf16[4096,256]{1,0:T(8,128)(2,1)} %attend_back.3.d0_ref,, ...), custom_call_target="tpu_custom_call" | custom-call | tf_op jit(solution)/shard_map/settle/pallas_call | solution.py:790
  391.0 1.4 convert_bitcast_fusion
  392.4 2.0 copy.37
  395.4 1.6 convert_element_type.112
  401.0 0.9 slice.111
  404.0 1.1 copy.42
  406.0 1.1 copy.43
  (89 shorter events, 14.1 us)
Async XLA Ops:
  0.7 3.0 copy-start
  70.4 31.4 %collective-permute-start = (bf16[240,768]{1,0:T(8,128)(2,1)S(1)}, bf16[240,768]{1,0:T(8,128)(2,1)S(1)}, u32[]{:S(2)}, u32[]{:S(2)}) collective-permute-start(bf16[240,768]{1,0:T(8,128)(2,1)S(1)} %pad_maximum_fusion.1), channel_id=1, source_target_pairs={{0,1},{1,2},{2,3},{3,0},{4,5},{5,6},{6,7},{7,4},{8,9},{9,10},{10,1... | collective-permute-start | bytes 1105928 | tf_op jit(solution)/shard_map/ppermute | solution.py:1127
  70.5 31.3 %collective-permute-start.1 = (bf16[240,768]{1,0:T(8,128)(2,1)S(1)}, bf16[240,768]{1,0:T(8,128)(2,1)S(1)}, u32[]{:S(2)}, u32[]{:S(2)}) collective-permute-start(bf16[240,768]{1,0:T(8,128)(2,1)S(1)} %pad_maximum_fusion.1), channel_id=1, source_target_pairs={{0,2},{1,3},{2,0},{3,1},{4,6},{5,7},{6,4},{7,5},{8,10},{9,11},{10,... | collective-permute-start | bytes 1105928 | tf_op jit(solution)/shard_map/ppermute | solution.py:1127
  77.8 31.4 %collective-permute-start.2 = (bf16[240,768]{1,0:T(8,128)(2,1)S(1)}, bf16[240,768]{1,0:T(8,128)(2,1)S(1)}, u32[]{:S(2)}, u32[]{:S(2)}) collective-permute-start(bf16[240,768]{1,0:T(8,128)(2,1)S(1)} %pad_maximum_fusion.1), channel_id=1, source_target_pairs={{0,3},{1,0},{2,1},{3,2},{4,7},{5,4},{6,5},{7,6},{8,11},{9,8},{10,9... | collective-permute-start | bytes 1105928 | tf_op jit(solution)/shard_map/ppermute | solution.py:1127
  109.2 2.3 copy-start.14
  109.2 2.3 copy-start.15
  109.2 2.4 copy-start.16
  109.2 2.4 copy-start.17
  109.2 2.4 copy-start.18
  109.2 2.4 copy-start.19
  109.4 15.8 %copy-start.2 = (bf16[4,240,768]{2,1,0:T(8,128)(2,1)}, bf16[4,240,768]{2,1,0:T(8,128)(2,1)S(1)}, u32[]{:S(2)}) copy-start(bf16[4,240,768]{2,1,0:T(8,128)(2,1)S(1)} %pad_maximum_fusion.near_ref) | copy-start | bytes 4423684
  109.4 51.0 %collective-permute-start.3 = (bf16[4,240,768]{2,1,0:T(8,128)(2,1)S(1)}, bf16[4,240,768]{2,1,0:T(8,128)(2,1)S(1)}, u32[]{:S(2)}, u32[]{:S(2)}) collective-permute-start(bf16[4,240,768]{2,1,0:T(8,128)(2,1)S(1)} %pad_maximum_fusion.near_ref), channel_id=1, source_target_pairs={{0,8},{4,20},{8,0},{12,28},{16,24},{20,4},{24,16},{28,12},{1,9},{5... | collective-permute-start | bytes 4423688 | tf_op jit(solution)/shard_map/ppermute | solution.py:1092
  111.0 49.5 %collective-permute-start.4 = (bf16[4,240,768]{2,1,0:T(8,128)(2,1)S(1)}, bf16[4,240,768]{2,1,0:T(8,128)(2,1)}, u32[]{:S(2)}, u32[]{:S(2)}) collective-permute-start(bf16[4,240,768]{2,1,0:T(8,128)(2,1)S(1)} %pad_maximum_fusion.near_ref), channel_id=1, source_target_pairs={{0,16},{4,12},{8,24},{12,4},{16,0},{20,28},{24,8},{28,20},{1,17},{... | collective-permute-start | bytes 4423688 | tf_op jit(solution)/shard_map/ppermute | solution.py:1092
  160.4 1.1 copy-start.5
  230.8 37.1 %copy-start.8 = (bf16[2,4,48,768]{3,2,1,0:T(8,128)(2,1)S(1)}, bf16[2,4,48,768]{3,2,1,0:T(8,128)(2,1)}, u32[]{:S(2)}) copy-start(bf16[2,4,48,768]{3,2,1,0:T(8,128)(2,1)} %get-tuple-element.104) | copy-start | bytes 1769476
  230.8 37.1 %collective-permute-start.5 = (bf16[4,192,768]{2,1,0:T(8,128)(2,1)}, bf16[4,192,768]{2,1,0:T(8,128)(2,1)S(1)}, u32[]{:S(2)}, u32[]{:S(2)}) collective-permute-start(bf16[4,192,768]{2,1,0:T(8,128)(2,1)} %get-tuple-element.94), channel_id=1, source_target_pairs={{0,16},{4,12},{8,24},{12,4},{16,0},{20,28},{24,8},{28,20},{1,17},{... | collective-permute-start | bytes 3538952 | tf_op jit(solution)/shard_map/ppermute | solution.py:1092
  232.0 35.8 %collective-permute-start.6 = (bf16[4,192,768]{2,1,0:T(8,128)(2,1)}, bf16[4,192,768]{2,1,0:T(8,128)(2,1)S(1)}, u32[]{:S(2)}, u32[]{:S(2)}) collective-permute-start(bf16[4,192,768]{2,1,0:T(8,128)(2,1)} %get-tuple-element.95), channel_id=1, source_target_pairs={{0,8},{4,20},{8,0},{12,28},{16,24},{20,4},{24,16},{28,12},{1,9},{5... | collective-permute-start | bytes 3538952 | tf_op jit(solution)/shard_map/ppermute | solution.py:1092
  232.6 35.3 %collective-permute-start.7 = (bf16[2,4,48,768]{3,2,1,0:T(8,128)(2,1)}, bf16[2,4,48,768]{3,2,1,0:T(8,128)(2,1)}, u32[]{:S(2)}, u32[]{:S(2)}) collective-permute-start(bf16[2,4,48,768]{3,2,1,0:T(8,128)(2,1)} %get-tuple-element.97), channel_id=1, source_target_pairs={{0,8},{4,20},{8,0},{12,28},{16,24},{20,4},{24,16},{28,12},{1,9},{5... | collective-permute-start | bytes 1769480 | tf_op jit(solution)/shard_map/ppermute | solution.py:1092
  269.0 14.1 %collective-permute-start.8 = (bf16[4,48,768]{2,1,0:T(8,128)(2,1)S(1)}, bf16[4,48,768]{2,1,0:T(8,128)(2,1)}, u32[]{:S(2)}, u32[]{:S(2)}) collective-permute-start(bf16[4,48,768]{2,1,0:T(8,128)(2,1)S(1)} %get-tuple-element.160), channel_id=1, source_target_pairs={{0,16},{4,12},{8,24},{12,4},{16,0},{20,28},{24,8},{28,20},{1,17},{... | collective-permute-start | bytes 884744 | tf_op jit(solution)/shard_map/ppermute | solution.py:1092
  270.0 12.8 %copy-start.6 = (bf16[4,192,768]{2,1,0:T(8,128)(2,1)S(1)}, bf16[4,192,768]{2,1,0:T(8,128)(2,1)}, u32[]{:S(2)}) copy-start(bf16[4,192,768]{2,1,0:T(8,128)(2,1)} %get-tuple-element.101) | copy-start | bytes 3538948
  284.6 30.9 %collective-permute-start.10 = (bf16[240,768]{1,0:T(8,128)(2,1)S(1)}, bf16[240,768]{1,0:T(8,128)(2,1)S(1)}, u32[]{:S(2)}, u32[]{:S(2)}) collective-permute-start(bf16[240,768]{1,0:T(8,128)(2,1)S(1)} %get-tuple-element.159), channel_id=1, source_target_pairs={{0,2},{1,3},{2,0},{3,1},{4,6},{5,7},{6,4},{7,5},{8,10},{9,11},{10,... | collective-permute-start | bytes 1105928 | tf_op jit(solution)/shard_map/ppermute | solution.py:1153
  286.0 30.8 %collective-permute-start.11 = (bf16[240,768]{1,0:T(8,128)(2,1)S(1)}, bf16[240,768]{1,0:T(8,128)(2,1)S(1)}, u32[]{:S(2)}, u32[]{:S(2)}) collective-permute-start(bf16[240,768]{1,0:T(8,128)(2,1)S(1)} %get-tuple-element.156), channel_id=1, source_target_pairs={{0,3},{1,0},{2,1},{3,2},{4,7},{5,4},{6,5},{7,6},{8,11},{9,8},{10,9... | collective-permute-start | bytes 1105928 | tf_op jit(solution)/shard_map/ppermute | solution.py:1153
  289.9 26.9 %collective-permute-start.9 = (bf16[240,768]{1,0:T(8,128)(2,1)S(1)}, bf16[240,768]{1,0:T(8,128)(2,1)S(1)}, u32[]{:S(2)}, u32[]{:S(2)}) collective-permute-start(bf16[240,768]{1,0:T(8,128)(2,1)S(1)} %get-tuple-element.158), channel_id=1, source_target_pairs={{0,1},{1,2},{2,3},{3,0},{4,5},{5,6},{6,7},{7,4},{8,9},{9,10},{10,1... | collective-permute-start | bytes 1105928 | tf_op jit(solution)/shard_map/ppermute | solution.py:1153
  392.4 2.9 copy-start.7
  395.3 1.6 copy-start.12
  395.3 2.4 copy-start.11
  396.9 1.7 copy-start.10
  396.9 2.6 copy-start.9
  397.8 2.6 copy-start.13
  397.8 6.2 %copy-start.3 = (bf16[1024,768]{1,0:T(8,128)(2,1)S(1)}, bf16[1024,768]{1,0:T(8,128)(2,1)}, u32[]{:S(2)}) copy-start(bf16[1024,768]{1,0:T(8,128)(2,1)} %get-tuple-element.197) | copy-start | bytes 4718596
  404.0 2.0 copy-start.4
  404.0 3.1 copy-start.1

commit v4 on v3

--- a/solution.py
+++ b/solution.py
@@ -12,6 +12,7 @@
 GROUP = 2
 STEP = 1024
 GROUPS = STEP // (GROUP * C)
+HALVES = 2
 F32 = jnp.float32
 BF16 = jnp.bfloat16
 VMEM = pltpu.VMEM
@@ -32,7 +33,27 @@
     scatter(GROUPS - 1, outs[(GROUPS - 1) % 2])
 
 
-def attend_kernel(first, ord_ref, mask_ref, qkv_ref, c_ref, ts_ref, pr_ref, src, ctx, *slots):
+def each_window(ord_ref, windows, sems, first, step, steps, work):
+    def fetch(n, at_step):
+        start = pl.multiple_of((first + at_step * HALVES + n) * STEP, STEP)
+        return pltpu.make_async_copy(ord_ref.at[pl.ds(start, STEP)], windows[n], sems.at[n])
+
+    @pl.when(step == 0)
+    def _():
+        for n in range(HALVES):
+            fetch(n, step).start()
+
+    for n in range(HALVES):
+        fetch(n, step).wait()
+        work(n, windows[n])
+
+        @pl.when(step + 1 < steps)
+        def _():
+            fetch(n, step + 1).start()
+
+
+def attend_kernel(first, ord_ref, mask_ref, qkv_ref, c_ref, ts_ref, pr_ref, src, ctx, *rest):
+    slots, windows, sems = rest[:4], rest[4 : 4 + HALVES], rest[4 + HALVES]
     head, step = pl.program_id(0) + first, pl.program_id(1)
     live = jnp.sum(mask_ref[...].astype(F32), axis=1, keepdims=True).astype(jnp.int32)
 
@@ -41,34 +62,37 @@
         src[pl.ds(0, L, stride=2), :] = qkv_ref[0, :, :C].astype(F32)
         src[pl.ds(1, L, stride=2), :] = qkv_ref[0, :, C:].astype(F32)
 
-    def gather(group, buf):
-        for u in range(GROUP * C):
-            buf[pl.ds(2 * u, 2), :] = src[pl.ds(pl.multiple_of(ord_ref[group * GROUP * C + u], 2), 2), :]
-
-    def compute(group, buf, out):
-        each = range(GROUP)
-        rows = [pl.ds((group * GROUP + i) * C, C) for i in each]
-        t0 = [buf[pl.ds(2 * i * C, C, stride=2), :].astype(BF16) for i in each]
-        t1 = [buf[pl.ds(2 * i * C + 1, C, stride=2), :].astype(BF16) for i in each]
-        for i in each:
-            ts_ref[0, rows[i], :C] = t0[i]
-            ts_ref[0, rows[i], C:] = t1[i]
-        slot = [step * STEP + (group * GROUP + i) * C + lax.broadcasted_iota(jnp.int32, (C, C), 0) for i in each]
-        scores = [dot(t1[i], t0[i], 1, 1) * 0.125 + jnp.where(slot[i] < live, 0.0, -10000.0) for i in each]
-        e = [jnp.exp(scores[i] - jnp.max(scores[i], axis=0, keepdims=True)) for i in each]
-        probs = [e[i] * (1.0 / jnp.sum(e[i], axis=0, keepdims=True)) for i in each]
-        for i in each:
-            pr_ref[0, rows[i], :] = probs[i]
-        for i in each:
-            out[pl.ds(i * C, C), :] = dot(probs[i].astype(BF16), t0[i], 0, 0)
-
-    def scatter(group, out):
-        for u in range(GROUP * C):
-            ctx[pl.ds(ord_ref[group * GROUP * C + u], 1), :] = out[pl.ds(u, 1), :]
-
-    in_turn(gather, compute, scatter, slots[:2], slots[2:])
-
-    @pl.when(step == L // STEP - 1)
+    def work(n, window):
+        def gather(group, buf):
+            for u in range(GROUP * C):
+                buf[pl.ds(2 * u, 2), :] = src[pl.ds(pl.multiple_of(window[group * GROUP * C + u], 2), 2), :]
+
+        def compute(group, buf, out):
+            each = range(GROUP)
+            rows = [pl.ds(n * STEP + (group * GROUP + i) * C, C) for i in each]
+            t0 = [buf[pl.ds(2 * i * C, C, stride=2), :].astype(BF16) for i in each]
+            t1 = [buf[pl.ds(2 * i * C + 1, C, stride=2), :].astype(BF16) for i in each]
+            for i in each:
+                ts_ref[0, rows[i], :C] = t0[i]
+                ts_ref[0, rows[i], C:] = t1[i]
+            slot = [(step * HALVES + n) * STEP + (group * GROUP + i) * C + lax.broadcasted_iota(jnp.int32, (C, C), 0) for i in each]
+            scores = [dot(t1[i], t0[i], 1, 1) * 0.125 + jnp.where(slot[i] < live, 0.0, -10000.0) for i in each]
+            e = [jnp.exp(scores[i] - jnp.max(scores[i], axis=0, keepdims=True)) for i in each]
+            probs = [e[i] * (1.0 / jnp.sum(e[i], axis=0, keepdims=True)) for i in each]
+            for i in each:
+                pr_ref[0, rows[i], :] = probs[i]
+            for i in each:
+                out[pl.ds(i * C, C), :] = dot(probs[i].astype(BF16), t0[i], 0, 0)
+
+        def scatter(group, out):
+            for u in range(GROUP * C):
+                ctx[pl.ds(window[group * GROUP * C + u], 1), :] = out[pl.ds(u, 1), :]
+
+        in_turn(gather, compute, scatter, slots[:2], slots[2:])
+
+    each_window(ord_ref, windows, sems, head * (L // STEP), step, L // STEP // HALVES, work)
+
+    @pl.when(step == L // STEP // HALVES - 1)
     def _():
         lane = lax.broadcasted_iota(jnp.int32, (1, C), 1)
         if first == 2:
@@ -91,14 +115,13 @@
 def attend(first, order, mask, qkv):
     heads = 2 if first == 0 else 1
     whole = lambda shape: pl.BlockSpec(shape, lambda h, i: (0,) * len(shape), pipeline_mode=pl.Buffered(1))
-    per_step = lambda width: pl.BlockSpec((1, STEP, width), lambda h, i: (h, i, 0))
-    steps = L // STEP
+    per_step = lambda width: pl.BlockSpec((1, HALVES * STEP, width), lambda h, i: (h, i, 0))
     out_rows = L if first == 0 else L // 2
     return pl.pallas_call(
         functools.partial(attend_kernel, first),
-        grid=(heads, steps),
+        grid=(heads, L // STEP // HALVES),
         in_specs=[
-            pl.BlockSpec((STEP,), lambda h, i: ((h + first) * steps + i,), memory_space=pltpu.SMEM),
+            pl.BlockSpec(memory_space=pl.ANY),
             whole((1, L)),
             pl.BlockSpec((1, L, 2 * C), lambda h, i: (h + first, 0, 0)),
         ],
@@ -109,14 +132,16 @@
             jax.ShapeDtypeStruct((heads, L, C), F32),
         ],
         scratch_shapes=[VMEM((2 * L, C), F32), VMEM((2 * L, C), F32)]
-        + [VMEM((2 * GROUP * C, C), F32)] * 2 + [VMEM((GROUP * C, C), F32)] * 2,
+        + [VMEM((2 * GROUP * C, C), F32)] * 2 + [VMEM((GROUP * C, C), F32)] * 2
+        + [pltpu.SMEM((STEP,), jnp.int32)] * HALVES + [pltpu.SemaphoreType.DMA((HALVES,))],
         compiler_params=pltpu.CompilerParams(vmem_limit_bytes=60 << 20),
         cost_estimate=pl.CostEstimate(flops=heads * 9 * 10**9, bytes_accessed=10 << 20, transcendentals=0),
         name="attend",
     )(order, mask, qkv)
 
 
-def attend_back_kernel(head, ord_ref, g_ref, ts_ref, pr_ref, d_ref, gsrc, dst, *slots):
+def attend_back_kernel(head, ord_ref, g_ref, ts_ref, pr_ref, d_ref, gsrc, dst, *rest):
+    slots, windows, sems = rest[:4], rest[4 : 4 + HALVES], rest[4 + HALVES]
     step = pl.program_id(0)
     lane = lax.broadcasted_iota(jnp.int32, (1, C), 1)
 
@@ -132,52 +157,55 @@
 
     keep = (lane >= HD) if head == 1 else (lane < HD)
 
-    def gather(group, buf):
-        for u in range(GROUP * C):
-            buf[pl.ds(u, 1), :] = gsrc[pl.ds(ord_ref[group * GROUP * C + u], 1), :]
-
-    def compute(group, buf, out):
-        each = range(GROUP)
-        rows = [pl.ds((group * GROUP + i) * C, C) for i in each]
-        t0 = [ts_ref[0, rows[i], :C] for i in each]
-        t1 = [ts_ref[0, rows[i], C:] for i in each]
-        probs = [pr_ref[0, rows[i], :] for i in each]
-        g = [jnp.where(keep, buf[pl.ds(i * C, C), :], 0.0).astype(BF16) for i in each]
-        dp = [dot(t0[i], g[i], 1, 1) for i in each]
-        ds = [(probs[i] * (dp[i] - jnp.sum(probs[i] * dp[i], axis=0, keepdims=True))).astype(BF16) for i in each]
-        for i in each:
-            grad = dot(ds[i], t1[i], 0, 0) * 0.125 + jnp.dot(probs[i].astype(BF16), g[i], preferred_element_type=F32)
-            out[pl.ds(2 * i * C, C, stride=2), :] = grad
-        for i in each:
-            out[pl.ds(2 * i * C + 1, C, stride=2), :] = jnp.dot(ds[i], t0[i], preferred_element_type=F32) * 0.125
-
-    def scatter(group, out):
-        for u in range(GROUP * C):
-            dst[pl.ds(pl.multiple_of(ord_ref[group * GROUP * C + u], 2), 2), :] = out[pl.ds(2 * u, 2), :]
-
-    in_turn(gather, compute, scatter, slots[:2], slots[2:])
-
-    @pl.when(step == L // STEP - 1)
+    def work(n, window):
+        def gather(group, buf):
+            for u in range(GROUP * C):
+                buf[pl.ds(u, 1), :] = gsrc[pl.ds(window[group * GROUP * C + u], 1), :]
+
+        def compute(group, buf, out):
+            each = range(GROUP)
+            rows = [pl.ds(n * STEP + (group * GROUP + i) * C, C) for i in each]
+            t0 = [ts_ref[0, rows[i], :C] for i in each]
+            t1 = [ts_ref[0, rows[i], C:] for i in each]
+            probs = [pr_ref[0, rows[i], :] for i in each]
+            g = [jnp.where(keep, buf[pl.ds(i * C, C), :], 0.0).astype(BF16) for i in each]
+            dp = [dot(t0[i], g[i], 1, 1) for i in each]
+            ds = [(probs[i] * (dp[i] - jnp.sum(probs[i] * dp[i], axis=0, keepdims=True))).astype(BF16) for i in each]
+            for i in each:
+                grad = dot(ds[i], t1[i], 0, 0) * 0.125 + jnp.dot(probs[i].astype(BF16), g[i], preferred_element_type=F32)
+                out[pl.ds(2 * i * C, C, stride=2), :] = grad
+            for i in each:
+                out[pl.ds(2 * i * C + 1, C, stride=2), :] = jnp.dot(ds[i], t0[i], preferred_element_type=F32) * 0.125
+
+        def scatter(group, out):
+            for u in range(GROUP * C):
+                dst[pl.ds(pl.multiple_of(window[group * GROUP * C + u], 2), 2), :] = out[pl.ds(2 * u, 2), :]
+
+        in_turn(gather, compute, scatter, slots[:2], slots[2:])
+
+    each_window(ord_ref, windows, sems, head * (L // STEP), step, L // STEP // HALVES, work)
+
+    @pl.when(step == L // STEP // HALVES - 1)
     def _():
         d_ref[:, :C] = dst[pl.ds(0, L, stride=2), :].astype(BF16)
         d_ref[:, C:] = dst[pl.ds(1, L, stride=2), :].astype(BF16)
 
 
 def attend_back(head, order, g, ts, probs):
-    steps = L // STEP
     whole = lambda shape: pl.BlockSpec(shape, lambda i: (0,) * len(shape), pipeline_mode=pl.Buffered(1))
-    per_step = lambda width: pl.BlockSpec((1, STEP, width), lambda i: (head % 2, i, 0))
+    per_step = lambda width: pl.BlockSpec((1, HALVES * STEP, width), lambda i: (head % 2, i, 0))
     return pl.pallas_call(
         functools.partial(attend_back_kernel, head),
-        grid=(steps,),
+        grid=(L // STEP // HALVES,),
         in_specs=[
-            pl.BlockSpec((STEP,), lambda i: (head * steps + i,), memory_space=pltpu.SMEM),
+            pl.BlockSpec(memory_space=pl.ANY),
             whole(g.shape), per_step(2 * C), per_step(C),
         ],
         out_specs=whole((L, 2 * C)),
         out_shape=jax.ShapeDtypeStruct((L, 2 * C), BF16),
         scratch_shapes=[VMEM((2 * L, C), F32), VMEM((2 * L, C), F32)]
-        + [VMEM((GROUP * C, C), F32)] * 2 + [VMEM((2 * GROUP * C, C), F32)] * 2,
+        + [VMEM((GROUP * C, C), F32)] * 2 + [VMEM((2 * GROUP * C, C), F32)] * 2
+        + [pltpu.SMEM((STEP,), jnp.int32)] * HALVES + [pltpu.SemaphoreType.DMA((HALVES,))],
         compiler_params=pltpu.CompilerParams(vmem_limit_bytes=60 << 20),
         cost_estimate=pl.CostEstimate(flops=9 * 10**9, bytes_accessed=10 << 20, transcendentals=0),
         name="attend_back",
@@ -250,11 +278,11 @@
     return at(dp_base + half, jnp.where(half == 0, u, 3 - u))
 
 
-def collect_kernel(x_ref, wq_ref, wk_ref, wv_ref, bsrc_ref, osrc_ref, msrc_ref,
-                   xs_ref, qkv_ref, w_ref, ord_ref, mask_ref,
-                   xs, qkv, w, wsrc, bias, relay,
+def collect_kernel(x_ref, wq_ref, wk_ref, wv_ref, bsrc_ref, osrc_ref, msrc_ref, up_ref, down_ref, wout_ref, brow_ref,
+                   xs_ref, qkv_ref, w_ref, ord_ref, mask_ref, share_ref,
+                   xs, qkv, w, wsrc, bias, relay, up, up_t,
                    chain_recv, relay_recv, pair_recv, chain_send, relay_send, pair_send, own_sem,
-                   wz_recv, wz_send, wp_recv, wp_send, b_recv, b_send, o_recv, o_send, m_recv, m_send, xs_out, qkv_out, w_out, build_sem):
+                   wz_recv, wz_send, wp_recv, wp_send, b_recv, b_send, o_recv, o_send, m_recv, m_send, xs_out, qkv_out, w_out, build_sem, up_sem, share_sem):
     dp, mp, core, t = place()
     base, half, spot = dp - core, mp // 2, lax.rem(dp, 8) // 2
     step = 1 - 2 * core
@@ -283,11 +311,10 @@
                 copy = pltpu.make_async_copy(part.at[pl.ds(h * HD, HD)], wsrc.at[rows], build_sem.at[4 * h + n])
                 copy.start()
                 parts.append(copy)
+    greet(pltpu.get_barrier_semaphore(), False)
     for copy in parts:
         copy.wait()
 
-    greet(pltpu.get_barrier_semaphore(), False)
-
     for far in (0, 1):
         target = mp // 2 + 2 * far
 
@@ -325,6 +352,19 @@
     def _():
         for s in range(SUBS):
             send(x_ref.at[cut(s)], home(0, s), chain_send.at[0, s], chain_recv.at[0, s], upper)
+
+    number = lax.rem(dp, 8)
+    units = pl.ds(pl.multiple_of(96 * number, 32), 96)
+    out_rows = pl.ds(pl.multiple_of(32 * jnp.minimum(number, 5), 32), 32)
+    load = pltpu.make_async_copy(up_ref, up, up_sem)
+    load.start()
+    made = [
+        pltpu.make_async_copy(down_ref.at[units], share_ref.at[pl.ds(96, 96)], share_sem.at[0]),
+        pltpu.make_async_copy(brow_ref, share_ref.at[pl.ds(192, 16)], share_sem.at[1]),
+        pltpu.make_async_copy(wout_ref.at[out_rows], share_ref.at[pl.ds(SHARE, 32)], share_sem.at[2]),
+    ]
+    for copy in made:
+        copy.start()
 
     wait(w.at[quarter(spot)], wz_recv)
     for rel in (1, 2, 3):
@@ -382,6 +422,10 @@
     pltpu.make_async_copy(w, w_ref, w_out).start()
     for i, s in pieces[:3]:
         project(i, s)
+    load.wait()
+    up_t[...] = up[...].T
+    made.append(pltpu.make_async_copy(up_t.at[units], share_ref.at[pl.ds(0, 96)], share_sem.at[3]))
+    made[-1].start()
     for k in range(4, len(pieces)):
         receive(*pieces[k])
         project(*pieces[k - 1])
@@ -425,25 +469,27 @@
         wait(msrc_ref, m_send)
 
     wait(w, w_out)
-
-
-def collect(x, wq, wk, wv, b, order, mask):
+    for copy in made:
+        copy.wait()
+
+
+def collect(x, wq, wk, wv, b, order, mask, up, down, out, bias_row):
     return pl.pallas_call(
         collect_kernel,
         out_shape=[sds((4 * ROWS, WIDTH), BF16), sds((3, 4 * ROWS, 256), BF16), sds((WIDTH, WIDTH), BF16), sds((3 * L,), jnp.int32),
-                   sds((1, L), jnp.int32)],
-        in_specs=[ANY] * 7,
-        out_specs=[ANY] * 5,
+                   sds((1, L), jnp.int32), sds((SHARE_ALL, WIDTH), BF16)],
+        in_specs=[ANY] * 11,
+        out_specs=[ANY] * 6,
         scratch_shapes=[
             VMEM((4 * ROWS, WIDTH), BF16), VMEM((4 * ROWS, WIDTH), BF16), VMEM((WIDTH, WIDTH), BF16), VMEM((WIDTH, WIDTH), BF16),
-            VMEM((8, 256), F32), VMEM((ROWS, WIDTH), BF16),
+            VMEM((8, 256), F32), VMEM((ROWS, WIDTH), BF16), VMEM((WIDTH, WIDTH), BF16), VMEM((WIDTH, WIDTH), BF16),
             DMA((4, SUBS)), DMA((SUBS,)), DMA((4, SUBS)), DMA((3, SUBS)), DMA((SUBS,)), DMA((4, SUBS)), DMA,
             DMA, DMA((2,)), DMA((4,)), DMA((4,)), DMA, DMA((2,)), DMA, DMA, DMA, DMA,
-            DMA((4, SUBS)), DMA((4, SUBS, 3)), DMA, DMA((12,)),
+            DMA((4, SUBS)), DMA((4, SUBS, 3)), DMA, DMA((12,)), DMA, DMA((4,)),
         ],
         compiler_params=pltpu.CompilerParams(collective_id=0, has_side_effects=True, vmem_limit_bytes=60 << 20),
         name="collect",
-    )(x, wq, wk, wv, b, order, mask)
+    )(x, wq, wk, wv, b, order, mask, up, down, out, bias_row)
 
 
 def greet_exchange(barrier):
@@ -518,7 +564,8 @@
     greet_exchange(pltpu.get_barrier_semaphore())
     big = lambda u: oa_ref.at[pl.ds(u * 1024, 1024)]
     small = lambda u: ob_ref.at[pl.ds(u * 512, 512)]
-    for g in (0, 1, 2, 3):
+    for n in range(4):
+        g = lax.rem(n + 2 * core, 4)
         for k, (src, dst) in enumerate(((a_ref.at[g], big(t)), (b_ref.at[g], small(t)))):
             @pl.when((half != core) | (mine != g))
             def _():
@@ -1113,23 +1160,20 @@
     bq, bv, bz = b_query.reshape(3, HD), b_value.reshape(3, HD), jnp.zeros((C,), F32)
     b_heads = jnp.stack([jnp.concatenate([bq[h], bv[h], bz] if h == 1 else [bv[h], bq[h], bz]) for h in range(3)])
     b_heads = jnp.concatenate([b_heads, jnp.zeros((5, 256), F32)])
-    i = dp % 8
-    bias_row = lax.dynamic_update_slice(jnp.zeros((16, WIDTH), BF16), lax.dynamic_slice(b_up, (96 * i,), (96,)).reshape(1, 96), (0, 96 * mp))
-    share = jnp.concatenate([
-        lax.dynamic_slice(w_up, (0, 96 * i), (WIDTH, 96)).T,
-        lax.dynamic_slice(w_down, (96 * i, 0), (96, WIDTH)),
-        bias_row,
-        lax.dynamic_slice(w_out, (jnp.minimum(32 * i, 160), 0), (32, WIDTH)),
-    ])
-
-    xs, qkv, w_heads, order, mask = collect(tokens, w_query.T, w_key.T, w_value.T, b_heads, order, key_mask)
+    units = lax.dynamic_slice(b_up, (96 * (dp % 8),), (96,)).reshape(1, 96)
+    bias_row = lax.dynamic_update_slice(jnp.zeros((16, WIDTH), BF16), units, (0, 96 * mp))
+
+    xs, qkv, w_heads, order, mask, share = collect(
+        tokens, w_query.T, w_key.T, w_value.T, b_heads, order, key_mask, w_up, w_down, w_out, bias_row
+    )
     qkv, share = tie(qkv, share)
     shares = [share] + [lax.ppermute(share, "mp", ring(i)) for i in (1, 2, 3)]
     c01, ts01, probs01 = attend(0, order, mask, qkv)
-    c01, *shares = tie(c01, *shares)
+    c01, qkv = tie(c01, qkv)
+    c2, ts2, probs2 = attend(2, order, mask, qkv)
+    c2, *shares = tie(c2, *shares)
     near = jnp.stack(shares)
     along, across = swap(near, 2, 4, n_dp), swap(near, 4, 2, n_dp)
-    c2, ts2, probs2 = attend(2, order, mask, qkv)
     c01, c2 = spread(c01, c2)
 
     vecs = jnp.stack([b_out, norm1_gain, norm1_bias, b_down, norm2_gain, norm2_bias, b_out, b_out])
@@ -1140,25 +1184,27 @@
     got, got_nearer, got_tail = swap(give, 4, 2, n_dp), swap(nearer, 2, 4, n_dp), swap(give_tail, 2, 4, n_dp)
     g01, g2 = regroup(g01, g2)
     g01, keep, got, got_nearer, keep_tail, got_tail = tie(g01, keep, got, got_nearer, keep_tail, got_tail)
-    keep = total(keep, got_nearer)
+    groups = [1 << bit for bit in range(3, n_dp.bit_length() - 1)]
+
+    def shard_sums(sums):
+        for bits in groups:
+            sums = total(sums, swap(sums, bits, bits, n_dp))
+        return [pick(sums, mp, 0)] + [lax.ppermute(pick(sums, (mp + k) % 4, 0), "mp", ring(k)) for k in (1, 2, 3)]
+
+    keep = (keep.astype(F32) + got_nearer.astype(F32) + got.astype(F32)).astype(BF16)
     keep_tail, give_tail = total(keep_tail[0], got_tail[0]), total(keep_tail[1], got_tail[1])
     got_tail = swap(give_tail, 4, 2, n_dp)
     d0 = attend_back(0, order, g01, ts01, probs01)
-    d0, order, keep, got, keep_tail, got_tail = tie(d0, order, keep, got, keep_tail, got_tail)
-    sums = jnp.concatenate([total(keep, got), total(keep_tail, got_tail)], axis=1)
-    for bit in range(3, n_dp.bit_length() - 1):
-        sums = total(sums, swap(sums, 1 << bit, 1 << bit, n_dp))
-    parts = [pick(sums, mp, 0)]
-    for i in (1, 2, 3):
-        parts.append(lax.ppermute(pick(sums, (mp + i) % 4, 0), "mp", ring(i)))
+    d0, order, keep, keep_tail, got_tail = tie(d0, order, keep, keep_tail, got_tail)
+    parts = shard_sums(jnp.concatenate([keep, total(keep_tail, got_tail)], axis=1))
     d1 = attend_back(1, order, g01, ts01, probs01)
     d2 = attend_back(2, order, g2, ts2, probs2)
     d2, *parts = tie(d2, *parts)
     mine = sum(p.astype(F32) for p in parts).astype(BF16)
     grad_tokens, *sums = settle(d0, d1, d2, xs, w_heads, grad_residual, mine)
     hq, hk, hv, g_up, g_down, g_out, units, spare, vectors = (s.astype(F32) for s in sums)
-    for bit in range(3, n_dp.bit_length() - 1):
-        hq, hk, hv, spare = (s + swap(s, 1 << bit, 1 << bit, n_dp) for s in (hq, hk, hv, spare))
+    for bits in groups:
+        hq, hk, hv, spare = (s + swap(s, bits, bits, n_dp) for s in (hq, hk, hv, spare))
     sums_of = lambda where: jnp.concatenate([spare[h, 0, where[h] : where[h] + HD] for h in range(3)])
     g_b_up = lax.dynamic_slice(units.reshape(8, 16, WIDTH)[:, 0], (0, 96 * mp), (8, 96)).reshape(WIDTH)
     return (

time: 414 us -> 403 us (0.973)
  Pallas kernels: 350 us -> 345 us
    ppermute x3, waiting for transfers between devices: 7.41 us -> 0.01 us  [body(): shares = [share] + [lax.ppermute(share, 'mp', ring(i)) for i in (1, 2, 3)]]
    ppermute x3, waiting for transfers between devices: 1.29 us -> 5.56 us  [shard_sums(): lax.ppermute(pick(sums, (mp + k) % 4, 0), 'mp', ring(k))]
  transfers between devices with their start and end apart: 12 -> 12, of which waited for: 2 -> 1; matrix products, arithmetic and copies ran while one was open for 0% -> 0% of each run, Pallas kernels for 35% -> 36%
where the time goes in v4:
time: 403 us; the launch traced here: 398 us
  Pallas kernels  345 us (86%)
  starting transfers between devices  20 us (5%)
  other arithmetic  14.8 us (4%)
  local copies, waits for them, and re-layouts  11.1 us (3%)
  waiting for transfers between devices  5.58 us (1%)
    pallas_call x1, Pallas kernels, settle(): pl.pallas_call(settle_kernel, out_shape=[sds((ROWS, WIDTH), BF16)] + [sds...  71.4 us
    pallas_call x1, Pallas kernels, ffn(): pl.pallas_call(ffn_kernel, out_shape=[sds((1024, WIDTH), BF16), sds((1024...  68.7 us
    pallas_call x1, Pallas kernels, collect(): pl.pallas_call(collect_kernel, out_shape=[sds((4 * ROWS, WIDTH), BF16), s...  62.2 us
    pallas_call x1, Pallas kernels, spread(): pl.pallas_call(spread_kernel, out_shape=[jax.ShapeDtypeStruct((4, 1024, C...  37.8 us
    pallas_call x3, Pallas kernels, attend_back(): pl.pallas_call(functools.partial(attend_back_kernel, head), grid=(L // ST...  37.3 us
    pallas_call x2, Pallas kernels, attend(): pl.pallas_call(functools.partial(attend_kernel, first), grid=(heads, L //...  34.1 us
    pallas_call x1, Pallas kernels, regroup(): pl.pallas_call(regroup_kernel, out_shape=[jax.ShapeDtypeStruct((4096, C),...  33.6 us
  transfers between devices with their start and end apart: 12, of which 1 were waited for; matrix products, arithmetic and copies ran while one was open for 0% of the time, Pallas kernels for 36%

profile of v4, /device:TPU:10, one launch (start us, length us, event | category | flops | bytes accessed | tf_op | source)
XLA Modules:
  0.0 397.9 jit_solution(16800452285005978523)
XLA Ops:
  1.4 0.9 fusion.12
  2.4 1.5 fusion.10
  4.8 62.2 %collect.1 = (bf16[4096,768]{1,0:T(8,128)(2,1)}, bf16[3,4096,256]{2,1,0:T(8,128)(2,1)}, bf16[768,768]{1,0:T(8,128)(2,1)}, s32[12288]{0:T(1024)}, s32[1,4096]{1,0:T(1,128)}, /*index=5*/bf16[240,768]{1,0:T(8,128)(2,1)}) custom-call(bf16[1024,768]{1,0:T(8,128)(2,1)} %tok_ref.1, bf16[192,768]{1,0:T(8,128)(2,1)} %bitcast.50, bf16[192,768]{1,0:T(8,128)(2,1)} %bitcast.51, ...), custom_call_target="tpu_custom_call" | custom-call | tf_op jit(solution)/shard_map/collect/pallas_call | solution.py:477
  67.1 7.3 %collective-permute-start.1 = (bf16[240,768]{1,0:T(8,128)(2,1)}, bf16[240,768]{1,0:T(8,128)(2,1)S(1)}, u32[]{:S(2)}, u32[]{:S(2)}) collective-permute-start(bf16[240,768]{1,0:T(8,128)(2,1)} %get-tuple-element.90), channel_id=1, source_target_pairs={{0,2},{1,3},{2,0},{3,1},{4,6},{5,7},{6,4},{7,5},{8,10},{9,11},{10,... | collective-permute-start | bytes 1105928 | tf_op jit(solution)/shard_map/ppermute | solution.py:1170
  74.9 21.8 %attend.2 = (bf16[4096,128]{1,0:T(8,128)(2,1)}, bf16[2,4096,256]{2,1,0:T(8,128)(2,1)}, f32[2,4096,128]{2,1,0:T(8,128)}) custom-call(s32[12288]{0:T(1024)} %get-tuple-element.112.ord_ref, s32[1,4096]{1,0:T(1,128)} %get-tuple-element.78.mask_ref, bf16[3,4096,256]{2,1,0:T(8,128)(2,1)} %get-tuple-element.84.qkv_ref), custom_call_target="tpu_custom_call" | custom-call | flops 17999998976 | bytes 10485760 | tf_op jit(solution)/shard_map/attend/pallas_call | solution.py:120
  96.7 12.3 %attend.3 = (bf16[2048,128]{1,0:T(8,128)(2,1)}, bf16[1,4096,256]{2,1,0:T(8,128)(2,1)}, f32[1,4096,128]{2,1,0:T(8,128)}) custom-call(s32[12288]{0:T(1024)} %get-tuple-element.112.ord_ref, s32[1,4096]{1,0:T(1,128)} %get-tuple-element.78.mask_ref, bf16[3,4096,256]{2,1,0:T(8,128)(2,1)} %get-tuple-element.84.qkv_ref), custom_call_target="tpu_custom_call" | custom-call | flops 8999999488 | bytes 10485760 | tf_op jit(solution)/shard_map/attend/pallas_call | solution.py:120
  109.3 1.6 collective-permute-start.3
  112.4 37.8 %spread.1 = (bf16[4,1024,128]{2,1,0:T(8,128)(2,1)}, bf16[4,512,128]{2,1,0:T(8,128)(2,1)}) custom-call(bf16[4096,128]{1,0:T(8,128)(2,1)} %get-tuple-element.83.a_ref, bf16[2048,128]{1,0:T(8,128)(2,1)} %get-tuple-element.87.b_ref), custom_call_target="tpu_custom_call" | custom-call | tf_op jit(solution)/shard_map/spread/pallas_call | solution.py:549
  150.2 1.1 copy-done.5
  151.3 68.7 %ffn.1 = (bf16[1024,768]{1,0:T(8,128)(2,1)}, f32[1024,768]{1,0:T(8,128)}, bf16[4,1024,128]{2,1,0:T(8,128)(2,1)}, bf16[4,512,128]{2,1,0:T(8,128)(2,1)}, bf16[4,19...) custom-call(bf16[4,1024,128]{2,1,0:T(8,128)(2,1)} %get-tuple-element, ...), custom_call_target="tpu_custom_call" | custom-call | tf_op jit(solution)/shard_map/ffn/pallas_call | solution.py:1123
  220.0 1.1 collective-permute-start.5
  221.1 1.0 collective-permute-start.6
  222.1 1.0 collective-permute-start.7
  223.1 33.6 %regroup.1 = (bf16[4096,128]{1,0:T(8,128)(2,1)}, bf16[2048,128]{1,0:T(8,128)(2,1)}) custom-call(bf16[4,1024,128]{2,1,0:T(8,128)(2,1)} %get-tuple-element.95.a_ref, bf16[4,512,128]{2,1,0:T(8,128)(2,1)} %get-tuple-element.96.b_ref), custom_call_target="tpu_custom_call" | custom-call | tf_op jit(solution)/shard_map/regroup/pallas_call | solution.py:594
  256.8 1.2 fusion.9
  258.0 1.1 collective-permute-start.8
  259.0 12.5 %attend_back.3.d0_ref = bf16[4096,256]{1,0:T(8,128)(2,1)} custom-call(s32[12288]{0:T(1024)} %get-tuple-element.112.ord_ref, bf16[4096,128]{1,0:T(8,128)(2,1)} %get-tuple-element.103.g_ref, bf16[2,4096,256]{2,1,0:T(8,128)(2,1)} %get-tuple-element.104.ts_ref, f32[2,4096,128]{2,1,0:T(8,128)} %get-tuple-element.105.pr_ref), custom_call_target="tpu_custom_call" | custom-call | flops 8999999488 | bytes 10485760 | tf_op jit(solution)/shard_map/attend_back/pallas_call | solution.py:197
  272.0 1.0 add_convert_fusion.2
  273.2 5.2 %collective-permute-start.11 = (bf16[240,768]{1,0:T(8,128)(2,1)S(1)}, bf16[240,768]{1,0:T(8,128)(2,1)S(1)}, u32[]{:S(2)}, u32[]{:S(2)}) collective-permute-start(bf16[240,768]{1,0:T(8,128)(2,1)S(1)} %get-tuple-element.160), channel_id=1, source_target_pairs={{0,3},{1,0},{2,1},{3,2},{4,7},{5,4},{6,5},{7,6},{8,11},{9,8},{10,9... | collective-permute-start | bytes 1105928 | tf_op jit(solution)/shard_map/ppermute | solution.py:1192
  278.8 12.4 %attend_back.4.d1_ref = bf16[4096,256]{1,0:T(8,128)(2,1)} custom-call(s32[12288]{0:T(1024)} %get-tuple-element.112.ord_ref, bf16[4096,128]{1,0:T(8,128)(2,1)} %get-tuple-element.103.g_ref, bf16[2,4096,256]{2,1,0:T(8,128)(2,1)} %get-tuple-element.104.ts_ref, f32[2,4096,128]{2,1,0:T(8,128)} %get-tuple-element.105.pr_ref), custom_call_target="tpu_custom_call" | custom-call | flops 8999999488 | bytes 10485760 | tf_op jit(solution)/shard_map/attend_back/pallas_call | solution.py:197
  291.3 12.4 %attend_back.5.d2_ref = bf16[4096,256]{1,0:T(8,128)(2,1)} custom-call(s32[12288]{0:T(1024)} %get-tuple-element.112.ord_ref, bf16[2048,128]{1,0:T(8,128)(2,1)} %get-tuple-element.113.g_ref, bf16[1,4096,256]{2,1,0:T(8,128)(2,1)} %get-tuple-element.114.ts_ref, f32[1,4096,128]{2,1,0:T(8,128)} %get-tuple-element.115.pr_ref), custom_call_target="tpu_custom_call" | custom-call | flops 8999999488 | bytes 10485760 | tf_op jit(solution)/shard_map/attend_back/pallas_call | solution.py:197
  303.7 5.6 %collective-permute-done.11 = bf16[240,768]{1,0:T(8,128)(2,1)S(1)} collective-permute-done((bf16[240,768]{1,0:T(8,128)(2,1)S(1)}, bf16[240,768]{1,0:T(8,128)(2,1)S(1)}, u32[]{:S(2)}, u32[]{:S(2)}) %collective-permute-start.11) | collective-permute-done | bytes 368672 | tf_op jit(solution)/shard_map/ppermute | solution.py:1192
  309.2 0.9 add_convert_fusion.1.mine_ref
  310.2 71.4 %settle.1 = (bf16[1024,768]{1,0:T(8,128)(2,1)}, bf16[192,768]{1,0:T(8,128)(2,1)}, bf16[192,768]{1,0:T(8,128)(2,1)}, bf16[192,768]{1,0:T(8,128)(2,1)}, bf16[768,7...) custom-call(bf16[4096,256]{1,0:T(8,128)(2,1)} %attend_back.3.d0_ref,, ...), custom_call_target="tpu_custom_call" | custom-call | tf_op jit(solution)/shard_map/settle/pallas_call | solution.py:837
  381.6 1.4 convert_bitcast_fusion
  383.1 2.0 copy.36
  385.0 0.9 convert_element_type.101
  386.0 1.6 convert_element_type.104
  387.6 0.9 convert_bitcast_fusion.1
  391.7 0.9 slice.111
  394.6 1.1 copy.40
  396.6 1.1 copy.41
  (87 shorter events, 11.2 us)
Async XLA Ops:
  67.0 42.0 %collective-permute-start = (bf16[240,768]{1,0:T(8,128)(2,1)}, bf16[240,768]{1,0:T(8,128)(2,1)S(1)}, u32[]{:S(2)}, u32[]{:S(2)}) collective-permute-start(bf16[240,768]{1,0:T(8,128)(2,1)} %get-tuple-element.90), channel_id=1, source_target_pairs={{0,1},{1,2},{2,3},{3,0},{4,5},{5,6},{6,7},{7,4},{8,9},{9,10},{10,1... | collective-permute-start | bytes 1105928 | tf_op jit(solution)/shard_map/ppermute | solution.py:1170
  67.1 41.9 %collective-permute-start.1 = (bf16[240,768]{1,0:T(8,128)(2,1)}, bf16[240,768]{1,0:T(8,128)(2,1)S(1)}, u32[]{:S(2)}, u32[]{:S(2)}) collective-permute-start(bf16[240,768]{1,0:T(8,128)(2,1)} %get-tuple-element.90), channel_id=1, source_target_pairs={{0,2},{1,3},{2,0},{3,1},{4,6},{5,7},{6,4},{7,5},{8,10},{9,11},{10,... | collective-permute-start | bytes 1105928 | tf_op jit(solution)/shard_map/ppermute | solution.py:1170
  74.4 34.6 %collective-permute-start.2 = (bf16[240,768]{1,0:T(8,128)(2,1)}, bf16[240,768]{1,0:T(8,128)(2,1)S(1)}, u32[]{:S(2)}, u32[]{:S(2)}) collective-permute-start(bf16[240,768]{1,0:T(8,128)(2,1)} %get-tuple-element.90), channel_id=1, source_target_pairs={{0,3},{1,0},{2,1},{3,2},{4,7},{5,4},{6,5},{7,6},{8,11},{9,8},{10,9... | collective-permute-start | bytes 1105928 | tf_op jit(solution)/shard_map/ppermute | solution.py:1170
  96.7 12.4 %copy-start.9 = (bf16[240,768]{1,0:T(8,128)(2,1)S(1)}, bf16[240,768]{1,0:T(8,128)(2,1)}, u32[]{:S(2)}) copy-start(bf16[240,768]{1,0:T(8,128)(2,1)} %get-tuple-element.90) | copy-start | bytes 1105924
  109.1 2.6 copy-start.16
  109.1 2.6 copy-start.17
  109.1 2.6 copy-start.18
  109.1 2.6 copy-start.19
  109.1 2.6 copy-start.20
  109.1 2.6 copy-start.21
  109.3 1.6 copy-start.2
  109.3 40.8 %collective-permute-start.3 = (bf16[4,240,768]{2,1,0:T(8,128)(2,1)S(1)}, bf16[4,240,768]{2,1,0:T(8,128)(2,1)S(1)}, u32[]{:S(2)}, u32[]{:S(2)}) collective-permute-start(bf16[4,240,768]{2,1,0:T(8,128)(2,1)S(1)} %pad_maximum_fusion.near_ref), channel_id=1, source_target_pairs={{0,8},{4,20},{8,0},{12,28},{16,24},{20,4},{24,16},{28,12},{1,9},{5... | collective-permute-start | bytes 4423688 | tf_op jit(solution)/shard_map/ppermute | solution.py:1139
  110.9 39.3 %collective-permute-start.4 = (bf16[4,240,768]{2,1,0:T(8,128)(2,1)S(1)}, bf16[4,240,768]{2,1,0:T(8,128)(2,1)}, u32[]{:S(2)}, u32[]{:S(2)}) collective-permute-start(bf16[4,240,768]{2,1,0:T(8,128)(2,1)S(1)} %pad_maximum_fusion.near_ref), channel_id=1, source_target_pairs={{0,16},{4,12},{8,24},{12,4},{16,0},{20,28},{24,8},{28,20},{1,17},{... | collective-permute-start | bytes 4423688 | tf_op jit(solution)/shard_map/ppermute | solution.py:1139
  150.2 1.1 copy-start.5
  220.0 36.7 %copy-start.8 = (bf16[2,4,48,768]{3,2,1,0:T(8,128)(2,1)S(1)}, bf16[2,4,48,768]{3,2,1,0:T(8,128)(2,1)}, u32[]{:S(2)}) copy-start(bf16[2,4,48,768]{3,2,1,0:T(8,128)(2,1)} %get-tuple-element.109) | copy-start | bytes 1769476
  220.0 36.7 %collective-permute-start.5 = (bf16[4,192,768]{2,1,0:T(8,128)(2,1)}, bf16[4,192,768]{2,1,0:T(8,128)(2,1)S(1)}, u32[]{:S(2)}, u32[]{:S(2)}) collective-permute-start(bf16[4,192,768]{2,1,0:T(8,128)(2,1)} %get-tuple-element.99), channel_id=1, source_target_pairs={{0,16},{4,12},{8,24},{12,4},{16,0},{20,28},{24,8},{28,20},{1,17},{... | collective-permute-start | bytes 3538952 | tf_op jit(solution)/shard_map/ppermute | solution.py:1139
  221.1 35.6 %collective-permute-start.6 = (bf16[4,192,768]{2,1,0:T(8,128)(2,1)}, bf16[4,192,768]{2,1,0:T(8,128)(2,1)S(1)}, u32[]{:S(2)}, u32[]{:S(2)}) collective-permute-start(bf16[4,192,768]{2,1,0:T(8,128)(2,1)} %get-tuple-element.100), channel_id=1, source_target_pairs={{0,8},{4,20},{8,0},{12,28},{16,24},{20,4},{24,16},{28,12},{1,9},{5... | collective-permute-start | bytes 3538952 | tf_op jit(solution)/shard_map/ppermute | solution.py:1139
  222.1 34.6 %collective-permute-start.7 = (bf16[2,4,48,768]{3,2,1,0:T(8,128)(2,1)}, bf16[2,4,48,768]{3,2,1,0:T(8,128)(2,1)}, u32[]{:S(2)}, u32[]{:S(2)}) collective-permute-start(bf16[2,4,48,768]{3,2,1,0:T(8,128)(2,1)} %get-tuple-element.102), channel_id=1, source_target_pairs={{0,8},{4,20},{8,0},{12,28},{16,24},{20,4},{24,16},{28,12},{1,9},{5... | collective-permute-start | bytes 1769480 | tf_op jit(solution)/shard_map/ppermute | solution.py:1139
  258.0 14.0 %collective-permute-start.8 = (bf16[4,48,768]{2,1,0:T(8,128)(2,1)S(1)}, bf16[4,48,768]{2,1,0:T(8,128)(2,1)}, u32[]{:S(2)}, u32[]{:S(2)}) collective-permute-start(bf16[4,48,768]{2,1,0:T(8,128)(2,1)S(1)} %get-tuple-element.164), channel_id=1, source_target_pairs={{0,16},{4,12},{8,24},{12,4},{16,0},{20,28},{24,8},{28,20},{1,17},{... | collective-permute-start | bytes 884744 | tf_op jit(solution)/shard_map/ppermute | solution.py:1139
  259.0 12.5 %copy-start.7 = (bf16[4,192,768]{2,1,0:T(8,128)(2,1)S(1)}, bf16[4,192,768]{2,1,0:T(8,128)(2,1)}, u32[]{:S(2)}) copy-start(bf16[4,192,768]{2,1,0:T(8,128)(2,1)} %get-tuple-element.106) | copy-start | bytes 3538948
  273.1 30.6 %collective-permute-start.10 = (bf16[240,768]{1,0:T(8,128)(2,1)S(1)}, bf16[240,768]{1,0:T(8,128)(2,1)S(1)}, u32[]{:S(2)}, u32[]{:S(2)}) collective-permute-start(bf16[240,768]{1,0:T(8,128)(2,1)S(1)} %get-tuple-element.163), channel_id=1, source_target_pairs={{0,2},{1,3},{2,0},{3,1},{4,6},{5,7},{6,4},{7,5},{8,10},{9,11},{10,... | collective-permute-start | bytes 1105928 | tf_op jit(solution)/shard_map/ppermute | solution.py:1192
  273.2 36.0 %collective-permute-start.11 = (bf16[240,768]{1,0:T(8,128)(2,1)S(1)}, bf16[240,768]{1,0:T(8,128)(2,1)S(1)}, u32[]{:S(2)}, u32[]{:S(2)}) collective-permute-start(bf16[240,768]{1,0:T(8,128)(2,1)S(1)} %get-tuple-element.160), channel_id=1, source_target_pairs={{0,3},{1,0},{2,1},{3,2},{4,7},{5,4},{6,5},{7,6},{8,11},{9,8},{10,9... | collective-permute-start | bytes 1105928 | tf_op jit(solution)/shard_map/ppermute | solution.py:1192
  278.4 30.8 %collective-permute-start.9 = (bf16[240,768]{1,0:T(8,128)(2,1)S(1)}, bf16[240,768]{1,0:T(8,128)(2,1)S(1)}, u32[]{:S(2)}, u32[]{:S(2)}) collective-permute-start(bf16[240,768]{1,0:T(8,128)(2,1)S(1)} %get-tuple-element.162), channel_id=1, source_target_pairs={{0,1},{1,2},{2,3},{3,0},{4,5},{5,6},{6,7},{7,4},{8,9},{9,10},{10,1... | collective-permute-start | bytes 1105928 | tf_op jit(solution)/shard_map/ppermute | solution.py:1192
  383.1 2.9 copy-start.6
  386.0 1.6 copy-start.13
  386.0 2.4 copy-start.12
  387.6 1.7 copy-start.11
  387.6 2.6 copy-start.10
  388.5 2.6 copy-start.15
  388.5 6.2 %copy-start.3 = (bf16[1024,768]{1,0:T(8,128)(2,1)S(1)}, bf16[1024,768]{1,0:T(8,128)(2,1)}, u32[]{:S(2)}) copy-start(bf16[1024,768]{1,0:T(8,128)(2,1)} %get-tuple-element.201) | copy-start | bytes 4718596
  394.6 2.0 copy-start.4
  394.6 3.1 copy-start.1
  (2 other events, 1.5 us)

commit v5 on v4

--- a/solution.py
+++ b/solution.py
@@ -602,9 +602,9 @@
     )(a, b)
 
 
-def settle_kernel(d0_ref, d1_ref, d2_ref, xs_ref, w_ref, extra_ref, mine_ref, out_ref, *rest):
+def settle_kernel(d0_ref, d1_ref, d2_ref, xs_in, w_ref, extra_in, mine_ref, out_ref, *rest):
     pieces_out, rest = rest[:9], rest[9:]
-    (heads_ref, grads_ref, stage, pair_in, chain_in, gw, gwl, h_in, z_in, z_out,
+    (xs_ref, extra_ref, up_t, in_sem, heads_ref, grads_ref, stage, pair_in, chain_in, gw, gwl, h_in, z_in, z_out,
                   pair_recv, pair_send, chain_recv, chain_send, relay_send,
                   s_recv, s_send, c_recv, c_send, h_recv, h_send, z_recv, z_send, q_recv, q_send, out_sem) = rest
     dp, mp, core, t = place()
@@ -616,6 +616,9 @@
     quarter = lambda q: pl.ds(pl.multiple_of(q * QUARTER, QUARTER), QUARTER)
     share = lambda j, parity: grads_ref.at[2 * j + parity]
 
+    later = [pltpu.make_async_copy(src, dst, in_sem.at[n]) for n, (src, dst) in enumerate(((xs_in, xs_ref), (extra_in, extra_ref)))]
+    for copy in later:
+        copy.start()
     greet(pltpu.get_barrier_semaphore(), True)
 
     grads_ref[2 * spot + core] = mine_ref[...]
@@ -623,6 +626,7 @@
         send(mine_ref, share(spot, core), s_send.at[rel], s_recv.at[rel], at(mate(dp, rel), mp))
 
     def weight_gradients():
+        later[0].wait()
         gw[...] = jnp.zeros_like(gw)
 
         def part(i, sums):
@@ -760,6 +764,22 @@
             send(mine, mine, q_send.at[rel], q_recv.at[spot], at(mate(dp, rel), mp))
             send(mine, mine, q_send.at[rel + 3], q_recv.at[spot], at(mate(dp, rel) + step, mp))
 
+    for j in range(4):
+        wait(share(j, 1 - core), c_recv.at[j])
+    up_t[...] = grads_ref[:, pl.ds(0, 96), :].reshape(WIDTH, WIDTH).T
+    copies = [pltpu.make_async_copy(up_t, pieces_out[3], out_sem.at[1])]
+    for i in range(8):
+        for n, (first, rows) in enumerate(((0, 96), (96, 96), (192, 32), (224, 16))):
+            if n == 0 or (n == 2 and i >= 6):
+                continue
+            dst = pieces_out[3 + n].at[pl.ds(i * rows, rows)]
+            copies.append(pltpu.make_async_copy(grads_ref.at[i, pl.ds(first, rows)], dst, out_sem.at[20 + 4 * i + n]))
+    copies.append(pltpu.make_async_copy(grads_ref.at[6, pl.ds(192, 16)], pieces_out[8], out_sem.at[0]))
+    early = len(copies)
+    for copy in copies:
+        copy.start()
+    later[1].wait()
+
     for s in range(SUBS):
         cut = pl.ds(s * SUB, SUB)
         rows = pl.ds(pl.multiple_of(t * ROWS + s * SUB, SUB), SUB)
@@ -779,23 +799,13 @@
         @pl.when(jnp.logical_not(gives) | (spot != q))
         def _():
             wait(heads_ref.at[quarter(q)], q_recv.at[q])
-    for j in range(4):
-        wait(share(j, 1 - core), c_recv.at[j])
-    copies = []
-    for i in range(8):
-        for n, (first, rows) in enumerate(((0, 96), (96, 96), (192, 32), (224, 16))):
-            if n == 2 and i >= 6:
-                continue
-            dst = pieces_out[3 + n].at[pl.ds(i * rows, rows)]
-            copies.append(pltpu.make_async_copy(grads_ref.at[i, pl.ds(first, rows)], dst, out_sem.at[20 + 4 * i + n]))
-    copies.append(pltpu.make_async_copy(grads_ref.at[6, pl.ds(192, 16)], pieces_out[8], out_sem.at[0]))
     for h in range(3):
         for n, where in enumerate((0, 2, 1) if h == 1 else (1, 3, 0)):
             src = heads_ref.at[pl.ds((4 * h + where) * HD, HD)]
             copies.append(pltpu.make_async_copy(src, pieces_out[n].at[pl.ds(h * HD, HD)], out_sem.at[8 + 3 * h + n]))
         src = heads_ref.at[pl.ds(h * 256 + (192 if h == 1 else 128), 16)]
         copies.append(pltpu.make_async_copy(src, pieces_out[7].at[h], out_sem.at[17 + h]))
-    for copy in copies:
+    for copy in copies[early:]:
         copy.start()
 
     for s in range(SUBS):
@@ -838,9 +848,10 @@
         settle_kernel,
         out_shape=[sds((ROWS, WIDTH), BF16)] + [sds((rows, WIDTH), BF16) for rows in (192, 192, 192, 768, 768, 192, 128)]
         + [sds((3, 16, WIDTH), BF16), sds((16, WIDTH), BF16)],
-        in_specs=[VM] * 7,
+        in_specs=[VM, VM, VM, ANY, VM, ANY, VM],
         out_specs=[VM] + [ANY] * 9,
-        scratch_shapes=[VMEM((WIDTH, WIDTH), BF16), VMEM((8, SHARE_ALL, WIDTH), BF16)] + [VMEM((4 * ROWS, WIDTH), BF16)] * 3 + [
+        scratch_shapes=[VMEM((4 * ROWS, WIDTH), BF16), VMEM((ROWS, WIDTH), F32), VMEM((WIDTH, WIDTH), BF16), DMA((2,)),
+                        VMEM((WIDTH, WIDTH), BF16), VMEM((8, SHARE_ALL, WIDTH), BF16)] + [VMEM((4 * ROWS, WIDTH), BF16)] * 3 + [
             VMEM((WIDTH, WIDTH), F32), VMEM((WIDTH, WIDTH), BF16), VMEM((4, QUARTER, WIDTH), BF16), VMEM((2, QUARTER, WIDTH), BF16),
             VMEM((QUARTER, WIDTH), BF16),
             DMA((4, SUBS)), DMA((4, SUBS)), DMA((4, SUBS)), DMA((3, SUBS)), DMA((SUBS,)),
@@ -870,9 +881,9 @@
     return jnp.sum(v, axis=-1, keepdims=True) * (1.0 / FF_MODEL)
 
 
-def ffn_kernel(c01_ref, c2_ref, tok_ref, cot_ref, vec_ref, near_ref, a_ref, b_ref,
-               out_ref, res_ref, g01_ref, g2_ref, keep_ref, next_ref, give_ref, keep_tail_ref, give_tail_ref,
-               w, wout, ctx, x, gf, act, slope, zhat, acc, rstd, cols, recv, recv2, tail, tail_in,
+def ffn_kernel(c01_ref, c2_ref, tok_in, cot_in, vec_ref, near_ref, a_ref, b_ref,
+               out_o, res_o, g01_o, g2_o, keep_ref, next_ref, give_ref, keep_tail_ref, give_tail_ref,
+               tok_ref, cot_ref, out_ref, res_ref, g01_ref, g2_ref, in_sem, early_sem, w, wout, ctx, x, gf, act, slope, zhat, acc, rstd, cols, recv, recv2, tail, tail_in,
                o_local, o_send, o_recv, f_send, f_recv, w_local, w_send, w_recv, d_send, d_recv,
                g_send, g_recv, m_send, m_recv, t_send, t_recv, out_sem, tail_sem):
     dp, mp, core, t = place()
@@ -882,6 +893,11 @@
     one, two = jnp.where(core == 0, 1, 2), jnp.where(core == 0, 2, 1)
     mate_a, mate_b = at(dp + 2 * ((spot ^ one) - spot), mp), at(dp + 2 * ((spot ^ two) - spot), mp)
     shard = lambda k: lax.rem(mp - k + 4, 4)
+    later = [pltpu.make_async_copy(src, dst, in_sem.at[n]) for n, (src, dst) in enumerate(((tok_in, tok_ref), (cot_in, cot_ref)))]
+    for copy in later:
+        copy.start()
+    results = [pltpu.make_async_copy(src, dst, early_sem.at[n])
+               for n, (src, dst) in enumerate(((out_ref, out_o), (res_ref, res_o), (g01_ref, g01_o), (g2_ref, g2_o)))]
     barrier = pltpu.get_barrier_semaphore()
     for device in (partner, mate_a, mate_b):
         signal(barrier, device)
@@ -943,6 +959,7 @@
 
             wait(part, o_recv.at[j, k])
 
+    later[0].wait()
     for rows in row_chunks:
         h = jnp.dot(ctx[rows, :], wout[...], preferred_element_type=F32) + tok_ref[rows, :].astype(F32) + b_out
         h = h - row_mean(h)
@@ -987,6 +1004,7 @@
             before = rows
         down(j, rel, before)
 
+    later[1].wait()
     for rows in row_chunks:
         z = acc[rows, :]
         z = z - row_mean(z)
@@ -1001,6 +1019,8 @@
         cols[pl.ds(5, 1), :] += jnp.sum(gs, axis=0, keepdims=True)
         acc[rows, :] = gs
         gf[rows, :] = gs.astype(BF16)
+
+    results[0].start()
 
     for rel in range(4):
         for k in range(4):
@@ -1064,6 +1084,9 @@
         g2_ref[g] = jnp.where(lane < HD, top, pltpu.roll(low, HD, 1)).astype(BF16)
         g2_ref[g + 1] = jnp.where(lane < HD, pltpu.roll(top, HD, 1), low).astype(BF16)
 
+    for copy in results[1:]:
+        copy.start()
+
     for n in range(3):
         got = dot(ctx[:, pl.ds(n * 256, 256)], gf[...], 0, 0).astype(BF16)
         for i in range(8):
@@ -1099,6 +1122,8 @@
             def _():
                 pltpu.make_async_copy(tail_in.at[j], ref.at[across], tail_sem.at[rel]).start()
     give.wait()
+    for copy in results:
+        copy.wait()
     wait(recv2, out_sem.at[0])
     wait(recv2, out_sem.at[1])
     for rel in range(4):
@@ -1123,9 +1148,10 @@
     return pl.pallas_call(
         ffn_kernel,
         out_shape=[sds((1024, WIDTH), BF16), sds((1024, WIDTH), F32), sds((4, 1024, C), BF16), sds((4, 512, C), BF16), main, main, main, rest, rest],
-        in_specs=[VM] * 5 + [ANY] * 3,
-        out_specs=[VM] * 4 + [ANY] * 5,
+        in_specs=[VM, VM, ANY, ANY, VM] + [ANY] * 3,
+        out_specs=[ANY] * 9,
         scratch_shapes=[
+            rows(BF16), rows(BF16), rows(BF16), rows(F32), four(1024, C), four(512, C), DMA((2,)), DMA((4,)),
             VMEM((8, 4, SHARE, WIDTH), BF16), VMEM((WIDTH, WIDTH), BF16), rows(BF16), rows(BF16), rows(BF16), four(1024, WIDTH), four(1024, WIDTH),
             rows(F32), rows(F32), VMEM((1024, 1), F32), VMEM((16, WIDTH), F32), four(4, 192, WIDTH), four(192, WIDTH),
             VMEM((2, 4, 4, 48, WIDTH), BF16), four(4, 48, WIDTH),
@@ -1219,7 +1245,7 @@
         vectors[4],
         vectors[0],
         vectors[1],
-        g_up.T,
+        g_up,
         g_b_up,
         g_down,
         vectors[5],

time: 403 us -> 396 us (0.983)
  Pallas kernels: 345 us -> 338 us
  transfers between devices with their start and end apart: 12 -> 12, of which waited for: 1 -> 1; matrix products, arithmetic and copies ran while one was open for 0% -> 0% of each run, Pallas kernels for 36% -> 37%
where the time goes in v5:
time: 396 us; the launch traced here: 391 us
  Pallas kernels  338 us (85%)
  starting transfers between devices  20 us (5%)
  other arithmetic  16.3 us (4%)
  local copies, waits for them, and re-layouts  9.18 us (2%)
  waiting for transfers between devices  5.6 us (1%)
    pallas_call x1, Pallas kernels, settle(): pl.pallas_call(settle_kernel, out_shape=[sds((ROWS, WIDTH), BF16)] + [sds...  67.9 us
    pallas_call x1, Pallas kernels, ffn(): pl.pallas_call(ffn_kernel, out_shape=[sds((1024, WIDTH), BF16), sds((1024...  65.5 us
    pallas_call x1, Pallas kernels, collect(): pl.pallas_call(collect_kernel, out_shape=[sds((4 * ROWS, WIDTH), BF16), s...  62.2 us
    pallas_call x1, Pallas kernels, spread(): pl.pallas_call(spread_kernel, out_shape=[jax.ShapeDtypeStruct((4, 1024, C...  37.8 us
    pallas_call x3, Pallas kernels, attend_back(): pl.pallas_call(functools.partial(attend_back_kernel, head), grid=(L // ST...  37.3 us
    pallas_call x2, Pallas kernels, attend(): pl.pallas_call(functools.partial(attend_kernel, first), grid=(heads, L //...  34.1 us
    pallas_call x1, Pallas kernels, regroup(): pl.pallas_call(regroup_kernel, out_shape=[jax.ShapeDtypeStruct((4096, C),...  33.6 us
  transfers between devices with their start and end apart: 12, of which 1 were waited for; matrix products, arithmetic and copies ran while one was open for 0% of the time, Pallas kernels for 37%

profile of v5, /device:TPU:10, one launch (start us, length us, event | category | flops | bytes accessed | tf_op | source)
XLA Modules:
  0.0 390.8 jit_solution(1447925224195856538)
XLA Ops:
  1.4 0.9 fusion.12
  2.4 1.5 fusion.10
  4.8 62.2 %collect.1 = (bf16[4096,768]{1,0:T(8,128)(2,1)}, bf16[3,4096,256]{2,1,0:T(8,128)(2,1)}, bf16[768,768]{1,0:T(8,128)(2,1)}, s32[12288]{0:T(1024)}, s32[1,4096]{1,0:T(1,128)}, /*index=5*/bf16[240,768]{1,0:T(8,128)(2,1)}) custom-call(bf16[1024,768]{1,0:T(8,128)(2,1)} %tok_in.1, bf16[192,768]{1,0:T(8,128)(2,1)} %bitcast.48, bf16[192,768]{1,0:T(8,128)(2,1)} %bitcast.49, ...), custom_call_target="tpu_custom_call" | custom-call | tf_op jit(solution)/shard_map/collect/pallas_call | solution.py:477
  67.1 7.3 %collective-permute-start.1 = (bf16[240,768]{1,0:T(8,128)(2,1)}, bf16[240,768]{1,0:T(8,128)(2,1)S(1)}, u32[]{:S(2)}, u32[]{:S(2)}) collective-permute-start(bf16[240,768]{1,0:T(8,128)(2,1)} %get-tuple-element.90), channel_id=1, source_target_pairs={{0,2},{1,3},{2,0},{3,1},{4,6},{5,7},{6,4},{7,5},{8,10},{9,11},{10,... | collective-permute-start | bytes 1105928 | tf_op jit(solution)/shard_map/ppermute | solution.py:1196
  74.9 21.8 %attend.2 = (bf16[4096,128]{1,0:T(8,128)(2,1)}, bf16[2,4096,256]{2,1,0:T(8,128)(2,1)}, f32[2,4096,128]{2,1,0:T(8,128)}) custom-call(s32[12288]{0:T(1024)} %get-tuple-element.112.ord_ref, s32[1,4096]{1,0:T(1,128)} %get-tuple-element.78.mask_ref, bf16[3,4096,256]{2,1,0:T(8,128)(2,1)} %get-tuple-element.84.qkv_ref), custom_call_target="tpu_custom_call" | custom-call | flops 17999998976 | bytes 10485760 | tf_op jit(solution)/shard_map/attend/pallas_call | solution.py:120
  96.7 12.3 %attend.3 = (bf16[2048,128]{1,0:T(8,128)(2,1)}, bf16[1,4096,256]{2,1,0:T(8,128)(2,1)}, f32[1,4096,128]{2,1,0:T(8,128)}) custom-call(s32[12288]{0:T(1024)} %get-tuple-element.112.ord_ref, s32[1,4096]{1,0:T(1,128)} %get-tuple-element.78.mask_ref, bf16[3,4096,256]{2,1,0:T(8,128)(2,1)} %get-tuple-element.84.qkv_ref), custom_call_target="tpu_custom_call" | custom-call | flops 8999999488 | bytes 10485760 | tf_op jit(solution)/shard_map/attend/pallas_call | solution.py:120
  109.3 1.5 collective-permute-start.3
  112.4 37.8 %spread.1 = (bf16[4,1024,128]{2,1,0:T(8,128)(2,1)}, bf16[4,512,128]{2,1,0:T(8,128)(2,1)}) custom-call(bf16[4096,128]{1,0:T(8,128)(2,1)} %get-tuple-element.83.a_ref, bf16[2048,128]{1,0:T(8,128)(2,1)} %get-tuple-element.87.b_ref), custom_call_target="tpu_custom_call" | custom-call | tf_op jit(solution)/shard_map/spread/pallas_call | solution.py:549
  150.2 1.1 copy-done.5
  151.3 65.5 %ffn.1 = (bf16[1024,768]{1,0:T(8,128)(2,1)}, f32[1024,768]{1,0:T(8,128)}, bf16[4,1024,128]{2,1,0:T(8,128)(2,1)}, bf16[4,512,128]{2,1,0:T(8,128)(2,1)}, bf16[4,19...) custom-call(bf16[4,1024,128]{2,1,0:T(8,128)(2,1)} %get-tuple-element, ...), custom_call_target="tpu_custom_call" | custom-call | tf_op jit(solution)/shard_map/ffn/pallas_call | solution.py:1148
  216.8 1.1 collective-permute-start.5
  217.9 1.0 collective-permute-start.6
  218.9 1.0 collective-permute-start.7
  219.9 33.6 %regroup.1 = (bf16[4096,128]{1,0:T(8,128)(2,1)}, bf16[2048,128]{1,0:T(8,128)(2,1)}) custom-call(bf16[4,1024,128]{2,1,0:T(8,128)(2,1)} %get-tuple-element.95.a_ref, bf16[4,512,128]{2,1,0:T(8,128)(2,1)} %get-tuple-element.96.b_ref), custom_call_target="tpu_custom_call" | custom-call | tf_op jit(solution)/shard_map/regroup/pallas_call | solution.py:594
  253.6 1.2 fusion.9
  254.8 1.1 collective-permute-start.8
  255.9 12.5 %attend_back.3.d0_ref = bf16[4096,256]{1,0:T(8,128)(2,1)} custom-call(s32[12288]{0:T(1024)} %get-tuple-element.112.ord_ref, bf16[4096,128]{1,0:T(8,128)(2,1)} %get-tuple-element.103.g_ref, bf16[2,4096,256]{2,1,0:T(8,128)(2,1)} %get-tuple-element.104.ts_ref, f32[2,4096,128]{2,1,0:T(8,128)} %get-tuple-element.105.pr_ref), custom_call_target="tpu_custom_call" | custom-call | flops 8999999488 | bytes 10485760 | tf_op jit(solution)/shard_map/attend_back/pallas_call | solution.py:197
  268.8 1.0 add_convert_fusion.2
  270.0 5.2 %collective-permute-start.11 = (bf16[240,768]{1,0:T(8,128)(2,1)S(1)}, bf16[240,768]{1,0:T(8,128)(2,1)S(1)}, u32[]{:S(2)}, u32[]{:S(2)}) collective-permute-start(bf16[240,768]{1,0:T(8,128)(2,1)S(1)} %get-tuple-element.143), channel_id=1, source_target_pairs={{0,3},{1,0},{2,1},{3,2},{4,7},{5,4},{6,5},{7,6},{8,11},{9,8},{10,9... | collective-permute-start | bytes 1105928 | tf_op jit(solution)/shard_map/ppermute | solution.py:1218
  275.6 12.4 %attend_back.4.d1_ref = bf16[4096,256]{1,0:T(8,128)(2,1)} custom-call(s32[12288]{0:T(1024)} %get-tuple-element.112.ord_ref, bf16[4096,128]{1,0:T(8,128)(2,1)} %get-tuple-element.103.g_ref, bf16[2,4096,256]{2,1,0:T(8,128)(2,1)} %get-tuple-element.104.ts_ref, f32[2,4096,128]{2,1,0:T(8,128)} %get-tuple-element.105.pr_ref), custom_call_target="tpu_custom_call" | custom-call | flops 8999999488 | bytes 10485760 | tf_op jit(solution)/shard_map/attend_back/pallas_call | solution.py:197
  288.1 12.4 %attend_back.5.d2_ref = bf16[4096,256]{1,0:T(8,128)(2,1)} custom-call(s32[12288]{0:T(1024)} %get-tuple-element.112.ord_ref, bf16[2048,128]{1,0:T(8,128)(2,1)} %get-tuple-element.113.g_ref, bf16[1,4096,256]{2,1,0:T(8,128)(2,1)} %get-tuple-element.114.ts_ref, f32[1,4096,128]{2,1,0:T(8,128)} %get-tuple-element.115.pr_ref), custom_call_target="tpu_custom_call" | custom-call | flops 8999999488 | bytes 10485760 | tf_op jit(solution)/shard_map/attend_back/pallas_call | solution.py:197
  300.5 5.6 %collective-permute-done.11 = bf16[240,768]{1,0:T(8,128)(2,1)S(1)} collective-permute-done((bf16[240,768]{1,0:T(8,128)(2,1)S(1)}, bf16[240,768]{1,0:T(8,128)(2,1)S(1)}, u32[]{:S(2)}, u32[]{:S(2)}) %collective-permute-start.11) | collective-permute-done | bytes 368672 | tf_op jit(solution)/shard_map/ppermute | solution.py:1218
  306.1 0.9 add_convert_fusion.1.mine_ref
  307.0 67.9 %settle.1 = (bf16[1024,768]{1,0:T(8,128)(2,1)}, bf16[192,768]{1,0:T(8,128)(2,1)}, bf16[192,768]{1,0:T(8,128)(2,1)}, bf16[192,768]{1,0:T(8,128)(2,1)}, bf16[768,7...) custom-call(bf16[4096,256]{1,0:T(8,128)(2,1)} %attend_back.3.d0_ref,, ...), custom_call_target="tpu_custom_call" | custom-call | tf_op jit(solution)/shard_map/settle/pallas_call | solution.py:847
  374.9 0.9 convert_element_type.103
  375.9 2.9 convert_element_type.106
  378.8 1.6 convert_element_type.107
  380.4 0.9 convert_bitcast_fusion
  382.1 0.9 convert_bitcast_fusion.2
  384.5 0.9 slice.111
  387.5 1.1 copy.39
  389.4 1.1 copy.40
  (86 shorter events, 10.3 us)
Async XLA Ops:
  67.0 42.0 %collective-permute-start = (bf16[240,768]{1,0:T(8,128)(2,1)}, bf16[240,768]{1,0:T(8,128)(2,1)S(1)}, u32[]{:S(2)}, u32[]{:S(2)}) collective-permute-start(bf16[240,768]{1,0:T(8,128)(2,1)} %get-tuple-element.90), channel_id=1, source_target_pairs={{0,1},{1,2},{2,3},{3,0},{4,5},{5,6},{6,7},{7,4},{8,9},{9,10},{10,1... | collective-permute-start | bytes 1105928 | tf_op jit(solution)/shard_map/ppermute | solution.py:1196
  67.1 41.9 %collective-permute-start.1 = (bf16[240,768]{1,0:T(8,128)(2,1)}, bf16[240,768]{1,0:T(8,128)(2,1)S(1)}, u32[]{:S(2)}, u32[]{:S(2)}) collective-permute-start(bf16[240,768]{1,0:T(8,128)(2,1)} %get-tuple-element.90), channel_id=1, source_target_pairs={{0,2},{1,3},{2,0},{3,1},{4,6},{5,7},{6,4},{7,5},{8,10},{9,11},{10,... | collective-permute-start | bytes 1105928 | tf_op jit(solution)/shard_map/ppermute | solution.py:1196
  74.4 34.6 %collective-permute-start.2 = (bf16[240,768]{1,0:T(8,128)(2,1)}, bf16[240,768]{1,0:T(8,128)(2,1)S(1)}, u32[]{:S(2)}, u32[]{:S(2)}) collective-permute-start(bf16[240,768]{1,0:T(8,128)(2,1)} %get-tuple-element.90), channel_id=1, source_target_pairs={{0,3},{1,0},{2,1},{3,2},{4,7},{5,4},{6,5},{7,6},{8,11},{9,8},{10,9... | collective-permute-start | bytes 1105928 | tf_op jit(solution)/shard_map/ppermute | solution.py:1196
  96.7 12.4 %copy-start.9 = (bf16[240,768]{1,0:T(8,128)(2,1)S(1)}, bf16[240,768]{1,0:T(8,128)(2,1)}, u32[]{:S(2)}) copy-start(bf16[240,768]{1,0:T(8,128)(2,1)} %get-tuple-element.90) | copy-start | bytes 1105924
  109.1 2.6 copy-start.16
  109.1 2.6 copy-start.17
  109.1 2.6 copy-start.18
  109.1 2.6 copy-start.19
  109.1 2.6 copy-start.20
  109.1 2.6 copy-start.21
  109.3 1.5 copy-start.2
  109.3 40.8 %collective-permute-start.3 = (bf16[4,240,768]{2,1,0:T(8,128)(2,1)S(1)}, bf16[4,240,768]{2,1,0:T(8,128)(2,1)S(1)}, u32[]{:S(2)}, u32[]{:S(2)}) collective-permute-start(bf16[4,240,768]{2,1,0:T(8,128)(2,1)S(1)} %pad_maximum_fusion.near_ref), channel_id=1, source_target_pairs={{0,8},{4,20},{8,0},{12,28},{16,24},{20,4},{24,16},{28,12},{1,9},{5... | collective-permute-start | bytes 4423688 | tf_op jit(solution)/shard_map/ppermute | solution.py:1165
  110.9 39.3 %collective-permute-start.4 = (bf16[4,240,768]{2,1,0:T(8,128)(2,1)S(1)}, bf16[4,240,768]{2,1,0:T(8,128)(2,1)}, u32[]{:S(2)}, u32[]{:S(2)}) collective-permute-start(bf16[4,240,768]{2,1,0:T(8,128)(2,1)S(1)} %pad_maximum_fusion.near_ref), channel_id=1, source_target_pairs={{0,16},{4,12},{8,24},{12,4},{16,0},{20,28},{24,8},{28,20},{1,17},{... | collective-permute-start | bytes 4423688 | tf_op jit(solution)/shard_map/ppermute | solution.py:1165
  150.2 1.1 copy-start.5
  216.8 36.7 %copy-start.8 = (bf16[2,4,48,768]{3,2,1,0:T(8,128)(2,1)S(1)}, bf16[2,4,48,768]{3,2,1,0:T(8,128)(2,1)}, u32[]{:S(2)}) copy-start(bf16[2,4,48,768]{3,2,1,0:T(8,128)(2,1)} %get-tuple-element.109) | copy-start | bytes 1769476
  216.8 36.7 %collective-permute-start.5 = (bf16[4,192,768]{2,1,0:T(8,128)(2,1)}, bf16[4,192,768]{2,1,0:T(8,128)(2,1)S(1)}, u32[]{:S(2)}, u32[]{:S(2)}) collective-permute-start(bf16[4,192,768]{2,1,0:T(8,128)(2,1)} %get-tuple-element.99), channel_id=1, source_target_pairs={{0,16},{4,12},{8,24},{12,4},{16,0},{20,28},{24,8},{28,20},{1,17},{... | collective-permute-start | bytes 3538952 | tf_op jit(solution)/shard_map/ppermute | solution.py:1165
  217.9 35.6 %collective-permute-start.6 = (bf16[4,192,768]{2,1,0:T(8,128)(2,1)}, bf16[4,192,768]{2,1,0:T(8,128)(2,1)S(1)}, u32[]{:S(2)}, u32[]{:S(2)}) collective-permute-start(bf16[4,192,768]{2,1,0:T(8,128)(2,1)} %get-tuple-element.100), channel_id=1, source_target_pairs={{0,8},{4,20},{8,0},{12,28},{16,24},{20,4},{24,16},{28,12},{1,9},{5... | collective-permute-start | bytes 3538952 | tf_op jit(solution)/shard_map/ppermute | solution.py:1165
  218.9 34.6 %collective-permute-start.7 = (bf16[2,4,48,768]{3,2,1,0:T(8,128)(2,1)}, bf16[2,4,48,768]{3,2,1,0:T(8,128)(2,1)}, u32[]{:S(2)}, u32[]{:S(2)}) collective-permute-start(bf16[2,4,48,768]{3,2,1,0:T(8,128)(2,1)} %get-tuple-element.102), channel_id=1, source_target_pairs={{0,8},{4,20},{8,0},{12,28},{16,24},{20,4},{24,16},{28,12},{1,9},{5... | collective-permute-start | bytes 1769480 | tf_op jit(solution)/shard_map/ppermute | solution.py:1165
  254.8 14.0 %collective-permute-start.8 = (bf16[4,48,768]{2,1,0:T(8,128)(2,1)S(1)}, bf16[4,48,768]{2,1,0:T(8,128)(2,1)}, u32[]{:S(2)}, u32[]{:S(2)}) collective-permute-start(bf16[4,48,768]{2,1,0:T(8,128)(2,1)S(1)} %get-tuple-element.147), channel_id=1, source_target_pairs={{0,16},{4,12},{8,24},{12,4},{16,0},{20,28},{24,8},{28,20},{1,17},{... | collective-permute-start | bytes 884744 | tf_op jit(solution)/shard_map/ppermute | solution.py:1165
  255.9 12.5 %copy-start.7 = (bf16[4,192,768]{2,1,0:T(8,128)(2,1)S(1)}, bf16[4,192,768]{2,1,0:T(8,128)(2,1)}, u32[]{:S(2)}) copy-start(bf16[4,192,768]{2,1,0:T(8,128)(2,1)} %get-tuple-element.106) | copy-start | bytes 3538948
  269.9 30.5 %collective-permute-start.10 = (bf16[240,768]{1,0:T(8,128)(2,1)S(1)}, bf16[240,768]{1,0:T(8,128)(2,1)S(1)}, u32[]{:S(2)}, u32[]{:S(2)}) collective-permute-start(bf16[240,768]{1,0:T(8,128)(2,1)S(1)} %get-tuple-element.146), channel_id=1, source_target_pairs={{0,2},{1,3},{2,0},{3,1},{4,6},{5,7},{6,4},{7,5},{8,10},{9,11},{10,... | collective-permute-start | bytes 1105928 | tf_op jit(solution)/shard_map/ppermute | solution.py:1218
  270.0 36.0 %collective-permute-start.11 = (bf16[240,768]{1,0:T(8,128)(2,1)S(1)}, bf16[240,768]{1,0:T(8,128)(2,1)S(1)}, u32[]{:S(2)}, u32[]{:S(2)}) collective-permute-start(bf16[240,768]{1,0:T(8,128)(2,1)S(1)} %get-tuple-element.143), channel_id=1, source_target_pairs={{0,3},{1,0},{2,1},{3,2},{4,7},{5,4},{6,5},{7,6},{8,11},{9,8},{10,9... | collective-permute-start | bytes 1105928 | tf_op jit(solution)/shard_map/ppermute | solution.py:1218
  275.2 30.8 %collective-permute-start.9 = (bf16[240,768]{1,0:T(8,128)(2,1)S(1)}, bf16[240,768]{1,0:T(8,128)(2,1)S(1)}, u32[]{:S(2)}, u32[]{:S(2)}) collective-permute-start(bf16[240,768]{1,0:T(8,128)(2,1)S(1)} %get-tuple-element.145), channel_id=1, source_target_pairs={{0,1},{1,2},{2,3},{3,0},{4,5},{5,6},{6,7},{7,4},{8,9},{9,10},{10,1... | collective-permute-start | bytes 1105928 | tf_op jit(solution)/shard_map/ppermute | solution.py:1218
  375.9 2.9 copy-start.6
  378.8 1.6 copy-start.13
  378.8 2.4 copy-start.12
  380.4 1.7 copy-start.11
  380.4 2.6 copy-start.10
  381.3 2.6 copy-start.15
  381.3 6.2 %copy-start.3 = (bf16[1024,768]{1,0:T(8,128)(2,1)S(1)}, bf16[1024,768]{1,0:T(8,128)(2,1)}, u32[]{:S(2)}) copy-start(bf16[1024,768]{1,0:T(8,128)(2,1)} %get-tuple-element.184) | copy-start | bytes 4718596
  387.4 2.0 copy-start.4
  387.5 3.1 copy-start.1
  (2 other events, 1.5 us)

commit v6 on v5

--- a/solution.py
+++ b/solution.py
@@ -9,7 +9,7 @@
 L = 4096
 C = 128
 HD = 64
-GROUP = 2
+GROUP = 4
 STEP = 1024
 GROUPS = STEP // (GROUP * C)
 HALVES = 2

time: 396 us -> 393 us (level)
  Pallas kernels: 338 us -> 333 us
  transfers between devices with their start and end apart: 12 -> 12, of which waited for: 1 -> 1; matrix products, arithmetic and copies ran while one was open for 0% -> 0% of each run, Pallas kernels for 37% -> 35%
where the time goes in v6:
time: 393 us; the launch traced here: 387 us
  Pallas kernels  333 us (85%)
  starting transfers between devices  20 us (5%)
  other arithmetic  16.3 us (4%)
  local copies, waits for them, and re-layouts  9.18 us (2%)
  waiting for transfers between devices  7.71 us (2%)
    pallas_call x1, Pallas kernels, settle(): pl.pallas_call(settle_kernel, out_shape=[sds((ROWS, WIDTH), BF16)] + [sds...  67.9 us
    pallas_call x1, Pallas kernels, ffn(): pl.pallas_call(ffn_kernel, out_shape=[sds((1024, WIDTH), BF16), sds((1024...  65.5 us
    pallas_call x1, Pallas kernels, collect(): pl.pallas_call(collect_kernel, out_shape=[sds((4 * ROWS, WIDTH), BF16), s...  62.2 us
    pallas_call x1, Pallas kernels, spread(): pl.pallas_call(spread_kernel, out_shape=[jax.ShapeDtypeStruct((4, 1024, C...  37.8 us
    pallas_call x3, Pallas kernels, attend_back(): pl.pallas_call(functools.partial(attend_back_kernel, head), grid=(L // ST...  34.1 us
    pallas_call x1, Pallas kernels, regroup(): pl.pallas_call(regroup_kernel, out_shape=[jax.ShapeDtypeStruct((4096, C),...  33.6 us
    pallas_call x2, Pallas kernels, attend(): pl.pallas_call(functools.partial(attend_kernel, first), grid=(heads, L //...  31.8 us
  transfers between devices with their start and end apart: 12, of which 1 were waited for; matrix products, arithmetic and copies ran while one was open for 0% of the time, Pallas kernels for 35%

profile of v6, /device:TPU:10, one launch (start us, length us, event | category | flops | bytes accessed | tf_op | source)
XLA Modules:
  0.0 387.4 jit_solution(5677685405282752755)
XLA Ops:
  1.4 0.9 fusion.12
  2.4 1.5 fusion.10
  4.8 62.2 %collect.1 = (bf16[4096,768]{1,0:T(8,128)(2,1)}, bf16[3,4096,256]{2,1,0:T(8,128)(2,1)}, bf16[768,768]{1,0:T(8,128)(2,1)}, s32[12288]{0:T(1024)}, s32[1,4096]{1,0:T(1,128)}, /*index=5*/bf16[240,768]{1,0:T(8,128)(2,1)}) custom-call(bf16[1024,768]{1,0:T(8,128)(2,1)} %tok_in.1, bf16[192,768]{1,0:T(8,128)(2,1)} %bitcast.48, bf16[192,768]{1,0:T(8,128)(2,1)} %bitcast.49, ...), custom_call_target="tpu_custom_call" | custom-call | tf_op jit(solution)/shard_map/collect/pallas_call | solution.py:477
  67.1 7.3 %collective-permute-start.1 = (bf16[240,768]{1,0:T(8,128)(2,1)}, bf16[240,768]{1,0:T(8,128)(2,1)S(1)}, u32[]{:S(2)}, u32[]{:S(2)}) collective-permute-start(bf16[240,768]{1,0:T(8,128)(2,1)} %get-tuple-element.90), channel_id=1, source_target_pairs={{0,2},{1,3},{2,0},{3,1},{4,6},{5,7},{6,4},{7,5},{8,10},{9,11},{10,... | collective-permute-start | bytes 1105928 | tf_op jit(solution)/shard_map/ppermute | solution.py:1196
  74.9 20.2 %attend.2 = (bf16[4096,128]{1,0:T(8,128)(2,1)}, bf16[2,4096,256]{2,1,0:T(8,128)(2,1)}, f32[2,4096,128]{2,1,0:T(8,128)}) custom-call(s32[12288]{0:T(1024)} %get-tuple-element.112.ord_ref, s32[1,4096]{1,0:T(1,128)} %get-tuple-element.78.mask_ref, bf16[3,4096,256]{2,1,0:T(8,128)(2,1)} %get-tuple-element.84.qkv_ref), custom_call_target="tpu_custom_call" | custom-call | flops 17999998976 | bytes 10485760 | tf_op jit(solution)/shard_map/attend/pallas_call | solution.py:120
  95.1 11.6 %attend.3 = (bf16[2048,128]{1,0:T(8,128)(2,1)}, bf16[1,4096,256]{2,1,0:T(8,128)(2,1)}, f32[1,4096,128]{2,1,0:T(8,128)}) custom-call(s32[12288]{0:T(1024)} %get-tuple-element.112.ord_ref, s32[1,4096]{1,0:T(1,128)} %get-tuple-element.78.mask_ref, bf16[3,4096,256]{2,1,0:T(8,128)(2,1)} %get-tuple-element.84.qkv_ref), custom_call_target="tpu_custom_call" | custom-call | flops 8999999488 | bytes 10485760 | tf_op jit(solution)/shard_map/attend/pallas_call | solution.py:120
  107.1 1.5 collective-permute-start.3
  110.1 37.8 %spread.1 = (bf16[4,1024,128]{2,1,0:T(8,128)(2,1)}, bf16[4,512,128]{2,1,0:T(8,128)(2,1)}) custom-call(bf16[4096,128]{1,0:T(8,128)(2,1)} %get-tuple-element.83.a_ref, bf16[2048,128]{1,0:T(8,128)(2,1)} %get-tuple-element.87.b_ref), custom_call_target="tpu_custom_call" | custom-call | tf_op jit(solution)/shard_map/spread/pallas_call | solution.py:549
  148.0 1.1 copy-done.5
  149.0 65.5 %ffn.1 = (bf16[1024,768]{1,0:T(8,128)(2,1)}, f32[1024,768]{1,0:T(8,128)}, bf16[4,1024,128]{2,1,0:T(8,128)(2,1)}, bf16[4,512,128]{2,1,0:T(8,128)(2,1)}, bf16[4,19...) custom-call(bf16[4,1024,128]{2,1,0:T(8,128)(2,1)} %get-tuple-element, ...), custom_call_target="tpu_custom_call" | custom-call | tf_op jit(solution)/shard_map/ffn/pallas_call | solution.py:1148
  214.6 1.1 collective-permute-start.5
  215.7 1.0 collective-permute-start.6
  216.7 1.0 collective-permute-start.7
  217.7 33.6 %regroup.1 = (bf16[4096,128]{1,0:T(8,128)(2,1)}, bf16[2048,128]{1,0:T(8,128)(2,1)}) custom-call(bf16[4,1024,128]{2,1,0:T(8,128)(2,1)} %get-tuple-element.95.a_ref, bf16[4,512,128]{2,1,0:T(8,128)(2,1)} %get-tuple-element.96.b_ref), custom_call_target="tpu_custom_call" | custom-call | tf_op jit(solution)/shard_map/regroup/pallas_call | solution.py:594
  251.3 1.2 fusion.9
  252.5 1.1 collective-permute-start.8
  253.6 11.4 %attend_back.3.d0_ref = bf16[4096,256]{1,0:T(8,128)(2,1)} custom-call(s32[12288]{0:T(1024)} %get-tuple-element.112.ord_ref, bf16[4096,128]{1,0:T(8,128)(2,1)} %get-tuple-element.103.g_ref, bf16[2,4096,256]{2,1,0:T(8,128)(2,1)} %get-tuple-element.104.ts_ref, f32[2,4096,128]{2,1,0:T(8,128)} %get-tuple-element.105.pr_ref), custom_call_target="tpu_custom_call" | custom-call | flops 8999999488 | bytes 10485760 | tf_op jit(solution)/shard_map/attend_back/pallas_call | solution.py:197
  265.5 1.0 add_convert_fusion.2
  266.7 5.2 %collective-permute-start.11 = (bf16[240,768]{1,0:T(8,128)(2,1)S(1)}, bf16[240,768]{1,0:T(8,128)(2,1)S(1)}, u32[]{:S(2)}, u32[]{:S(2)}) collective-permute-start(bf16[240,768]{1,0:T(8,128)(2,1)S(1)} %get-tuple-element.143), channel_id=1, source_target_pairs={{0,3},{1,0},{2,1},{3,2},{4,7},{5,4},{6,5},{7,6},{8,11},{9,8},{10,9... | collective-permute-start | bytes 1105928 | tf_op jit(solution)/shard_map/ppermute | solution.py:1218
  272.3 11.4 %attend_back.4.d1_ref = bf16[4096,256]{1,0:T(8,128)(2,1)} custom-call(s32[12288]{0:T(1024)} %get-tuple-element.112.ord_ref, bf16[4096,128]{1,0:T(8,128)(2,1)} %get-tuple-element.103.g_ref, bf16[2,4096,256]{2,1,0:T(8,128)(2,1)} %get-tuple-element.104.ts_ref, f32[2,4096,128]{2,1,0:T(8,128)} %get-tuple-element.105.pr_ref), custom_call_target="tpu_custom_call" | custom-call | flops 8999999488 | bytes 10485760 | tf_op jit(solution)/shard_map/attend_back/pallas_call | solution.py:197
  283.7 11.3 %attend_back.5.d2_ref = bf16[4096,256]{1,0:T(8,128)(2,1)} custom-call(s32[12288]{0:T(1024)} %get-tuple-element.112.ord_ref, bf16[2048,128]{1,0:T(8,128)(2,1)} %get-tuple-element.113.g_ref, bf16[1,4096,256]{2,1,0:T(8,128)(2,1)} %get-tuple-element.114.ts_ref, f32[1,4096,128]{2,1,0:T(8,128)} %get-tuple-element.115.pr_ref), custom_call_target="tpu_custom_call" | custom-call | flops 8999999488 | bytes 10485760 | tf_op jit(solution)/shard_map/attend_back/pallas_call | solution.py:197
  295.1 7.7 %collective-permute-done.11 = bf16[240,768]{1,0:T(8,128)(2,1)S(1)} collective-permute-done((bf16[240,768]{1,0:T(8,128)(2,1)S(1)}, bf16[240,768]{1,0:T(8,128)(2,1)S(1)}, u32[]{:S(2)}, u32[]{:S(2)}) %collective-permute-start.11) | collective-permute-done | bytes 368672 | tf_op jit(solution)/shard_map/ppermute | solution.py:1218
  302.7 0.9 add_convert_fusion.1.mine_ref
  303.7 67.9 %settle.1 = (bf16[1024,768]{1,0:T(8,128)(2,1)}, bf16[192,768]{1,0:T(8,128)(2,1)}, bf16[192,768]{1,0:T(8,128)(2,1)}, bf16[192,768]{1,0:T(8,128)(2,1)}, bf16[768,7...) custom-call(bf16[4096,256]{1,0:T(8,128)(2,1)} %attend_back.3.d0_ref,, ...), custom_call_target="tpu_custom_call" | custom-call | tf_op jit(solution)/shard_map/settle/pallas_call | solution.py:847
  371.6 0.9 convert_element_type.103
  372.6 2.9 convert_element_type.106
  375.5 1.6 convert_element_type.107
  377.1 0.9 convert_bitcast_fusion
  378.8 0.9 convert_bitcast_fusion.2
  381.2 0.9 slice.111
  384.1 1.1 copy.39
  386.1 1.1 copy.40
  (86 shorter events, 10.3 us)
Async XLA Ops:
  67.0 39.7 %collective-permute-start = (bf16[240,768]{1,0:T(8,128)(2,1)}, bf16[240,768]{1,0:T(8,128)(2,1)S(1)}, u32[]{:S(2)}, u32[]{:S(2)}) collective-permute-start(bf16[240,768]{1,0:T(8,128)(2,1)} %get-tuple-element.90), channel_id=1, source_target_pairs={{0,1},{1,2},{2,3},{3,0},{4,5},{5,6},{6,7},{7,4},{8,9},{9,10},{10,1... | collective-permute-start | bytes 1105928 | tf_op jit(solution)/shard_map/ppermute | solution.py:1196
  67.1 39.7 %collective-permute-start.1 = (bf16[240,768]{1,0:T(8,128)(2,1)}, bf16[240,768]{1,0:T(8,128)(2,1)S(1)}, u32[]{:S(2)}, u32[]{:S(2)}) collective-permute-start(bf16[240,768]{1,0:T(8,128)(2,1)} %get-tuple-element.90), channel_id=1, source_target_pairs={{0,2},{1,3},{2,0},{3,1},{4,6},{5,7},{6,4},{7,5},{8,10},{9,11},{10,... | collective-permute-start | bytes 1105928 | tf_op jit(solution)/shard_map/ppermute | solution.py:1196
  74.4 32.3 %collective-permute-start.2 = (bf16[240,768]{1,0:T(8,128)(2,1)}, bf16[240,768]{1,0:T(8,128)(2,1)S(1)}, u32[]{:S(2)}, u32[]{:S(2)}) collective-permute-start(bf16[240,768]{1,0:T(8,128)(2,1)} %get-tuple-element.90), channel_id=1, source_target_pairs={{0,3},{1,0},{2,1},{3,2},{4,7},{5,4},{6,5},{7,6},{8,11},{9,8},{10,9... | collective-permute-start | bytes 1105928 | tf_op jit(solution)/shard_map/ppermute | solution.py:1196
  95.1 11.7 %copy-start.9 = (bf16[240,768]{1,0:T(8,128)(2,1)S(1)}, bf16[240,768]{1,0:T(8,128)(2,1)}, u32[]{:S(2)}) copy-start(bf16[240,768]{1,0:T(8,128)(2,1)} %get-tuple-element.90) | copy-start | bytes 1105924
  106.8 2.6 copy-start.16
  106.8 2.6 copy-start.17
  106.8 2.6 copy-start.18
  106.8 2.6 copy-start.19
  106.8 2.6 copy-start.20
  106.8 2.6 copy-start.21
  107.0 1.6 copy-start.2
  107.1 40.9 %collective-permute-start.3 = (bf16[4,240,768]{2,1,0:T(8,128)(2,1)S(1)}, bf16[4,240,768]{2,1,0:T(8,128)(2,1)S(1)}, u32[]{:S(2)}, u32[]{:S(2)}) collective-permute-start(bf16[4,240,768]{2,1,0:T(8,128)(2,1)S(1)} %pad_maximum_fusion.near_ref), channel_id=1, source_target_pairs={{0,8},{4,20},{8,0},{12,28},{16,24},{20,4},{24,16},{28,12},{1,9},{5... | collective-permute-start | bytes 4423688 | tf_op jit(solution)/shard_map/ppermute | solution.py:1165
  108.6 39.3 %collective-permute-start.4 = (bf16[4,240,768]{2,1,0:T(8,128)(2,1)S(1)}, bf16[4,240,768]{2,1,0:T(8,128)(2,1)}, u32[]{:S(2)}, u32[]{:S(2)}) collective-permute-start(bf16[4,240,768]{2,1,0:T(8,128)(2,1)S(1)} %pad_maximum_fusion.near_ref), channel_id=1, source_target_pairs={{0,16},{4,12},{8,24},{12,4},{16,0},{20,28},{24,8},{28,20},{1,17},{... | collective-permute-start | bytes 4423688 | tf_op jit(solution)/shard_map/ppermute | solution.py:1165
  147.9 1.1 copy-start.5
  214.6 36.7 %copy-start.8 = (bf16[2,4,48,768]{3,2,1,0:T(8,128)(2,1)S(1)}, bf16[2,4,48,768]{3,2,1,0:T(8,128)(2,1)}, u32[]{:S(2)}) copy-start(bf16[2,4,48,768]{3,2,1,0:T(8,128)(2,1)} %get-tuple-element.109) | copy-start | bytes 1769476
  214.6 36.7 %collective-permute-start.5 = (bf16[4,192,768]{2,1,0:T(8,128)(2,1)}, bf16[4,192,768]{2,1,0:T(8,128)(2,1)S(1)}, u32[]{:S(2)}, u32[]{:S(2)}) collective-permute-start(bf16[4,192,768]{2,1,0:T(8,128)(2,1)} %get-tuple-element.99), channel_id=1, source_target_pairs={{0,16},{4,12},{8,24},{12,4},{16,0},{20,28},{24,8},{28,20},{1,17},{... | collective-permute-start | bytes 3538952 | tf_op jit(solution)/shard_map/ppermute | solution.py:1165
  215.7 35.6 %collective-permute-start.6 = (bf16[4,192,768]{2,1,0:T(8,128)(2,1)}, bf16[4,192,768]{2,1,0:T(8,128)(2,1)S(1)}, u32[]{:S(2)}, u32[]{:S(2)}) collective-permute-start(bf16[4,192,768]{2,1,0:T(8,128)(2,1)} %get-tuple-element.100), channel_id=1, source_target_pairs={{0,8},{4,20},{8,0},{12,28},{16,24},{20,4},{24,16},{28,12},{1,9},{5... | collective-permute-start | bytes 3538952 | tf_op jit(solution)/shard_map/ppermute | solution.py:1165
  216.7 34.6 %collective-permute-start.7 = (bf16[2,4,48,768]{3,2,1,0:T(8,128)(2,1)}, bf16[2,4,48,768]{3,2,1,0:T(8,128)(2,1)}, u32[]{:S(2)}, u32[]{:S(2)}) collective-permute-start(bf16[2,4,48,768]{3,2,1,0:T(8,128)(2,1)} %get-tuple-element.102), channel_id=1, source_target_pairs={{0,8},{4,20},{8,0},{12,28},{16,24},{20,4},{24,16},{28,12},{1,9},{5... | collective-permute-start | bytes 1769480 | tf_op jit(solution)/shard_map/ppermute | solution.py:1165
  252.5 13.0 %collective-permute-start.8 = (bf16[4,48,768]{2,1,0:T(8,128)(2,1)S(1)}, bf16[4,48,768]{2,1,0:T(8,128)(2,1)}, u32[]{:S(2)}, u32[]{:S(2)}) collective-permute-start(bf16[4,48,768]{2,1,0:T(8,128)(2,1)S(1)} %get-tuple-element.147), channel_id=1, source_target_pairs={{0,16},{4,12},{8,24},{12,4},{16,0},{20,28},{24,8},{28,20},{1,17},{... | collective-permute-start | bytes 884744 | tf_op jit(solution)/shard_map/ppermute | solution.py:1165
  253.6 11.4 %copy-start.7 = (bf16[4,192,768]{2,1,0:T(8,128)(2,1)S(1)}, bf16[4,192,768]{2,1,0:T(8,128)(2,1)}, u32[]{:S(2)}) copy-start(bf16[4,192,768]{2,1,0:T(8,128)(2,1)} %get-tuple-element.106) | copy-start | bytes 3538948
  266.6 28.4 %collective-permute-start.10 = (bf16[240,768]{1,0:T(8,128)(2,1)S(1)}, bf16[240,768]{1,0:T(8,128)(2,1)S(1)}, u32[]{:S(2)}, u32[]{:S(2)}) collective-permute-start(bf16[240,768]{1,0:T(8,128)(2,1)S(1)} %get-tuple-element.146), channel_id=1, source_target_pairs={{0,2},{1,3},{2,0},{3,1},{4,6},{5,7},{6,4},{7,5},{8,10},{9,11},{10,... | collective-permute-start | bytes 1105928 | tf_op jit(solution)/shard_map/ppermute | solution.py:1218
  266.7 36.0 %collective-permute-start.11 = (bf16[240,768]{1,0:T(8,128)(2,1)S(1)}, bf16[240,768]{1,0:T(8,128)(2,1)S(1)}, u32[]{:S(2)}, u32[]{:S(2)}) collective-permute-start(bf16[240,768]{1,0:T(8,128)(2,1)S(1)} %get-tuple-element.143), channel_id=1, source_target_pairs={{0,3},{1,0},{2,1},{3,2},{4,7},{5,4},{6,5},{7,6},{8,11},{9,8},{10,9... | collective-permute-start | bytes 1105928 | tf_op jit(solution)/shard_map/ppermute | solution.py:1218
  271.9 30.8 %collective-permute-start.9 = (bf16[240,768]{1,0:T(8,128)(2,1)S(1)}, bf16[240,768]{1,0:T(8,128)(2,1)S(1)}, u32[]{:S(2)}, u32[]{:S(2)}) collective-permute-start(bf16[240,768]{1,0:T(8,128)(2,1)S(1)} %get-tuple-element.145), channel_id=1, source_target_pairs={{0,1},{1,2},{2,3},{3,0},{4,5},{5,6},{6,7},{7,4},{8,9},{9,10},{10,1... | collective-permute-start | bytes 1105928 | tf_op jit(solution)/shard_map/ppermute | solution.py:1218
  372.6 2.9 copy-start.6
  375.5 1.6 copy-start.13
  375.5 2.4 copy-start.12
  377.1 1.7 copy-start.11
  377.1 2.6 copy-start.10
  377.9 2.6 copy-start.15
  377.9 6.2 %copy-start.3 = (bf16[1024,768]{1,0:T(8,128)(2,1)S(1)}, bf16[1024,768]{1,0:T(8,128)(2,1)}, u32[]{:S(2)}) copy-start(bf16[1024,768]{1,0:T(8,128)(2,1)} %get-tuple-element.184) | copy-start | bytes 4718596
  384.1 2.0 copy-start.4
  384.1 3.1 copy-start.1
  (2 other events, 1.5 us)
